TPU v7x, 128 devices: a whole 4x4x4 slice. The times are simulated.
128 devices in a mesh: ctx: 32 (over y, z_lo, x), wsh: 4 (over z_hi, core).
Axes of the slice: x: 4, y: 4, z: 4 (z_hi: 2, z_lo: 2; z = z_hi * 2 + z_lo), core: 2. Of those that a mesh axis runs over, the one named last changes fastest.
Arguments:
- tokens: bfloat16 [4, 4096, 1536], P('wsh', 'ctx'), may hold values from -6 to 6
- lengths: int32 [4, 4], replicated, may hold values from 1 to 2048, as said below
- deal: int32 [4, 64], replicated, may hold values from 0 to 63, as said below
- expert_ids: int32 [4, 4096, 2], P('wsh', 'ctx'), may hold values from 0 to 15, all different within a row; in each aligned block of 128 rows (0 to 127, 128 to 255, ..., all dimensions but the last counted through in order) at most 32 rows name the same one
- gain_attn: float32 [1536], P('wsh'), may hold values from 0.5 to 1.5
- w_qkv: float32 [1536, 2560], P('wsh'), may hold values from -0.15625 to 0.15625
- w_out: float32 [1536, 1536], P('wsh'), may hold values from -1.25 to 1.25
- gain_moe: float32 [1536], P('wsh'), may hold values from 0.5 to 1.5
- w_router: float32 [1536, 16], P('wsh'), may hold values from -0.109375 to 0.109375
- w_gate: float32 [32, 1536, 512], P('ctx', 'wsh'), may hold values from -0.15625 to 0.15625
- w_up: float32 [32, 1536, 512], P('ctx', 'wsh'), may hold values from -0.15625 to 0.15625
- w_down: float32 [32, 512, 1536], P('ctx', None, 'wsh'), may hold values from -0.375 to 0.375
- cotangent: bfloat16 [4, 4096, 1536], P('wsh', 'ctx'), may hold values from -6 to 6
Outputs:
- block_output: bfloat16 [4, 4096, 1536], P('wsh', 'ctx')
- d_tokens: bfloat16 [4, 4096, 1536], P('wsh', 'ctx')
- d_gain_attn: float32 [1536], P('wsh')
- d_w_qkv: float32 [1536, 2560], P('wsh')
- d_w_out: float32 [1536, 1536], P('wsh')
- d_gain_moe: float32 [1536], P('wsh')
- d_w_router: float32 [1536, 16], P('wsh')
- d_w_gate: float32 [32, 1536, 512], P('ctx', 'wsh')
- d_w_up: float32 [32, 1536, 512], P('ctx', 'wsh')
- d_w_down: float32 [32, 512, 1536], P('ctx', None, 'wsh')
Inputs may be any that keep to these rules, and one draw needn't show every extreme that they name: `lengths`: each row adds up to 4096, and its largest entry is 2048. `deal`: each row is a permutation of 0 to 63 in which the entries at 2 i and 2 i + 1 add up to 63. `expert_ids`: each row names 2 different experts; within the rows of one device (aligned blocks of 128 rows along the first two dimensions) no expert is named by more than 32 rows, and in some blocks one is named by exactly 32.
All inputs are finite; a program needn't handle non-finite values.
Results may differ from a plain program's by a relative error of at most 0.03.
Values may be sent and summed in bfloat16 or wider, within the bound.
A program may use at most 192 MiB of HBM per device.

v0:
```python
import math

import jax
import jax.numpy as jnp
from jax import lax
from jax.sharding import PartitionSpec as P

QUERY_HEADS = 24
KEY_VALUE_HEADS = 8
HEAD_SIZE = 64
TOP = 2


EPSILON = 1e-05
NEG_BIG = -1e30


def stream_positions(deal_row, lengths_row, block_rows):
    count_blocks = deal_row.shape[0]
    within = jnp.tile(jnp.arange(block_rows, dtype=jnp.int32), count_blocks)
    positions = jnp.repeat(deal_row * block_rows, block_rows) + within
    bounds = jnp.cumsum(lengths_row)
    documents = jnp.sum((bounds[None, :] <= positions[:, None]).astype(jnp.int32), axis=1)
    return (positions, documents)


def rms_forward(values, gain_row):
    scale_row = lax.rsqrt(jnp.mean(values * values, axis=-1, keepdims=True) + EPSILON)
    return (values * scale_row * gain_row, scale_row)


def rms_backward(values, scale_row, gain_row, upstream):
    scaled = upstream * gain_row
    inner_mean = jnp.mean(scaled * values, axis=-1, keepdims=True)
    d_in = scale_row * scaled - values * scale_row**3 * inner_mean
    d_gain = jnp.sum(upstream * values * scale_row, axis=0)
    return (d_in, d_gain)


def body(
    tokens,
    lengths,
    deal,
    expert_ids,
    gain_attn,
    w_qkv,
    w_out,
    gain_moe,
    w_router,
    w_gate,
    w_up,
    w_down,
    cotangent,
):
    stream_index = lax.axis_index("wsh")
    ctx_count = lax.axis_size("ctx")
    ctx_index = lax.axis_index("ctx")
    device_local_rows = tokens.shape[1]
    model_width = tokens.shape[2]
    block_rows = device_local_rows // 2
    stream_rows = device_local_rows * ctx_count
    query_group_width = QUERY_HEADS // KEY_VALUE_HEADS
    query_total_width = QUERY_HEADS * HEAD_SIZE
    key_value_width = KEY_VALUE_HEADS * HEAD_SIZE
    scaling = HEAD_SIZE ** (-0.5)
    expert_count = w_router.shape[1]
    capacity = 2 * device_local_rows * TOP // expert_count
    assign_count = device_local_rows * TOP
    lengths_row = lax.dynamic_index_in_dim(lengths, stream_index, 0, keepdims=False)
    deal_row = lax.dynamic_index_in_dim(deal, stream_index, 0, keepdims=False)
    key_pos, key_doc = stream_positions(deal_row, lengths_row, block_rows)
    query_pos = lax.dynamic_slice_in_dim(key_pos, ctx_index * device_local_rows, device_local_rows)
    query_doc = lax.dynamic_slice_in_dim(key_doc, ctx_index * device_local_rows, device_local_rows)
    dense_full = (
        lax.all_gather(w_qkv.astype(jnp.bfloat16), "wsh", axis=0, tiled=True),
        lax.all_gather(w_out.astype(jnp.bfloat16), "wsh", axis=0, tiled=True),
        lax.all_gather(w_router.astype(jnp.bfloat16), "wsh", axis=0, tiled=True),
        lax.all_gather(gain_attn.astype(jnp.bfloat16), "wsh", axis=0, tiled=True),
        lax.all_gather(gain_moe.astype(jnp.bfloat16), "wsh", axis=0, tiled=True),
    )
    full_qkv, full_out, full_router = (dense_full[0], dense_full[1], dense_full[2])
    gain_first = dense_full[3].astype(jnp.float32)
    gain_second = dense_full[4].astype(jnp.float32)
    experts_full = (
        lax.all_gather(w_gate.astype(jnp.bfloat16), "wsh", axis=1, tiled=True),
        lax.all_gather(w_up.astype(jnp.bfloat16), "wsh", axis=1, tiled=True),
        lax.all_gather(w_down.astype(jnp.bfloat16), "wsh", axis=2, tiled=True),
    )
    gate_full = experts_full[0][0]
    up_full = experts_full[1][0]
    down_full = experts_full[2][0]
    x_first = tokens[0].astype(jnp.float32)
    normed_first, scale_first = rms_forward(x_first, gain_first)
    act_attn = normed_first.astype(jnp.bfloat16)
    query_key_value = jnp.dot(act_attn, full_qkv, preferred_element_type=jnp.float32).astype(
        jnp.bfloat16
    )
    query_head_rows = query_key_value[:, :query_total_width].reshape(
        device_local_rows, KEY_VALUE_HEADS, query_group_width, HEAD_SIZE
    )
    kv_all = lax.all_gather(query_key_value[:, query_total_width:], "ctx", axis=0, tiled=True)
    current_key_block = math.gcd(stream_rows, 512)
    total_blocks = stream_rows // current_key_block

    def block_mask(key_start):
        pos_block = lax.dynamic_slice_in_dim(key_pos, key_start, current_key_block)
        doc_block = lax.dynamic_slice_in_dim(key_doc, key_start, current_key_block)
        return (query_doc[:, None] == doc_block[None, :]) & (
            pos_block[None, :] <= query_pos[:, None]
        )

    def block_keys(key_start):
        key_row_count = lax.dynamic_slice_in_dim(kv_all, key_start, current_key_block, 0)
        return (
            key_row_count[:, :key_value_width].reshape(
                current_key_block, KEY_VALUE_HEADS, HEAD_SIZE
            ),
            key_row_count[:, key_value_width:].reshape(
                current_key_block, KEY_VALUE_HEADS, HEAD_SIZE
            ),
        )

    def block_scores(k_block):
        return (
            jnp.einsum(
                "qhgd,khd->hgqk", query_head_rows, k_block, preferred_element_type=jnp.float32
            )
            * scaling
        )

    def stats_step(block_index, running):
        key_start = block_index * current_key_block
        allowed = block_mask(key_start)
        top_now, sum_now = running
        k_block = block_keys(key_start)[0]
        scores = jnp.where(allowed, block_scores(k_block), NEG_BIG)
        top_new = jnp.maximum(top_now, jnp.max(scores, axis=-1))
        weights = jnp.where(allowed, jnp.exp(scores - top_new[..., None]), 0.0)
        return (top_new, sum_now * jnp.exp(top_now - top_new) + jnp.sum(weights, axis=-1))

    statistic_layout = (KEY_VALUE_HEADS, query_group_width, device_local_rows)
    top_final, sum_final = lax.fori_loop(
        0,
        total_blocks,
        stats_step,
        (
            jnp.full(statistic_layout, NEG_BIG, jnp.float32),
            jnp.zeros(statistic_layout, jnp.float32),
        ),
    )
    log_total = top_final + jnp.log(sum_final)

    def output_update(block_index, running):
        key_start = block_index * current_key_block
        allowed = block_mask(key_start)
        k_block, v_block = block_keys(key_start)
        probs = jnp.where(
            allowed, jnp.exp(block_scores(k_block) - log_total[..., None]), 0.0
        ).astype(jnp.bfloat16)
        return running + jnp.einsum(
            "hgqk,khd->qhgd", probs, v_block, preferred_element_type=jnp.float32
        )

    attn_heads = lax.fori_loop(
        0,
        total_blocks,
        output_update,
        jnp.zeros((device_local_rows, KEY_VALUE_HEADS, query_group_width, HEAD_SIZE), jnp.float32),
    )
    attn_low = attn_heads.reshape(device_local_rows, query_total_width).astype(jnp.bfloat16)
    middle = x_first + jnp.dot(attn_low, full_out, preferred_element_type=jnp.float32)
    normed_second, scale_second = rms_forward(middle, gain_second)
    act_moe = normed_second.astype(jnp.bfloat16)
    logits = jnp.dot(act_moe, full_router, preferred_element_type=jnp.float32)
    choice_ids = expert_ids[0]
    picked_onehot = (
        choice_ids[:, :, None] == jnp.arange(expert_count, dtype=jnp.int32)[None, None, :]
    )
    picked = jnp.sum(jnp.where(picked_onehot, logits[:, None, :], 0.0), axis=-1)
    picked_top = jnp.max(picked, axis=-1, keepdims=True)
    picked_exp = jnp.exp(picked - picked_top)
    gates = picked_exp / jnp.sum(picked_exp, axis=-1, keepdims=True)
    flat_ids = choice_ids.reshape(-1)
    assign_hot = (flat_ids[:, None] == jnp.arange(expert_count, dtype=jnp.int32)[None, :]).astype(
        jnp.int32
    )
    ranks = jnp.sum((jnp.cumsum(assign_hot, axis=0) - 1) * assign_hot, axis=1)
    slot_of_assign = flat_ids * capacity + ranks
    assign_range = jnp.arange(assign_count, dtype=jnp.int32)
    slot_hit = (
        slot_of_assign[None, :] == jnp.arange(expert_count * capacity, dtype=jnp.int32)[:, None]
    )
    has_assign = jnp.any(slot_hit, axis=1)
    slot_assign = jnp.where(
        has_assign, jnp.sum(jnp.where(slot_hit, assign_range[None, :], 0), axis=1), assign_count
    )
    slot_token = jnp.where(has_assign, slot_assign // TOP, device_local_rows)
    act_pad = jnp.concatenate([act_moe, jnp.zeros((1, model_width), jnp.bfloat16)], axis=0)
    send_rows = jnp.take(act_pad, slot_token, axis=0).reshape(expert_count, capacity, model_width)
    send_rows = jnp.repeat(send_rows, 2, axis=0)
    recv_rows = lax.all_to_all(send_rows, "ctx", split_axis=0, concat_axis=0, tiled=True)
    inputs = recv_rows.reshape(-1, model_width)
    pre_gate = jnp.dot(inputs, gate_full, preferred_element_type=jnp.float32)
    pre_up = jnp.dot(inputs, up_full, preferred_element_type=jnp.float32)
    sigmoid_gate = jax.nn.sigmoid(pre_gate)
    silu_gate = pre_gate * sigmoid_gate
    hidden = (silu_gate * pre_up).astype(jnp.bfloat16)
    expert_out = jnp.dot(hidden, down_full, preferred_element_type=jnp.float32).astype(jnp.bfloat16)
    back_rows = lax.all_to_all(
        expert_out.reshape(ctx_count, capacity, model_width),
        "ctx",
        split_axis=0,
        concat_axis=0,
        tiled=True,
    )
    back_flat = back_rows.reshape(-1, model_width)
    first_index = flat_ids * 2 * capacity + ranks
    second_index = first_index + capacity
    expert_sum = (
        jnp.take(back_flat, first_index, axis=0).astype(jnp.float32)
        + jnp.take(back_flat, second_index, axis=0).astype(jnp.float32)
    ).reshape(device_local_rows, TOP, model_width)
    mixed = jnp.sum(gates[:, :, None] * expert_sum, axis=1)
    output_rows = (middle + mixed).astype(jnp.bfloat16)
    d_out = cotangent[0].astype(jnp.float32)
    d_gates = jnp.sum(d_out[:, None, :] * expert_sum, axis=-1)
    d_picked = gates * (d_gates - jnp.sum(gates * d_gates, axis=-1, keepdims=True))
    d_logits = jnp.sum(jnp.where(picked_onehot, d_picked[:, :, None], 0.0), axis=1).astype(
        jnp.bfloat16
    )
    gate_pad = jnp.concatenate([gates.reshape(-1), jnp.zeros((1,), jnp.float32)])
    slot_gate = jnp.take(gate_pad, slot_assign)
    d_out_pad = jnp.concatenate([d_out, jnp.zeros((1, model_width), jnp.float32)], axis=0)
    send_grads = (slot_gate[:, None] * jnp.take(d_out_pad, slot_token, axis=0)).astype(jnp.bfloat16)
    send_grads = jnp.repeat(send_grads.reshape(expert_count, capacity, model_width), 2, axis=0)
    recv_grads = lax.all_to_all(send_grads, "ctx", split_axis=0, concat_axis=0, tiled=True).reshape(
        -1, model_width
    )
    d_down_local = jnp.einsum("rf,rd->fd", hidden, recv_grads, preferred_element_type=jnp.float32)
    d_hidden = jnp.einsum("rd,fd->rf", recv_grads, down_full, preferred_element_type=jnp.float32)
    d_pre_gate = (
        d_hidden * pre_up * sigmoid_gate * (1.0 + pre_gate * (1.0 - sigmoid_gate))
    ).astype(jnp.bfloat16)
    d_pre_up = (d_hidden * silu_gate).astype(jnp.bfloat16)
    d_inputs = jnp.einsum("rf,df->rd", d_pre_gate, gate_full, preferred_element_type=jnp.float32)
    d_inputs = (
        d_inputs + jnp.einsum("rf,df->rd", d_pre_up, up_full, preferred_element_type=jnp.float32)
    ).astype(jnp.bfloat16)
    d_gate_local = jnp.einsum("rd,rf->df", inputs, d_pre_gate, preferred_element_type=jnp.float32)
    d_up_local = jnp.einsum("rd,rf->df", inputs, d_pre_up, preferred_element_type=jnp.float32)
    returned = lax.all_to_all(
        d_inputs.reshape(ctx_count, capacity, model_width),
        "ctx",
        split_axis=0,
        concat_axis=0,
        tiled=True,
    ).reshape(-1, model_width)
    d_copies = jnp.take(returned, first_index, axis=0).astype(jnp.float32) + jnp.take(
        returned, second_index, axis=0
    ).astype(jnp.float32)
    d_act_moe = jnp.sum(d_copies.reshape(device_local_rows, TOP, model_width), axis=1)
    d_act_moe = d_act_moe + jnp.einsum(
        "re,de->rd", d_logits, full_router, preferred_element_type=jnp.float32
    )
    d_router_local = jnp.einsum("rd,re->de", act_moe, d_logits, preferred_element_type=jnp.float32)
    d_mid_norm, d_gain_second = rms_backward(middle, scale_second, gain_second, d_act_moe)
    d_middle = d_out + d_mid_norm
    d_branch = d_middle.astype(jnp.bfloat16)
    d_out_local = jnp.einsum("rk,rd->kd", attn_low, d_branch, preferred_element_type=jnp.float32)
    attention_gradient = jnp.einsum(
        "rd,kd->rk", d_branch, full_out, preferred_element_type=jnp.float32
    ).astype(jnp.bfloat16)
    head_attention_gradient = attention_gradient.reshape(
        device_local_rows, KEY_VALUE_HEADS, query_group_width, HEAD_SIZE
    )
    delta = jnp.sum(head_attention_gradient.astype(jnp.float32) * attn_heads, axis=-1).transpose(
        1, 2, 0
    )

    def back_step(block_index, running):
        key_start = block_index * current_key_block
        allowed = block_mask(key_start)
        d_query, kv_term = running
        k_block, v_block = block_keys(key_start)
        probs = jnp.where(allowed, jnp.exp(block_scores(k_block) - log_total[..., None]), 0.0)
        probs_low = probs.astype(jnp.bfloat16)
        d_probs = jnp.einsum(
            "qhgd,khd->hgqk", head_attention_gradient, v_block, preferred_element_type=jnp.float32
        )
        d_scores = (probs * (d_probs - delta[..., None])).astype(jnp.bfloat16)
        d_query = (
            d_query
            + jnp.einsum("hgqk,khd->qhgd", d_scores, k_block, preferred_element_type=jnp.float32)
            * scaling
        )
        d_key = (
            jnp.einsum(
                "hgqk,qhgd->khd", d_scores, query_head_rows, preferred_element_type=jnp.float32
            )
            * scaling
        )
        d_value = jnp.einsum(
            "hgqk,qhgd->khd", probs_low, head_attention_gradient, preferred_element_type=jnp.float32
        )
        piece_term = jnp.concatenate(
            [
                d_key.reshape(current_key_block, key_value_width),
                d_value.reshape(current_key_block, key_value_width),
            ],
            axis=1,
        )
        return (d_query, lax.dynamic_update_slice_in_dim(kv_term, piece_term, key_start, 0))

    d_query, kv_term = lax.fori_loop(
        0,
        total_blocks,
        back_step,
        (
            jnp.zeros(
                (device_local_rows, KEY_VALUE_HEADS, query_group_width, HEAD_SIZE), jnp.float32
            ),
            jnp.zeros((stream_rows, 2 * key_value_width), jnp.float32),
        ),
    )
    kv_owned = lax.psum_scatter(
        kv_term.astype(jnp.bfloat16), "ctx", scatter_dimension=0, tiled=True
    )
    d_qkv = jnp.concatenate(
        [d_query.reshape(device_local_rows, query_total_width).astype(jnp.bfloat16), kv_owned],
        axis=1,
    )
    d_act_attn = jnp.einsum("rk,dk->rd", d_qkv, full_qkv, preferred_element_type=jnp.float32)
    d_qkv_local = jnp.einsum("rd,rk->dk", act_attn, d_qkv, preferred_element_type=jnp.float32)
    d_x_norm, d_gain_first = rms_backward(x_first, scale_first, gain_first, d_act_attn)
    d_tokens = (d_middle + d_x_norm).astype(jnp.bfloat16)
    dense_grads = (d_qkv_local, d_out_local, d_router_local, d_gain_first, d_gain_second)
    summed = (
        lax.psum(dense_grads[0].astype(jnp.bfloat16), "ctx").astype(jnp.float32),
        lax.psum(dense_grads[1].astype(jnp.bfloat16), "ctx").astype(jnp.float32),
        lax.psum(dense_grads[2].astype(jnp.bfloat16), "ctx").astype(jnp.float32),
        lax.psum(dense_grads[3].astype(jnp.bfloat16), "ctx").astype(jnp.float32),
        lax.psum(dense_grads[4].astype(jnp.bfloat16), "ctx").astype(jnp.float32),
    )
    owned = (
        lax.psum_scatter(
            summed[0].astype(jnp.bfloat16), "wsh", scatter_dimension=0, tiled=True
        ).astype(jnp.float32),
        lax.psum_scatter(
            summed[1].astype(jnp.bfloat16), "wsh", scatter_dimension=0, tiled=True
        ).astype(jnp.float32),
        lax.psum_scatter(
            summed[2].astype(jnp.bfloat16), "wsh", scatter_dimension=0, tiled=True
        ).astype(jnp.float32),
        lax.psum_scatter(
            summed[3].astype(jnp.bfloat16), "wsh", scatter_dimension=0, tiled=True
        ).astype(jnp.float32),
        lax.psum_scatter(
            summed[4].astype(jnp.bfloat16), "wsh", scatter_dimension=0, tiled=True
        ).astype(jnp.float32),
    )
    expert_owned = (
        lax.psum_scatter(
            d_gate_local[None].astype(jnp.bfloat16), "wsh", scatter_dimension=1, tiled=True
        ).astype(jnp.float32),
        lax.psum_scatter(
            d_up_local[None].astype(jnp.bfloat16), "wsh", scatter_dimension=1, tiled=True
        ).astype(jnp.float32),
        lax.psum_scatter(
            d_down_local[None].astype(jnp.bfloat16), "wsh", scatter_dimension=2, tiled=True
        ).astype(jnp.float32),
    )
    return (
        output_rows[None],
        d_tokens[None],
        owned[3],
        owned[0],
        owned[1],
        owned[4],
        owned[2],
        expert_owned[0],
        expert_owned[1],
        expert_owned[2],
    )


def solution(mesh):
    placed = (
        P("wsh", "ctx", None),
        P(),
        P(),
        P("wsh", "ctx", None),
        P("wsh"),
        P("wsh", None),
        P("wsh", None),
        P("wsh"),
        P("wsh", None),
        P("ctx", "wsh", None),
        P("ctx", "wsh", None),
        P("ctx", None, "wsh"),
        P("wsh", "ctx", None),
    )
    return jax.shard_map(
        body,
        mesh=mesh,
        in_specs=placed,
        out_specs=(
            P("wsh", "ctx", None),
            P("wsh", "ctx", None),
            P("wsh"),
            P("wsh", None),
            P("wsh", None),
            P("wsh"),
            P("wsh", None),
            P("ctx", "wsh", None),
            P("ctx", "wsh", None),
            P("ctx", None, "wsh"),
        ),
        check_vma=False,
    )
```

profile of v0, /device:TPU:8, one launch (start us, length us, event | category | flops | bytes accessed | tf_op | source)
XLA Modules:
  0.0 1568.3 jit_solution(17303514624026712794)
XLA Ops:
  11.0 7.0 all-gather
  18.8 54.1 %all-gather.9.cloned.1.call-done = bf16[1536,2560]{1,0:T(8,128)(2,1)} async-done(((bf16[384,2560]{1,0:T(8,128)(2,1)}), bf16[1536,2560]{1,0:T(8,128)(2,1)}) %all-gather.9.cloned.1.call-update) | async-done | bytes 7864336 | tf_op jit(solution)/shard_map/all_gather | solution.py:75
  72.9 4.5 convolution_convert_fusion.3
  89.2 6.7 all-gather.1
  96.4 140.3 %all-gather.11.cloned.1.call-done = bf16[4096,1024]{1,0:T(8,128)(2,1)} async-done(((bf16[128,1024]{1,0:T(8,128)(2,1)}), bf16[4096,1024]{1,0:T(8,128)(2,1)}) %all-gather.11.cloned.1.call-update) | async-done | bytes 8388624 | tf_op jit(solution)/shard_map/all_gather | solution.py:101
  236.7 11.2 copy.69
  248.0 88.1 %while.46 = (s32[]{:T(128)}, f32[8,3,128]{2,1,0:T(4,128)S(1)}, f32[8,3,128]{2,1,0:T(4,128)S(1)}, s32[128]{0:T(128)S(1)}, s32[4096]{0:T(1024)}, /*index=5*/s32[40...) while((s32[]{:T(128)}, f32[8,3,128]{2,1,0:T(4,128)S(1)}, ...), condition=%wide.region_6.7_spmd.clone, body=%wide.region_3.6_spmd.clone.sunk | while | flops 214121472 | bytes 14918858 | solution.py:142
  254.5 4.6 select_reduce_fusion.5
  265.8 4.3 select_reduce_fusion.5
  276.7 4.3 select_reduce_fusion.5
  287.7 4.3 select_reduce_fusion.5
  294.8 3.8 fusion.144
  298.6 4.6 select_reduce_fusion.5
  306.1 3.8 fusion.144
  309.9 4.3 select_reduce_fusion.5
  320.8 4.3 select_reduce_fusion.5
  331.7 4.3 select_reduce_fusion.5
  336.1 40.1 %while.47 = (s32[]{:T(128)}, f32[128,8,3,64]{0,3,2,1:T(8,128)S(1)}, bf16[4096,1024]{0,1:T(8,128)(2,1)}, s32[128]{0:T(128)S(1)}, s32[4096]{0:T(1024)}, /*index=5*...) while((s32[]{:T(128)}, f32[128,8,3,64]{0,3,2,1:T(8,128)S(1)}, ...), condition=%wide.region_8.9_spmd.clone, body=%wide.region_7.8_spmd.clone.sunk | while | flops 409534464 | bytes 5268705 | solution.py:164
  387.6 15.8 %all-to-all-start = ((bf16[32,32,1536]{2,1,0:T(8,128)(2,1)}), bf16[32,32,1536]{2,1,0:T(8,128)(2,1)}, u32[]{:S(2)}, u32[]{:S(2)}) async-start(bf16[32,32,1536]{2,1,0:T(8,128)(2,1)} %bitcast.12), calls=%async_computation | async-start | bytes 6291456 | tf_op jit(solution)/shard_map/all_to_all | solution.py:201
  404.7 23.8 %all-to-all-done = bf16[32,32,1536]{2,1,0:T(8,128)(2,1)} async-done(((bf16[32,32,1536]{2,1,0:T(8,128)(2,1)}), bf16[32,32,1536]{2,1,0:T(8,128)(2,1)}, u32[]{:S(2)}, u32[]{:S(2)}) %all-to-all-start) | async-done | bytes 3145760 | tf_op jit(solution)/shard_map/all_to_all | solution.py:201
  428.5 5.5 fusion.43
  434.0 6.3 multiply_convert_fusion.3
  440.3 5.3 convolution_convert_fusion.2
  445.6 5.8 all-to-all-start.1
  459.4 17.4 %all_gather.32 = bf16[1536,16]{0,1:T(8,128)(2,1)S(1)} all-gather(bf16[384,16]{0,1:T(8,128)(2,1)S(1)} %convert_element_type.229), channel_id=1, replica_groups=mesh['ctx'=32,'wsh'=4] {'wsh'}, dimensions={0}, use_global_device_ids=true | all-gather | bytes 61440 | tf_op jit(solution)/shard_map/all_gather | solution.py:77
  478.8 9.7 all-to-all-done.1
  488.5 5.2 gather_fusion.4
  493.7 5.2 gather_fusion.3
  498.9 4.2 multiply_reduce_fusion
  511.5 4.8 gather_fusion.1
  519.8 46.3 %all_to_all.20 = bf16[32,32,1536]{2,1,0:T(8,128)(2,1)S(1)} all-to-all(bf16[32,32,1536]{2,1,0:T(8,128)(2,1)S(1)} %bitcast.285), channel_id=1, replica_groups=mesh['ctx'=32,'wsh'=4] {'ctx'}, dimensions={0} | all-to-all | bytes 6291456 | tf_op jit(solution)/shard_map/all_to_all | solution.py:236
  574.3 5.6 all-to-all-start.3
  584.6 4.6 multiply_reduce_fusion.1
  589.2 27.3 %all-to-all-done.3 = bf16[32,32,1536]{2,1,0:T(8,128)(2,1)S(1)} async-done(((bf16[32,32,1536]{2,1,0:T(8,128)(2,1)}), bf16[32,32,1536]{2,1,0:T(8,128)(2,1)S(1)}, u32[]{:S(2)}, u32[]{:S(2)}) %all-to-all-start.3) | async-done | bytes 3145760 | tf_op jit(solution)/shard_map/all_to_all | solution.py:251
  631.3 4.1 convolution_convert_fusion.7
  638.0 4.3 broadcast_in_dim.249
  642.2 134.3 %while.48 = (s32[]{:T(128)}, f32[128,8,3,64]{0,3,2,1:T(8,128)}, bf16[4096,1024]{0,1:T(8,128)(2,1)}, bf16[4096,1024]{0,1:T(8,128)(2,1)}, s32[128]{0:T(128)S(1)}, ...) while((s32[]{:T(128)}, f32[128,8,3,64]{0,3,2,1:T(8,128)}, ...), condition=%wide.region_26.28_spmd.clone, body=%wide.region_25.27_spmd.clone.sunk | while | flops 1025769472 | bytes 66454976 | solution.py:314
  652.7 4.1 fusion.165
  669.5 4.1 fusion.165
  686.3 4.1 fusion.165
  703.1 4.1 fusion.165
  719.9 4.1 fusion.165
  736.6 4.1 fusion.165
  753.4 4.1 fusion.165
  770.2 4.1 fusion.165
  776.5 12.0 copy.90
  794.6 161.6 %reduce-scatter.22.cloned.1.call-done = bf16[128,1024]{1,0:T(8,128)(2,1)} async-done(((bf16[4096,1024]{1,0:T(8,128)(2,1)}), bf16[128,1024]{1,0:T(8,128)(2,1)}) %reduce-scatter.22.cloned.1.call-update) | async-done | bytes 262160
  957.3 5.4 convolution_convert_fusion
  964.9 5.2 fusion.33
  970.1 8.7 copy.92
  978.7 4.4 copy.100
  983.2 5.2 fusion.31
  988.4 5.1 fusion.32
  993.7 30.2 %reduce-scatter.20.cloned.1.call-done = bf16[384,1536]{1,0:T(8,128)(2,1)} async-done(((bf16[1536,1536]{1,0:T(8,128)(2,1)}), bf16[384,1536]{1,0:T(8,128)(2,1)}) %reduce-scatter.20.cloned.1.call-update) | async-done | bytes 1179664 | tf_op jit(solution)/shard_map/reduce_scatter | solution.py:348
  1023.9 78.1 %reduce-scatter.18.cloned.1.call-done = bf16[384,2560]{1,0:T(8,128)(2,1)} async-done(((bf16[1536,2560]{1,0:T(8,128)(2,1)}), bf16[384,2560]{1,0:T(8,128)(2,1)}) %reduce-scatter.18.cloned.1.call-update) | async-done | bytes 1966096 | tf_op jit(solution)/shard_map/reduce_scatter | solution.py:345
  1103.2 28.9 %reduce-scatter.26.cloned.1.call-done = bf16[384,16]{1,0:T(8,128)(2,1)} async-done(((bf16[1536,16]{1,0:T(8,128)(2,1)}), bf16[384,16]{1,0:T(8,128)(2,1)}) %reduce-scatter.26.cloned.1.call-update) | async-done | bytes 12304
  1133.1 36.2 %reduce-scatter.24.cloned.1.call-done = bf16[384,512]{1,0:T(8,128)(2,1)} async-done(((bf16[1536,512]{1,0:T(8,128)(2,1)}), bf16[384,512]{1,0:T(8,128)(2,1)}) %reduce-scatter.24.cloned.1.call-update) | async-done | bytes 393232
  1172.1 34.8 %reduce-scatter.14.cloned.1.call-done = bf16[1,384,512]{2,1,0:T(8,128)(2,1)} async-done(((bf16[1,1536,512]{2,1,0:T(8,128)(2,1)}), bf16[1,384,512]{2,1,0:T(8,128)(2,1)}) %reduce-scatter.14.cloned.1.call-update) | async-done | bytes 393232 | tf_op jit(solution)/shard_map/reduce_scatter | solution.py:362
  1208.9 35.7 %reduce-scatter.16.cloned.1.call-done = bf16[1,384,512]{2,1,0:T(8,128)(2,1)} async-done(((bf16[1,1536,512]{2,1,0:T(8,128)(2,1)}), bf16[1,384,512]{2,1,0:T(8,128)(2,1)}) %reduce-scatter.16.cloned.1.call-update) | async-done | bytes 393232 | tf_op jit(solution)/shard_map/reduce_scatter | solution.py:365
  1246.6 6.1 fusion.54
  1252.7 7.4 all-reduce.6
  1260.2 144.5 %all-reduce.4 = (bf16[384]{0:T(512)(128)(2,1)S(1)}, bf16[384]{0:T(512)(128)(2,1)S(1)}, bf16[384,16]{0,1:T(8,128)(2,1)S(1)}) all-reduce(bf16[384]{0:T(512)(128)(2,1)S(1)} %dynamic-slice.1, bf16[384]{0:T(512)(128)(2,1)S(1)} %dynamic-slice.3, bf16[384,16]{0,1:T(8,128)(2,1)S(1)} %copy.95), channel_id=1, replica_groups=mesh['ctx'=32,'wsh'=4] {'ctx'}, use_global_device_ids=true, to_apply=%region_30.32 | all-reduce | flops 6912 | bytes 27648 | tf_op jit(solution)/shard_map/psum | solution.py:341
  1407.6 147.9 %all-reduce.9.cloned.1.call-done = (bf16[384,2560]{1,0:T(8,128)(2,1)}, bf16[384,1536]{1,0:T(8,128)(2,1)}) async-done(((bf16[384,2560]{1,0:T(8,128)(2,1)}, bf16[384,1536]{1,0:T(8,128)(2,1)}), (bf16[384,2560]{1,0:T(8,128)(2,1)}, bf16[384,1536]{1,0:T(8,128)(2,1)})) %all-reduce.9.cloned.1.call-update) | async-done | bytes 3145744 | tf_op jit(solution)/shard_map/psum | solution.py:338
  1555.6 4.0 convert_element_type.258
  (553 shorter events, 288.9 us)
Async XLA Ops:
  7.2 78.9 %copy-start = (s32[4,4]{1,0:T(4,128)S(1)}, s32[4,4]{1,0:T(4,128)}, u32[]{:S(2)}) copy-start(s32[4,4]{1,0:T(4,128)} %param.22) | copy-start | bytes 196
  7.2 10.9 copy-start.5
  7.2 65.7 %all-gather.9.cloned.1.call-start = ((), (), s32[]{:S(2)}) async-start(), calls=%async_computation.11 | async-start | bytes 9830400 | tf_op jit(solution)/shard_map/all_gather | solution.py:75
  10.9 225.8 %all-gather.11.cloned.1.call-start = ((), (), s32[]{:S(2)}) async-start(), calls=%async_computation.12 | async-start | bytes 8650752 | tf_op jit(solution)/shard_map/all_gather | solution.py:101
  18.1 59.3 %copy-start.30 = (f32[1536]{0:T(1024)}, f32[1536]{0:T(1024)S(1)}, u32[]{:S(2)}) copy-start(f32[1536]{0:T(1024)S(1)} %reshape.547) | copy-start | bytes 18436
  18.8 58.6 %copy-start.42 = (f32[128]{0:T(128)}, f32[128]{0:T(128)S(1)}, u32[]{:S(2)}) copy-start(f32[128]{0:T(128)S(1)} %get-tuple-element.838) | copy-start | bytes 1540
  78.2 4.8 copy-start.49
  78.2 298.2 %all-gather.13.cloned.1.call-start = ((), (), s32[]{:S(2)}) async-start(), calls=%async_computation.13 | async-start | bytes 5898240 | tf_op jit(solution)/shard_map/all_gather | solution.py:76
  81.1 8.1 copy-start.57
  81.1 323.6 %all-gather.15.cloned.1.call-start = ((), (), s32[]{:S(2)}) async-start(), calls=%async_computation.14 | async-start | bytes 1966080 | tf_op jit(solution)/shard_map/all_gather | solution.py:85
  82.0 352.0 %all-gather.17.cloned.1.call-start = ((), (), s32[]{:S(2)}) async-start(), calls=%async_computation.15 | async-start | bytes 1966080 | tf_op jit(solution)/shard_map/all_gather | solution.py:86
  96.0 152.0 %copy-start.40 = (pred[16,32]{1,0:T(8,128)(4,1)}, pred[16,32]{1,0:T(8,128)(4,1)S(1)}, u32[]{:S(2)}) copy-start(pred[16,32]{1,0:T(8,128)(4,1)S(1)} %reduce_or.14) | copy-start | bytes 1540
  96.1 151.9 %copy-start.36 = (s32[16,32]{1,0:T(8,128)}, s32[16,32]{1,0:T(8,128)S(1)}, u32[]{:S(2)}) copy-start(s32[16,32]{1,0:T(8,128)S(1)} %reduce_sum.179) | copy-start | bytes 6148
  96.1 287.8 %copy-start.41 = (pred[16,32]{1,0:T(8,128)(4,1)}, pred[16,32]{1,0:T(8,128)(4,1)S(1)}, u32[]{:S(2)}) copy-start(pred[16,32]{1,0:T(8,128)(4,1)S(1)} %compare_and_fusion.3) | copy-start | bytes 1540
  381.0 97.0 %copy-start.12 = (bf16[128,1536]{1,0:T(8,128)(2,1)}, bf16[128,1536]{1,0:T(8,128)(2,1)S(1)}, u32[]{:S(2)}) copy-start(bf16[128,1536]{1,0:T(8,128)(2,1)S(1)} %multiply_convert_fusion.4) | copy-start | bytes 1179652
  387.6 16.3 %copy-start.29 = (f32[1,512,384]{2,1,0:T(8,128)S(1)}, f32[1,512,384]{2,1,0:T(8,128)}, u32[]{:S(2)}) copy-start(f32[1,512,384]{2,1,0:T(8,128)} %param.32) | copy-start | bytes 2359300
  387.6 40.9 %all-to-all-start = ((bf16[32,32,1536]{2,1,0:T(8,128)(2,1)}), bf16[32,32,1536]{2,1,0:T(8,128)(2,1)}, u32[]{:S(2)}, u32[]{:S(2)}) async-start(bf16[32,32,1536]{2,1,0:T(8,128)(2,1)} %bitcast.12), calls=%async_computation | async-start | bytes 6291456 | tf_op jit(solution)/shard_map/all_to_all | solution.py:201
  403.5 36.8 %all-gather.19.cloned.1.call-start = ((), (), s32[]{:S(2)}) async-start(), calls=%async_computation.16 | async-start | bytes 1966080 | tf_op jit(solution)/shard_map/all_gather | solution.py:87
  440.3 5.3 copy-start.63
  445.6 5.8 copy-start.22
  445.6 42.9 %all-to-all-start.1 = ((bf16[32,32,1536]{2,1,0:T(8,128)(2,1)}), bf16[32,32,1536]{2,1,0:T(8,128)(2,1)}, u32[]{:S(2)}, u32[]{:S(2)}) async-start(bf16[32,32,1536]{2,1,0:T(8,128)(2,1)} %bitcast.296), calls=%async_computation.1 | async-start | bytes 6291456 | tf_op jit(solution)/shard_map/all_to_all | solution.py:209
  454.5 4.9 copy-start.39
  476.8 16.9 %copy-start.32 = (bf16[1536,16]{0,1:T(8,128)(2,1)}, bf16[1536,16]{0,1:T(8,128)(2,1)S(1)}, u32[]{:S(2)}) copy-start(bf16[1536,16]{0,1:T(8,128)(2,1)S(1)} %all_gather.32) | copy-start | bytes 147460
  478.0 15.7 %copy-start.52 = (s32[1024]{0:T(1024)}, s32[1024]{0:T(1024)S(1)}, u32[]{:S(2)}) copy-start(s32[1024]{0:T(1024)S(1)} %get-tuple-element.847) | copy-start | bytes 12292
  478.0 15.7 %copy-start.51 = (s32[1024]{0:T(1024)}, s32[1024]{0:T(1024)S(1)}, u32[]{:S(2)}) copy-start(s32[1024]{0:T(1024)S(1)} %get-tuple-element.848) | copy-start | bytes 12292
  478.2 15.5 copy-start.55
  498.9 19.5 %copy-start.7 = (f32[512,1536]{1,0:T(8,128)S(1)}, f32[512,1536]{1,0:T(8,128)}, u32[]{:S(2)}) copy-start(f32[512,1536]{1,0:T(8,128)} %gather_fusion.2) | copy-start | bytes 9437188
  519.8 46.3 %copy-start.61 = (bf16[1,512,1536]{2,1,0:T(8,128)(2,1)S(1)}, bf16[1,512,1536]{2,1,0:T(8,128)(2,1)}, u32[]{:S(2)}) copy-start(bf16[1,512,1536]{2,1,0:T(8,128)(2,1)} %all-gather.19.cloned.1.call-done) | copy-start | bytes 4718596
  519.8 46.3 %copy-start.65 = (f32[1024,512]{1,0:T(8,128)S(1)}, f32[1024,512]{1,0:T(8,128)}, u32[]{:S(2)}) copy-start(f32[1024,512]{1,0:T(8,128)} %fusion.43) | copy-start | bytes 6291460
  519.8 46.3 %copy-start.66 = (f32[1024,512]{1,0:T(8,128)S(1)}, f32[1024,512]{1,0:T(8,128)}, u32[]{:S(2)}) copy-start(f32[1024,512]{1,0:T(8,128)} %get-tuple-element.844) | copy-start | bytes 6291460
  574.3 42.2 %all-to-all-start.3 = ((bf16[32,32,1536]{2,1,0:T(8,128)(2,1)}), bf16[32,32,1536]{2,1,0:T(8,128)(2,1)S(1)}, u32[]{:S(2)}, u32[]{:S(2)}) async-start(bf16[32,32,1536]{2,1,0:T(8,128)(2,1)} %bitcast.287), calls=%async_computation.3 | async-start | bytes 6291456 | tf_op jit(solution)/shard_map/all_to_all | solution.py:251
  580.0 376.2 %reduce-scatter.22.cloned.1.call-start = ((), (), s32[]{:S(2)}) async-start(), calls=%async_computation.21 | async-start | bytes 8650752
  584.6 43.7 %copy-start.37 = (bf16[128,16]{0,1:T(8,128)(2,1)}, bf16[128,16]{0,1:T(8,128)(2,1)S(1)}, u32[]{:S(2)}) copy-start(bf16[128,16]{0,1:T(8,128)(2,1)S(1)} %select_reduce_fusion.2) | copy-start | bytes 12292
  622.8 5.5 copy-start.9
  622.8 5.5 copy-start.33
  622.8 5.5 copy-start.54
  624.9 4.4 copy-start.19
  624.9 4.4 copy-start.23
  624.9 4.4 copy-start.59
  631.2 5.0 copy-start.18
  638.0 4.3 copy-start.35
  644.8 5.2 copy-start.2
  661.4 5.2 copy-start.2
  678.2 5.2 copy-start.2
  695.0 5.2 copy-start.2
  711.8 5.2 copy-start.2
  728.5 5.2 copy-start.2
  745.3 5.2 copy-start.2
  762.1 5.2 copy-start.2
  788.6 235.3 %reduce-scatter.20.cloned.1.call-start = ((), (), s32[]{:S(2)}) async-start(), calls=%async_computation.20 | async-start | bytes 5898240 | tf_op jit(solution)/shard_map/reduce_scatter | solution.py:348
  793.4 163.9 %copy-start.6 = (bf16[1,128,1536]{2,1,0:T(8,128)(2,1)S(1)}, bf16[1,128,1536]{2,1,0:T(8,128)(2,1)}, u32[]{:S(2)}) copy-start(bf16[1,128,1536]{2,1,0:T(8,128)(2,1)} %param.21) | copy-start | bytes 1179652
  793.4 163.9 %copy-start.31 = (f32[1536]{0:T(1024)S(1)}, f32[1536]{0:T(1024)}, u32[]{:S(2)}) copy-start(f32[1536]{0:T(1024)} %copy-done.30) | copy-start | bytes 18436
  793.4 163.9 %copy-start.43 = (f32[128]{0:T(128)S(1)}, f32[128]{0:T(128)}, u32[]{:S(2)}) copy-start(f32[128]{0:T(128)} %copy-done.42) | copy-start | bytes 1540
  793.4 308.6 %reduce-scatter.18.cloned.1.call-start = ((), (), s32[]{:S(2)}) async-start(), calls=%async_computation.19 | async-start | bytes 9830400 | tf_op jit(solution)/shard_map/reduce_scatter | solution.py:345
  962.8 169.3 %reduce-scatter.26.cloned.1.call-start = ((), (), s32[]{:S(2)}) async-start(), calls=%async_computation.23 | async-start | bytes 491520
  964.8 204.4 %reduce-scatter.24.cloned.1.call-start = ((), (), s32[]{:S(2)}) async-start(), calls=%async_computation.22 | async-start | bytes 1966080
  983.1 223.8 %reduce-scatter.14.cloned.1.call-start = ((), (), s32[]{:S(2)}) async-start(), calls=%async_computation.17 | async-start | bytes 1966080 | tf_op jit(solution)/shard_map/reduce_scatter | solution.py:362
  988.4 256.2 %reduce-scatter.16.cloned.1.call-start = ((), (), s32[]{:S(2)}) async-start(), calls=%async_computation.18 | async-start | bytes 1966080 | tf_op jit(solution)/shard_map/reduce_scatter | solution.py:365
  993.6 108.4 %copy-start.62 = (u32[128]{0:T(128)S(1)}, u32[128]{0:T(128)}, u32[]{:S(2)}) copy-start(u32[128]{0:T(128)} %constant.276) | copy-start | bytes 1540
  993.6 562.0 %all-reduce.9.cloned.1.call-start = ((), (), s32[]{:S(2)}) async-start(), calls=%async_computation.24 | async-start | bytes 6291456 | tf_op jit(solution)/shard_map/psum | solution.py:338
  1246.6 6.1 copy-start.45
  1246.6 160.0 %copy-start.58 = (f32[128]{0:T(128)S(1)}, f32[128]{0:T(128)}, u32[]{:S(2)}) copy-start(f32[128]{0:T(128)} %get-tuple-element.837) | copy-start | bytes 1540
  1555.6 4.1 copy-start.25
  1555.6 5.8 copy-start.1
  (69 other events, 178.7 us)
Sparse Core Ops, SparseCore 0:
  11.0 61.7 all-gather.8
  78.3 158.3 all-gather.10
  239.0 50.2 all-gather.12
  291.4 23.0 all-gather.14
  316.6 23.0 all-gather.16
  406.2 29.7 all-gather.18
  788.7 167.4 reduce-scatter.21
  958.8 65.0 reduce-scatter.19
  1026.7 75.2 reduce-scatter.17
  1105.0 27.0 reduce-scatter.25
  1134.8 34.4 reduce-scatter.23
  1172.5 34.4 reduce-scatter.13
  1210.1 34.4 reduce-scatter.15
  1247.2 308.3 all-reduce.8
where the time goes:
time: 1590 us; the launch traced here: 1570 us
  waiting for transfers between devices  809 us (51%)
  blocking collectives  229 us (14%)
  matrix products  214 us (13%)
  local copies, waits for them, and re-layouts  168 us (11%)
  other arithmetic  102 us (6%)
  starting transfers between devices  28.4 us (2%)
  between operations  15.9 us (1%)
    unnamed x17, waiting for transfers between devices  227 us
    psum x1, waiting for transfers between devices, body(): lax.psum(dense_grads[0].astype(jnp.bfloat16), 'ctx').astype(jnp.float32)  148 us
    psum x1, blocking collectives, body(): lax.psum(dense_grads[3].astype(jnp.bfloat16), 'ctx').astype(jnp.float32)  145 us
    all_gather x1, waiting for transfers between devices, body(): lax.all_gather(query_key_value[:, query_total_width:], 'ctx', axis=0, til...  140 us
    reduce_scatter x1, waiting for transfers between devices, body(): lax.psum_scatter(summed[0].astype(jnp.bfloat16), 'wsh', scatter_dimension...  78.1 us
    all_gather x1, waiting for transfers between devices, body(): lax.all_gather(w_qkv.astype(jnp.bfloat16), 'wsh', axis=0, tiled=True)  54.1 us
    unnamed x135, local copies, waits for them, and re-layouts  47 us
    all_to_all x1, blocking collectives, body(): lax.all_to_all(send_grads, 'ctx', split_axis=0, concat_axis=0, tiled=True)  46.3 us
  transfers between devices with their start and end apart: 17, of which 13 were waited for; matrix products, arithmetic and copies ran while one was open for 16% of the time, Pallas kernels for 0%

commit v1 on v0

v1 whole, which is shorter than its diff:
```python
import functools

import jax
import jax.numpy as jnp
from jax import lax
from jax.experimental import pallas as pl
from jax.experimental.pallas import tpu as pltpu
from jax.sharding import PartitionSpec as P

QUERY_HEADS = 24
KEY_VALUE_HEADS = 8
HEAD_SIZE = 64
GROUP = QUERY_HEADS // KEY_VALUE_HEADS
TOP = 2
BLOCK = 64
WIDTH = GROUP * HEAD_SIZE
HEAD_COLUMNS = WIDTH + 2 * HEAD_SIZE
CHUNK = 256

EPSILON = 1e-05
NEG_BIG = -1e30
BF = jnp.bfloat16
F32 = jnp.float32

ROW = [[y * 8 + r for r in range(8)] for y in range(4)]
COLUMN = [[y * 8 + r for y in range(4)] for r in range(8)]
NEAR = [[y * 8 + z * 4 + x for y in range(4) for z in range(2) for x in xs] for xs in ((0, 3), (1, 2))]
OWNERS = [[(2 * e + k) * 4 + w for k in range(2) for w in range(4)] for e in range(16)]
OTHER_HALF = [(c, c ^ 1) for c in range(32)]
OTHER_SIDE = [(w, w ^ 2) for w in range(4)]
OTHER_CORE = [(w, w ^ 1) for w in range(4)]
NEXT_Z = [(c * 4 + w, (c ^ 4) * 4 + (w ^ 2)) for c in range(32) for w in range(4)]
TERMS = [[(y * 8 + r) * 4 + w for y in range(4) for w in range(4)] for r in range(8)]
MOVES = [
    ((y * 8 + r) * 4 + w, ((r % 2) * 16 + y * 4 + w) * 4 + r // 2)
    for r in range(8)
    for y in range(4)
    for w in range(4)
]


def dot(a, b, dims=((1,), (0,))):
    return lax.dot_general(a, b, (dims, ((), ())), preferred_element_type=F32)


NT = ((1,), (1,))
TN = ((0,), (0,))


def block_range(meta, b):
    position = meta[BLOCK + b]
    base = position * BLOCK
    bounds = [meta[80 + i] for i in range(3)]
    lane = lax.broadcasted_iota(jnp.int32, (1, WIDTH), 1)
    query = base + (lane & (BLOCK - 1))
    start = jnp.zeros((1, WIDTH), jnp.int32)
    first = jnp.int32(0)
    for bound in bounds:
        start = jnp.where(query >= bound, bound, start)
        first = jnp.where(base >= bound, bound, first)
    first = (first // 128) * 128
    count = (base + BLOCK - first + CHUNK - 1) // CHUNK
    return query, start, first, count


def allowed_of(key_start, query, start):
    key = key_start + lax.broadcasted_iota(jnp.int32, (CHUNK, WIDTH), 0)
    return (key <= query) & (key >= start)


def stack_heads(rows):
    return jnp.concatenate([rows[:, g * HEAD_SIZE : (g + 1) * HEAD_SIZE] for g in range(GROUP)], axis=0)


def sort_blocks(meta, kv_ref, sorted_ref):
    total = kv_ref.shape[0]

    def one(p, carry):
        source = pl.multiple_of(meta[p] * BLOCK, BLOCK)
        target = pl.multiple_of(p * BLOCK, BLOCK)
        sorted_ref[pl.ds(target, BLOCK), :] = kv_ref[pl.ds(source, BLOCK), :]
        return carry

    lax.fori_loop(0, total // BLOCK, one, 0)
    sorted_ref[total:, :] = jnp.zeros((CHUNK, sorted_ref.shape[1]), sorted_ref.dtype)


def transpose_all(sorted_ref, turned_ref):
    steps = sorted_ref.shape[0] // CHUNK

    def one(i, carry):
        at = pl.multiple_of(i * CHUNK, CHUNK)
        turned_ref[:, pl.ds(at, CHUNK)] = sorted_ref[pl.ds(at, CHUNK), :].T
        return carry

    lax.fori_loop(0, steps, one, 0)


def attention_forward(meta, q_ref, kv_ref, o_ref, lse_ref, sorted_ref, turned_ref):
    sort_blocks(meta, kv_ref, sorted_ref)
    transpose_all(sorted_ref, turned_ref)
    zeros = jnp.zeros((WIDTH, HEAD_SIZE), BF)

    def tile(b, carry):
        query, start, first, count = block_range(meta, b)
        at = pl.multiple_of(b * BLOCK, BLOCK)
        rows = stack_heads(q_ref[pl.ds(at, BLOCK), :]) * jnp.asarray(HEAD_SIZE**-0.5, BF)
        padded = jnp.concatenate([rows, zeros], axis=1)

        def chunk(i, running):
            top, total, acc = running
            key_start = pl.multiple_of(first + i * CHUNK, 128)
            keys = sorted_ref[pl.ds(key_start, CHUNK), :]
            scores = dot(keys, padded, NT)
            scores = jnp.where(allowed_of(key_start, query, start), scores, NEG_BIG)
            top_new = jnp.maximum(top, jnp.max(scores, axis=0, keepdims=True))
            weights = jnp.exp(scores - top_new)
            fade = jnp.exp(top - top_new)
            total = total * fade + jnp.sum(weights, axis=0, keepdims=True)
            acc = acc * fade + dot(turned_ref[:, pl.ds(key_start, CHUNK)], weights.astype(BF))
            return top_new, total, acc

        top, total, acc = lax.fori_loop(
            0,
            count,
            chunk,
            (
                jnp.full((1, WIDTH), NEG_BIG, F32),
                jnp.zeros((1, WIDTH), F32),
                jnp.zeros((2 * HEAD_SIZE, WIDTH), F32),
            ),
        )
        lse_ref[pl.ds(b, 1), :] = top + jnp.log(total)
        result = (acc / total).T[:, HEAD_SIZE:].astype(BF)
        o_ref[pl.ds(at, BLOCK), :] = jnp.concatenate(
            [result[g * BLOCK : (g + 1) * BLOCK] for g in range(GROUP)], axis=1
        )
        return carry

    lax.fori_loop(0, q_ref.shape[0] // BLOCK, tile, 0)


def attention_backward(
    meta, q_ref, kv_ref, o_ref, lse_ref, do_ref, dq_ref, dkv_ref, sorted_ref, turned_ref, total_ref
):
    sort_blocks(meta, kv_ref, sorted_ref)
    transpose_all(sorted_ref, turned_ref)
    total_ref[...] = jnp.zeros_like(total_ref)
    zeros = jnp.zeros((WIDTH, HEAD_SIZE), BF)
    scaling = HEAD_SIZE**-0.5

    def tile(b, carry):
        query, start, first, count = block_range(meta, b)
        at = pl.multiple_of(b * BLOCK, BLOCK)
        rows = stack_heads(q_ref[pl.ds(at, BLOCK), :]) * jnp.asarray(scaling, BF)
        grad = stack_heads(do_ref[pl.ds(at, BLOCK), :])
        value = stack_heads(o_ref[pl.ds(at, BLOCK), :])
        delta = jnp.sum((grad.astype(F32) * value.astype(F32)).T, axis=0, keepdims=True)
        lse = lse_ref[pl.ds(b, 1), :]
        query_pad = jnp.concatenate([rows, zeros], axis=1)
        grad_pad = jnp.concatenate([zeros, grad], axis=1)
        both = jnp.concatenate([query_pad, grad_pad], axis=0)

        def chunk(i, acc):
            key_start = pl.multiple_of(first + i * CHUNK, 128)
            keys = sorted_ref[pl.ds(key_start, CHUNK), :]
            scores = dot(keys, query_pad, NT)
            probs = jnp.where(allowed_of(key_start, query, start), jnp.exp(scores - lse), 0.0)
            d_probs = dot(keys, grad_pad, NT)
            d_scores = (probs * (d_probs - delta)).astype(BF)
            joined = jnp.concatenate([d_scores, probs.astype(BF)], axis=1)
            total_ref[pl.ds(key_start, CHUNK), :] += dot(joined, both)
            return acc + dot(turned_ref[:, pl.ds(key_start, CHUNK)], d_scores)

        acc = lax.fori_loop(0, count, chunk, jnp.zeros((2 * HEAD_SIZE, WIDTH), F32))
        result = (acc * scaling).T[:, :HEAD_SIZE].astype(BF)
        dq_ref[pl.ds(at, BLOCK), :] = jnp.concatenate(
            [result[g * BLOCK : (g + 1) * BLOCK] for g in range(GROUP)], axis=1
        )
        return carry

    lax.fori_loop(0, q_ref.shape[0] // BLOCK, tile, 0)

    def back(p, carry):
        target = pl.multiple_of(meta[p] * BLOCK, BLOCK)
        source = pl.multiple_of(p * BLOCK, BLOCK)
        dkv_ref[pl.ds(target, BLOCK), :] = total_ref[pl.ds(source, BLOCK), :].astype(BF)
        return carry

    lax.fori_loop(0, kv_ref.shape[0] // BLOCK, back, 0)


def local_call(kernel, outs, n_vmem, scratch, name):
    return pl.pallas_call(
        kernel,
        out_shape=outs,
        in_specs=[pl.BlockSpec(memory_space=pltpu.SMEM)] + [pl.BlockSpec(memory_space=pltpu.VMEM)] * n_vmem,
        out_specs=tuple(pl.BlockSpec(memory_space=pltpu.VMEM) for _ in outs),
        scratch_shapes=scratch,
        compiler_params=pltpu.CompilerParams(vmem_limit_bytes=40 * 2**20),
        cost_estimate=pl.CostEstimate(flops=4 * 10**9, bytes_accessed=10**7, transcendentals=4 * 10**6),
        name=name,
    )


def run_forward(meta, q, kv):
    rows, keys = q.shape[0], kv.shape[0]
    return local_call(
        attention_forward,
        (jax.ShapeDtypeStruct((rows, WIDTH), BF), jax.ShapeDtypeStruct((rows // BLOCK, WIDTH), F32)),
        2,
        [pltpu.VMEM((keys + CHUNK, 2 * HEAD_SIZE), BF), pltpu.VMEM((2 * HEAD_SIZE, keys + CHUNK), BF)],
        "attention_forward",
    )(meta, q, kv)


def run_backward(meta, q, kv, o, lse, d_o):
    rows, keys = q.shape[0], kv.shape[0]
    return local_call(
        attention_backward,
        (jax.ShapeDtypeStruct((rows, WIDTH), BF), jax.ShapeDtypeStruct((keys, 2 * HEAD_SIZE), BF)),
        5,
        [
            pltpu.VMEM((keys + CHUNK, 2 * HEAD_SIZE), BF),
            pltpu.VMEM((2 * HEAD_SIZE, keys + CHUNK), BF),
            pltpu.VMEM((keys + CHUNK, 2 * HEAD_SIZE), F32),
        ],
        "attention_backward",
    )(meta, q, kv, o, lse, d_o)


def expert_forward_kernel(x_ref, w_ref, gate_ref, up_ref, hidden_ref, out_ref, acc_ref):
    step = pl.program_id(0)
    quarter = w_ref.shape[2]
    gate = up = 0.0
    for q in range(4):
        part = x_ref[:, q * quarter : (q + 1) * quarter]
        gate += dot(part, w_ref[q, 0])
        up += dot(part, w_ref[q, 1])
    gate_ref[...] = gate
    up_ref[...] = up
    hidden = (gate * jax.nn.sigmoid(gate) * up).astype(BF)
    hidden_ref[...] = hidden

    @pl.when(step == 0)
    def _():
        acc_ref[...] = jnp.zeros_like(acc_ref)

    for q in range(4):
        acc_ref[:, q * quarter : (q + 1) * quarter] += dot(hidden, w_ref[q, 2], NT)

    @pl.when(step == pl.num_programs(0) - 1)
    def _():
        out_ref[...] = acc_ref[...].astype(BF)


def expert_backward_kernel(g_ref, w_ref, gate_ref, up_ref, d_gate_ref, d_up_ref, out_ref, acc_ref):
    step = pl.program_id(0)
    quarter = w_ref.shape[2]
    d_hidden = 0.0
    for q in range(4):
        d_hidden += dot(g_ref[:, q * quarter : (q + 1) * quarter], w_ref[q, 2])
    gate, up = gate_ref[...], up_ref[...]
    sigmoid = jax.nn.sigmoid(gate)
    d_gate = (d_hidden * up * sigmoid * (1.0 + gate * (1.0 - sigmoid))).astype(BF)
    d_up = (d_hidden * (gate * sigmoid)).astype(BF)
    d_gate_ref[...] = d_gate
    d_up_ref[...] = d_up

    @pl.when(step == 0)
    def _():
        acc_ref[...] = jnp.zeros_like(acc_ref)

    for q in range(4):
        acc_ref[:, q * quarter : (q + 1) * quarter] += dot(d_gate, w_ref[q, 0], NT) + dot(d_up, w_ref[q, 1], NT)

    @pl.when(step == pl.num_programs(0) - 1)
    def _():
        out_ref[...] = acc_ref[...].astype(BF)


def expert_gradients_kernel(core_ref, x_ref, g_ref, hidden_ref, d_gate_ref, d_up_ref, out_ref):
    x = x_ref[...].T
    out_ref[0, 0, 0] = dot(x, d_gate_ref[...]).astype(BF)
    out_ref[0, 0, 1] = dot(x, d_up_ref[...]).astype(BF)
    out_ref[0, 0, 2] = dot(g_ref[...].T, hidden_ref[...]).astype(BF)


FF_STEP = 256


def expert_specs(rows, width, weights):
    halves = weights.shape[3] // FF_STEP
    whole = pl.BlockSpec((rows, width), lambda i: (0, 0))
    part = pl.BlockSpec((rows, FF_STEP), lambda i: (0, i))
    weight = pl.BlockSpec((4, 3, weights.shape[2], FF_STEP), lambda i: (i // halves, 0, 0, i % halves))
    return 2 * halves, whole, part, weight


def expert_forward(x, weights):
    rows, width = x.shape
    steps, whole, part, weight = expert_specs(rows, width, weights)
    wide = jax.ShapeDtypeStruct((rows, steps * FF_STEP), F32)
    return pl.pallas_call(
        expert_forward_kernel,
        out_shape=(wide, wide, jax.ShapeDtypeStruct(wide.shape, BF), jax.ShapeDtypeStruct(x.shape, BF)),
        grid=(steps,),
        in_specs=[whole, weight],
        out_specs=(part, part, part, whole),
        scratch_shapes=[pltpu.VMEM((rows, width), F32)],
        compiler_params=pltpu.CompilerParams(vmem_limit_bytes=40 * 2**20),
        cost_estimate=pl.CostEstimate(flops=5 * 10**9, bytes_accessed=16 * 10**6, transcendentals=10**6),
        name="expert_forward",
    )(x, weights)


def expert_backward(g, weights, gate, up):
    rows, width = g.shape
    steps, whole, part, weight = expert_specs(rows, width, weights)
    low = jax.ShapeDtypeStruct(gate.shape, BF)
    return pl.pallas_call(
        expert_backward_kernel,
        out_shape=(low, low, jax.ShapeDtypeStruct(g.shape, BF)),
        grid=(steps,),
        in_specs=[whole, weight, part, part],
        out_specs=(part, part, whole),
        scratch_shapes=[pltpu.VMEM((rows, width), F32)],
        compiler_params=pltpu.CompilerParams(vmem_limit_bytes=40 * 2**20),
        cost_estimate=pl.CostEstimate(flops=5 * 10**9, bytes_accessed=16 * 10**6, transcendentals=10**6),
        name="expert_backward",
    )(g, weights, gate, up)


def expert_gradients(core, x, g, hidden, d_gate, d_up):
    rows, width = x.shape
    half = hidden.shape[1] // 2
    quarter = width // 4
    part = pl.BlockSpec((rows, quarter), lambda k, z, core: (0, 2 * z + core[0]))
    row = pl.BlockSpec((rows, half), lambda k, z, core: (0, k))
    return pl.pallas_call(
        expert_gradients_kernel,
        out_shape=jax.ShapeDtypeStruct((2, 2, 3, quarter, half), BF),
        grid_spec=pltpu.PrefetchScalarGridSpec(
            num_scalar_prefetch=1,
            grid=(2, 2),
            in_specs=[part, part, row, row, row],
            out_specs=pl.BlockSpec((1, 1, 3, quarter, half), lambda k, z, core: (k, z, 0, 0, 0)),
        ),
        compiler_params=pltpu.CompilerParams(vmem_limit_bytes=40 * 2**20),
        cost_estimate=pl.CostEstimate(flops=3 * 10**9, bytes_accessed=8 * 10**6, transcendentals=0),
        name="expert_gradients",
    )(core.reshape(1).astype(jnp.int32), x, g, hidden, d_gate, d_up)


def assemble_kernel(by_row_ref, by_head_ref, qkv_ref, out_ref, rest_ref):
    heads = [by_row_ref[0, h].astype(F32) for h in range(8)]
    ends = (0, WIDTH, WIDTH + HEAD_SIZE, HEAD_COLUMNS)
    qkv_ref[...] = jnp.concatenate([t[:, a:b] for a, b in zip(ends[:-1], ends[1:]) for t in heads], axis=1)
    tail = heads[0]
    for t in heads[1:]:
        tail = tail + t
    rest_ref[...] = tail[:, HEAD_COLUMNS + WIDTH :]
    for parity in range(2):
        parts = [by_head_ref[parity, y, 0, :, HEAD_COLUMNS : HEAD_COLUMNS + WIDTH].astype(F32).T for y in range(4)]
        out_ref[parity * WIDTH : (parity + 1) * WIDTH, :] = jnp.concatenate(parts, axis=1)


def assemble(gathered):
    _, piece, columns = gathered.shape
    shard = 4 * piece
    return pl.pallas_call(
        assemble_kernel,
        out_shape=(
            jax.ShapeDtypeStruct((shard, 8 * HEAD_COLUMNS), F32),
            jax.ShapeDtypeStruct((2 * WIDTH, 4 * shard), F32),
            jax.ShapeDtypeStruct((shard, columns - HEAD_COLUMNS - WIDTH), F32),
        ),
        grid=(4,),
        in_specs=[
            pl.BlockSpec((1, 8, piece, columns), lambda i: (i, 0, 0, 0)),
            pl.BlockSpec((2, 4, 1, piece, columns), lambda i: (0, 0, i, 0, 0)),
        ],
        out_specs=(
            pl.BlockSpec((piece, 8 * HEAD_COLUMNS), lambda i: (i, 0)),
            pl.BlockSpec((2 * WIDTH, shard), lambda i: (0, i)),
            pl.BlockSpec((piece, columns - HEAD_COLUMNS - WIDTH), lambda i: (i, 0)),
        ),
        compiler_params=pltpu.CompilerParams(vmem_limit_bytes=40 * 2**20),
        name="assemble",
    )(gathered.reshape(4, 8, piece, columns), gathered.reshape(2, 4, 4, piece, columns))


MESH = pl.DeviceIdType.MESH
ANY = pl.BlockSpec(memory_space=pl.ANY)


class Copies:
    def __init__(self, send, recv, local):
        self.send, self.recv, self.local = send, recv, local
        self.remote_count = self.local_count = 0
        self.started, self.kept = [], []

    def to(self, source, target, device):
        k = self.remote_count
        self.remote_count += 1
        copy = pltpu.make_async_remote_copy(
            source, target, self.send.at[k], self.recv.at[k], device_id=device, device_id_type=MESH
        )
        copy.start()
        self.started.append(copy)
        return copy

    def keep(self, source, middle, target):
        k = self.local_count
        self.local_count += 2
        first = pltpu.make_async_copy(source, middle, self.local.at[k])
        first.start()
        self.kept.append((first, pltpu.make_async_copy(middle, target, self.local.at[k + 1])))

    def move_kept(self):
        for first, second in self.kept:
            first.wait()
            second.start()

    def finish(self, arrived):
        for copy in self.started:
            copy.wait_send()
            if not any(copy is other for other in arrived):
                copy.wait_recv()
        for _, second in self.kept:
            second.wait()


def meet(devices):
    barrier = pltpu.get_barrier_semaphore()
    for device in devices:
        pl.semaphore_signal(barrier, inc=1, device_id=device, device_id_type=MESH)
    pl.semaphore_wait(barrier, len(devices))


def gather_rows_kernel(
    tok_ref, wp_ref, gain_ref, wo_ref, tok_out, wp_out, gain_out, wo_out, v_tok, v_wp, v_gain, v_wo, send, recv, local
):
    place, stream = lax.axis_index("ctx"), lax.axis_index("wsh")
    x, z = place % 4, (place // 4) % 2
    right, left = {"ctx": place - x + (x + 1) % 4}, {"ctx": place - x + (x + 3) % 4}
    across = place + 4 - 8 * z
    other = {"wsh": stream + 1 - 2 * (stream % 2)}
    far = {"ctx": across, "wsh": (stream + 2) % 4}
    meet([right, left, {"ctx": across}, other, far])
    copies = Copies(send, recv, local)
    half = tok_ref.shape[0] // 2
    own, own_z = z * 4 + x, (1 - z) * 4 + x
    left_id, right_id = z * 4 + (x + 3) % 4, z * 4 + (x + 1) % 4
    left_z, right_z = (1 - z) * 4 + (x + 3) % 4, (1 - z) * 4 + (x + 1) % 4

    def rows(ref, h):
        return ref.at[pl.ds(h * half, half)]

    def spot(block, h):
        return tok_out.at[block, pl.ds(h * half, half)]

    head = place % 8
    far_wp = copies.to(wp_ref.at[across % 8], wp_out.at[stream], far)
    far_gain = copies.to(gain_ref, gain_out.at[stream], far)
    cross = [copies.to(rows(tok_ref, h), spot(own, h), {"ctx": across}) for h in range(2)]
    to_right = [copies.to(rows(tok_ref, h), spot(own, h), right) for h in (0, 1)]
    to_left = [copies.to(rows(tok_ref, h), spot(own, h), left) for h in (1, 0)]
    copies.to(wp_ref.at[head], wp_out.at[stream], other)
    copies.to(gain_ref, gain_out.at[stream], other)
    third = wo_ref.shape[0] // 3
    parts = [pl.ds(i * third, third) for i in range(3)]
    far_wo = [copies.to(wo_ref.at[p], wo_out.at[stream, p], far) for p in parts]
    copies.to(wo_ref, wo_out.at[stream], other)
    copies.keep(tok_ref, v_tok, tok_out.at[own])
    copies.keep(wp_ref.at[head], v_wp, wp_out.at[stream])
    copies.keep(gain_ref, v_gain, gain_out.at[stream])
    copies.keep(wo_ref, v_wo, wo_out.at[stream])
    copies.move_kept()

    arrived = []

    def arrive(copy):
        copy.wait_recv()
        arrived.append(copy)

    far_stream = (stream + 2) % 4
    arrive(far_wp)
    copies.to(wp_out.at[far_stream], wp_out.at[far_stream], other)
    arrive(far_gain)
    copies.to(gain_out.at[far_stream], gain_out.at[far_stream], other)
    arrive(to_right[0])
    copies.to(spot(left_id, 0), spot(left_id, 0), right)
    arrive(to_left[0])
    copies.to(spot(right_id, 1), spot(right_id, 1), left)
    arrive(cross[0])
    arrive(cross[1])
    z_right = [copies.to(spot(own_z, h), spot(own_z, h), right) for h in (0, 1)]
    z_left = [copies.to(spot(own_z, h), spot(own_z, h), left) for h in (1, 0)]
    arrive(z_right[0])
    copies.to(spot(left_z, 0), spot(left_z, 0), right)
    arrive(z_left[0])
    copies.to(spot(right_z, 1), spot(right_z, 1), left)
    for p, copy in zip(parts, far_wo):
        arrive(copy)
        copies.to(wo_out.at[far_stream, p], wo_out.at[far_stream, p], other)
    copies.finish(arrived)


def gather_rows(tok, wp, gain, wo):
    return pl.pallas_call(
        gather_rows_kernel,
        out_shape=(
            jax.ShapeDtypeStruct((8,) + tok.shape, BF),
            jax.ShapeDtypeStruct((4,) + wp.shape[1:], BF),
            jax.ShapeDtypeStruct((4,) + gain.shape, BF),
            jax.ShapeDtypeStruct((4,) + wo.shape, BF),
        ),
        in_specs=[ANY] * 4,
        out_specs=(ANY,) * 4,
        scratch_shapes=[
            pltpu.VMEM(tok.shape, BF),
            pltpu.VMEM(wp.shape[1:], BF),
            pltpu.VMEM(gain.shape, BF),
            pltpu.VMEM(wo.shape, BF),
            pltpu.SemaphoreType.DMA((27,)),
            pltpu.SemaphoreType.DMA((27,)),
            pltpu.SemaphoreType.DMA((8,)),
        ],
        compiler_params=pltpu.CompilerParams(collective_id=1, has_side_effects=True, vmem_limit_bytes=40 * 2**20),
        name="gather_rows",
    )(tok, wp, gain, wo)


def gather_keys_kernel(kv_ref, kv_out, v_kv, send, recv, local):
    place = lax.axis_index("ctx")
    y = place // 8
    up, down = {"ctx": (place + 8) % 32}, {"ctx": (place + 24) % 32}
    meet([up, down])
    copies = Copies(send, recv, local)
    half = kv_ref.shape[0] // 2

    def rows(h):
        return kv_ref.at[pl.ds(h * half, half)]

    def spot(block, h):
        return kv_out.at[block, pl.ds(h * half, half)]

    to_up = [copies.to(rows(h), spot(y, h), up) for h in (0, 1)]
    to_down = [copies.to(rows(h), spot(y, h), down) for h in (1, 0)]
    copies.keep(kv_ref, v_kv, kv_out.at[y])
    copies.move_kept()
    to_up[0].wait_recv()
    copies.to(spot((y + 3) % 4, 0), spot((y + 3) % 4, 0), up)
    to_down[0].wait_recv()
    copies.to(spot((y + 1) % 4, 1), spot((y + 1) % 4, 1), down)
    copies.finish([to_up[0], to_down[0]])


def gather_keys(kv):
    return pl.pallas_call(
        gather_keys_kernel,
        out_shape=jax.ShapeDtypeStruct((4,) + kv.shape, BF),
        in_specs=[ANY],
        out_specs=ANY,
        scratch_shapes=[
            pltpu.VMEM(kv.shape, BF),
            pltpu.SemaphoreType.DMA((6,)),
            pltpu.SemaphoreType.DMA((6,)),
            pltpu.SemaphoreType.DMA((2,)),
        ],
        compiler_params=pltpu.CompilerParams(collective_id=2, has_side_effects=True, vmem_limit_bytes=40 * 2**20),
        name="gather_keys",
    )(kv)


def prepare_kernel(qkv_ref, router_ref, wo_ref, wp_out, wo_out):
    rows = qkv_ref.shape[0]
    experts = router_ref.shape[1]
    wo_out[...] = wo_ref[...].astype(BF)
    router = router_ref[...].astype(BF)
    tail = jnp.zeros((rows, wp_out.shape[2] - HEAD_COLUMNS - experts), BF)
    k_at, v_at = QUERY_HEADS * HEAD_SIZE, (QUERY_HEADS + KEY_VALUE_HEADS) * HEAD_SIZE
    for h in range(KEY_VALUE_HEADS):
        wp_out[h] = jnp.concatenate(
            [
                qkv_ref[:, h * WIDTH : (h + 1) * WIDTH].astype(BF),
                qkv_ref[:, k_at + h * HEAD_SIZE : k_at + (h + 1) * HEAD_SIZE].astype(BF),
                qkv_ref[:, v_at + h * HEAD_SIZE : v_at + (h + 1) * HEAD_SIZE].astype(BF),
                router,
                tail,
            ],
            axis=1,
        )


def prepare(w_qkv, w_router, w_out):
    shard = w_qkv.shape[0]
    step = shard // 3

    def block(n):
        return pl.BlockSpec((step, n), lambda i: (i, 0))

    return pl.pallas_call(
        prepare_kernel,
        out_shape=(
            jax.ShapeDtypeStruct((KEY_VALUE_HEADS, shard, 384), BF),
            jax.ShapeDtypeStruct(w_out.shape, BF),
        ),
        grid=(3,),
        in_specs=[block(w_qkv.shape[1]), block(w_router.shape[1]), block(w_out.shape[1])],
        out_specs=(
            pl.BlockSpec((KEY_VALUE_HEADS, step, 384), lambda i: (0, i, 0)),
            block(w_out.shape[1]),
        ),
        compiler_params=pltpu.CompilerParams(vmem_limit_bytes=40 * 2**20),
        name="prepare",
    )(w_qkv, w_router, w_out)


def input_gradient_kernel(stream_ref, d_qkv_ref, p0, p1, p2, p3, x_ref, d_mid_ref, gain_ref, out_ref, acc_ref):
    step = pl.program_id(0)
    stream = stream_ref[0]

    @pl.when(step == 0)
    def _():
        acc_ref[...] = jnp.zeros_like(acc_ref)

    grad = d_qkv_ref[0]
    for j, piece in enumerate((p0, p1, p2, p3)):
        acc_ref[stream ^ j] += dot(grad, piece[0, :, :HEAD_COLUMNS], NT)

    @pl.when(step == pl.num_programs(0) - 1)
    def _():
        x = x_ref[...].astype(F32)
        scale = rms_scale(x)
        quarter = acc_ref.shape[2]
        inner = 0.0
        for q in range(4):
            at = slice(q * quarter, (q + 1) * quarter)
            inner += jnp.sum(acc_ref[q] * gain_ref[:, at] * x[:, at], axis=-1, keepdims=True)
        inner = inner * (1.0 / x.shape[1])
        for q in range(4):
            at = slice(q * quarter, (q + 1) * quarter)
            out_ref[:, at] = (
                d_mid_ref[:, at] + scale * (acc_ref[q] * gain_ref[:, at]) - x[:, at] * scale**3 * inner
            ).astype(BF)


def input_gradient(stream, d_qkv, pieces, x, d_middle, gain):
    heads, rows, _ = d_qkv.shape
    width = x.shape[1]

    def whole(a):
        return pl.BlockSpec(a.shape, lambda h, s: (0, 0))

    def by_head(a):
        return pl.BlockSpec((1,) + a.shape[1:], lambda h, s: (h, 0, 0))

    gain = gain.reshape(1, width)
    return pl.pallas_call(
        input_gradient_kernel,
        out_shape=jax.ShapeDtypeStruct(x.shape, BF),
        grid_spec=pltpu.PrefetchScalarGridSpec(
            num_scalar_prefetch=1,
            grid=(heads,),
            in_specs=[by_head(d_qkv)] + [by_head(p) for p in pieces] + [whole(x), whole(d_middle), whole(gain)],
            out_specs=whole(x),
            scratch_shapes=[pltpu.VMEM((4, rows, width // 4), F32)],
        ),
        compiler_params=pltpu.CompilerParams(vmem_limit_bytes=40 * 2**20),
        cost_estimate=pl.CostEstimate(flops=10**9, bytes_accessed=12 * 10**6, transcendentals=0),
        name="input_gradient",
    )(stream.reshape(1).astype(jnp.int32), d_qkv, *pieces, x, d_middle, gain)


def swap(x, groups, axis="ctx"):
    return lax.all_to_all(x, axis, 0, 0, axis_index_groups=groups, tiled=True)


def spread(x, groups, count, axis="ctx"):
    return swap(jnp.broadcast_to(x[None], (count,) + x.shape), groups, axis)


def rms_scale(values):
    return lax.rsqrt(jnp.mean(values * values, axis=-1, keepdims=True) + EPSILON)


def body(
    tokens,
    lengths,
    deal,
    expert_ids,
    gain_attn,
    w_qkv,
    w_out,
    gain_moe,
    w_router,
    w_gate,
    w_up,
    w_down,
    cotangent,
):
    stream = lax.axis_index("wsh")
    place = lax.axis_index("ctx")
    rows, width = tokens.shape[1], tokens.shape[2]
    shard = w_qkv.shape[0]
    experts = w_router.shape[1]
    capacity = 2 * rows * TOP // experts
    head = place % 8
    head_row = place // 8
    lengths_row = lax.dynamic_index_in_dim(lengths, stream, 0, keepdims=False)
    deal_row = lax.dynamic_index_in_dim(deal, stream, 0, keepdims=False)
    blocks = deal_row.shape[0]
    block_ids = jnp.arange(blocks, dtype=jnp.int32)
    inverse = jnp.sum(jnp.where(deal_row[None, :] == block_ids[:, None], block_ids[None, :], 0), axis=1)
    own_blocks = lax.dynamic_slice_in_dim(deal_row, head_row * 16, 16)
    meta = jnp.concatenate([inverse, own_blocks, jnp.cumsum(lengths_row)]).astype(jnp.int32)

    q_columns = QUERY_HEADS * HEAD_SIZE
    by_head, own_out = prepare(w_qkv, w_router, w_out)
    own_gains = jnp.concatenate(
        [gain_attn.astype(BF)[None], gain_moe.astype(BF)[None], jnp.zeros((14, shard), BF)], axis=0
    )
    group_tokens, head_full, gains, full_out = gather_rows(tokens[0], by_head, own_gains, own_out)
    head_full = head_full.reshape(width, -1)
    head_weight = head_full[:, :HEAD_COLUMNS]
    full_router = head_full[:, HEAD_COLUMNS : HEAD_COLUMNS + experts]
    gain_first = gains[:, 0].reshape(width).astype(F32)
    gain_second = gains[:, 1].reshape(width).astype(F32)
    full_out = full_out.reshape(q_columns, width)

    w_gate, w_up, w_down, _ = lax.optimization_barrier((w_gate, w_up, w_down, gains))
    expert_shard = jnp.stack([w_gate[0].astype(BF), w_up[0].astype(BF), w_down[0].T.astype(BF)])
    expert_all = lax.all_gather(expert_shard, ("ctx", "wsh"), axis_index_groups=OWNERS)
    far_qkv = lax.ppermute(by_head, ("ctx", "wsh"), NEXT_Z)
    qkv_pieces = [
        by_head,
        lax.ppermute(by_head, "wsh", OTHER_CORE),
        far_qkv,
        lax.ppermute(far_qkv, "wsh", OTHER_CORE),
    ]

    group_x = group_tokens.reshape(8 * rows, width).astype(F32)
    group_act = (group_x * rms_scale(group_x) * gain_first).astype(BF)
    head_qkv = dot(group_act, head_weight).astype(BF)
    kv_all = gather_keys(head_qkv[:, WIDTH:]).reshape(32 * rows, 2 * HEAD_SIZE)
    head_q = head_qkv[:, :WIDTH]
    head_attn, lse = run_forward(meta, head_q, kv_all)
    attn_low = swap(head_attn.reshape(8, rows, WIDTH), ROW).transpose(1, 0, 2).reshape(rows, q_columns)

    x_first = tokens[0].astype(F32)
    middle = x_first + dot(attn_low, full_out)
    scale_second = rms_scale(middle)
    act_moe = (middle * scale_second * gain_second).astype(BF)
    logits = dot(act_moe, full_router)
    choice = expert_ids[0]
    expert_range = jnp.arange(experts, dtype=jnp.int32)
    picked_hot = choice[:, :, None] == expert_range[None, None, :]
    picked = jnp.sum(jnp.where(picked_hot, logits[:, None, :], 0.0), axis=-1)
    picked_exp = jnp.exp(picked - jnp.max(picked, axis=-1, keepdims=True))
    gates = picked_exp / jnp.sum(picked_exp, axis=-1, keepdims=True)
    flat_ids = choice.reshape(-1)
    assign_hot = (flat_ids[:, None] == expert_range[None, :]).astype(jnp.int32)
    ranks = jnp.sum((jnp.cumsum(assign_hot, axis=0) - 1) * assign_hot, axis=1)
    slots = (flat_ids * capacity + ranks).reshape(rows, TOP)
    slot_range = jnp.arange(experts * capacity, dtype=jnp.int32)
    hot = [slots[:, j][:, None] == slot_range[None, :] for j in range(TOP)]
    hot_low = [h.astype(BF) for h in hot]
    hot_any = hot_low[0] + hot_low[1]
    slot_gate = sum(jnp.sum(jnp.where(hot[j], gates[:, j][:, None], 0.0), axis=0) for j in range(TOP))

    send_rows = dot(hot_any, act_moe, TN).astype(BF).reshape(experts, capacity, width)
    send_grads = (slot_gate[:, None] * dot(hot_any, cotangent[0], TN)).astype(BF)
    inputs = swap(send_rows, NEAR).reshape(-1, width)
    inputs, send_grads, expert_all = lax.optimization_barrier((inputs, send_grads, expert_all))
    recv_grads = swap(send_grads.reshape(experts, capacity, width), NEAR).reshape(-1, width)
    pre_gate, pre_up, hidden, expert_out = expert_forward(inputs, expert_all)
    expert_out, recv_grads = lax.optimization_barrier((expert_out, recv_grads))
    back_rows = swap(expert_out.reshape(experts, capacity, width), NEAR).reshape(-1, width)
    d_pre_gate, d_pre_up, d_inputs = expert_backward(recv_grads, expert_all, pre_gate, pre_up)
    d_inputs, d_pre_gate, back_rows, qkv_pieces = lax.optimization_barrier(
        (d_inputs, d_pre_gate, back_rows, qkv_pieces)
    )
    returned = swap(d_inputs.reshape(experts, capacity, width), NEAR).reshape(-1, width)
    core = stream % 2
    send_terms = expert_gradients(1 - core, inputs, recv_grads, hidden, d_pre_gate, d_pre_up)
    recv_terms = lax.ppermute(send_terms, "wsh", OTHER_CORE)
    keep_terms = expert_gradients(core, inputs, recv_grads, hidden, d_pre_gate, d_pre_up)
    returned, keep_terms, recv_terms = lax.optimization_barrier((returned, keep_terms, recv_terms))
    expert_terms = (keep_terms.astype(F32) + recv_terms.astype(F32)).astype(BF)
    half = place % 2
    recv_terms = lax.ppermute(
        lax.dynamic_index_in_dim(expert_terms, 1 - half, 0, keepdims=False), "ctx", OTHER_HALF
    )
    keep_terms = lax.dynamic_index_in_dim(expert_terms, half, 0, keepdims=False)
    expert_terms = (keep_terms.astype(F32) + recv_terms.astype(F32)).astype(BF)
    side = stream // 2
    recv_terms = lax.ppermute(
        lax.dynamic_index_in_dim(expert_terms, 1 - side, 0, keepdims=False), "wsh", OTHER_SIDE
    )
    expert_own = lax.dynamic_index_in_dim(expert_terms, side, 0, keepdims=False).astype(F32) + recv_terms.astype(F32)

    both = [dot(hot_low[j], back_rows) for j in range(TOP)]
    output_rows = (middle + gates[:, :1] * both[0] + gates[:, 1:] * both[1]).astype(BF)
    d_out = cotangent[0].astype(F32)
    d_gates = jnp.stack([jnp.sum(d_out * both[j], axis=-1) for j in range(TOP)], axis=1)
    d_picked = gates * (d_gates - jnp.sum(gates * d_gates, axis=-1, keepdims=True))
    d_logits = jnp.sum(jnp.where(picked_hot, d_picked[:, :, None], 0.0), axis=1).astype(BF)
    d_act_moe = dot(hot_any, returned) + dot(d_logits, full_router, NT)
    d_router_local = dot(act_moe, d_logits, TN)
    d_gain_second = jnp.sum(d_act_moe * middle * scale_second, axis=0)
    scaled = d_act_moe * gain_second
    d_middle = (
        d_out
        + scale_second * scaled
        - middle * scale_second**3 * jnp.mean(scaled * middle, axis=-1, keepdims=True)
    )
    d_branch = d_middle.astype(BF)

    d_attn = dot(d_branch, full_out, NT).astype(BF)
    head_d_attn = swap(d_attn.reshape(rows, 8, WIDTH).transpose(1, 0, 2), ROW).reshape(8 * rows, WIDTH)
    group_branch = lax.all_gather(d_branch, "ctx", axis_index_groups=ROW).reshape(8 * rows, width)
    d_q, d_kv = run_backward(meta, head_q, kv_all, head_attn, lse, head_d_attn)
    d_kv_own = jnp.sum(swap(d_kv.reshape(4, 8 * rows, 2 * HEAD_SIZE), COLUMN).astype(F32), axis=0).astype(BF)
    head_d_qkv = jnp.concatenate([d_q, d_kv_own], axis=1)
    d_qkv = swap(head_d_qkv.reshape(8, rows, HEAD_COLUMNS), ROW)
    d_tokens = input_gradient(stream, d_qkv, qkv_pieces, tokens[0], d_middle, gain_first)

    term = jnp.concatenate(
        [
            dot(group_act, head_d_qkv, TN).astype(BF),
            dot(group_branch, head_attn, TN).astype(BF),
            d_router_local.astype(BF),
            d_gain_second.astype(BF)[:, None],
            jnp.zeros((width, 111), BF),
        ],
        axis=1,
    )
    columns = term.shape[1]
    piece = shard // 4
    term = term.reshape(4, 4, piece, columns).transpose(1, 0, 2, 3).reshape(16, piece, columns)
    summed = jnp.sum(swap(term, TERMS, ("ctx", "wsh")).astype(F32), axis=0).astype(BF)
    out_piece = lax.ppermute(summed[:, HEAD_COLUMNS : HEAD_COLUMNS + WIDTH], ("ctx", "wsh"), MOVES)
    summed = jnp.concatenate([summed[:, :HEAD_COLUMNS], out_piece, summed[:, HEAD_COLUMNS + WIDTH :]], axis=1)
    summed, expert_own = lax.optimization_barrier((summed, expert_own))
    gathered = spread(summed, None, 32)
    d_w_qkv, d_w_out, rest = assemble(gathered)
    d_gain_first = jnp.sum(d_w_qkv * w_qkv.astype(BF).astype(F32), axis=1) / gain_attn.astype(BF).astype(F32)
    return (
        output_rows[None],
        d_tokens[None],
        d_gain_first,
        d_w_qkv,
        d_w_out,
        rest[:, experts],
        rest[:, :experts],
        expert_own[0][None],
        expert_own[1][None],
        expert_own[2].T[None],
    )


def solution(mesh):
    placed = (
        P("wsh", "ctx", None),
        P(),
        P(),
        P("wsh", "ctx", None),
        P("wsh"),
        P("wsh", None),
        P("wsh", None),
        P("wsh"),
        P("wsh", None),
        P("ctx", "wsh", None),
        P("ctx", "wsh", None),
        P("ctx", None, "wsh"),
        P("wsh", "ctx", None),
    )
    return jax.shard_map(
        body,
        mesh=mesh,
        in_specs=placed,
        out_specs=(
            P("wsh", "ctx", None),
            P("wsh", "ctx", None),
            P("wsh"),
            P("wsh", None),
            P("wsh", None),
            P("wsh"),
            P("wsh", None),
            P("ctx", "wsh", None),
            P("ctx", "wsh", None),
            P("ctx", None, "wsh"),
        ),
        check_vma=False,
    )
```

time: 1590 us -> 528 us (0.33)
  waiting for transfers between devices: 809 us -> 98.5 us
  blocking collectives: 229 us -> 0 us
  Pallas kernels: 0 us -> 179 us
  matrix products: 214 us -> 35.8 us
  local copies, waits for them, and re-layouts: 168 us -> 77.6 us
  other arithmetic: 102 us -> 34.8 us
  starting transfers between devices: 28.4 us -> 79 us
    unnamed x17 -> x2, waiting for transfers between devices: 227 us -> 0.03 us
    all_gather x6 -> x2, waiting for transfers between devices: 194 us -> 0.01 us  [the longest x1 0.01 us: body(): lax.all_gather(expert_shard, ('ctx', 'wsh'), axis_index_groups=OWNERS)]
    pallas_call x0 -> x11, Pallas kernels: none -> 179 us  [the longest x1 41 us: gather_rows(): pl.pallas_call(gather_rows_kernel, out_shape=(jax.ShapeDtypeStruct((8,) +...]
    reduce_scatter x4 -> x0, waiting for transfers between devices: 179 us -> none  [the longest x1 78.1 us: body(): lax.psum_scatter(summed[0].astype(jnp.bfloat16), 'wsh', scatter_dimension...]
    dot_general x74 -> x13, matrix products: 214 us -> 35.8 us  [dot(): return lax.dot_general(a, b, (dims, ((), ())), preferred_element_type=F32)]
    psum x1 -> x0, waiting for transfers between devices: 148 us -> none  [body(): lax.psum(dense_grads[0].astype(jnp.bfloat16), 'ctx').astype(jnp.float32)]
    psum x1 -> x0, blocking collectives: 145 us -> none  [body(): lax.psum(dense_grads[3].astype(jnp.bfloat16), 'ctx').astype(jnp.float32)]
    all_to_all x1 -> x0, blocking collectives: 46.3 us -> none  [body(): lax.all_to_all(send_grads, 'ctx', split_axis=0, concat_axis=0, tiled=True)]
  transfers between devices with their start and end apart: 17 -> 19, of which waited for: 13 -> 10; matrix products, arithmetic and copies ran while one was open for 16% -> 18% of each run, Pallas kernels for 0% -> 24%
where the time goes in v1:
time: 528 us; the launch traced here: 519 us
  Pallas kernels  179 us (34%)
  waiting for transfers between devices  98.5 us (19%)
  starting transfers between devices  79 us (15%)
  local copies, waits for them, and re-layouts  77.6 us (15%)
  matrix products  35.8 us (7%)
  other arithmetic  34.8 us (7%)
  between operations  14.9 us (3%)
    all_to_all x10, waiting for transfers between devices, swap(): return lax.all_to_all(x, axis, 0, 0, axis_index_groups=groups, tiled=True)  83.9 us
    all_to_all x10, starting transfers between devices, swap(): return lax.all_to_all(x, axis, 0, 0, axis_index_groups=groups, tiled=True)  65.3 us
    pallas_call x1, Pallas kernels, gather_rows(): pl.pallas_call(gather_rows_kernel, out_shape=(jax.ShapeDtypeStruct((8,) +...  41 us
    pallas_call x1, Pallas kernels, run_backward(): local_call(attention_backward, (jax.ShapeDtypeStruct((rows, WIDTH), BF),...  37.9 us
    unnamed x150, local copies, waits for them, and re-layouts  37.5 us
    dot_general x13, matrix products, dot(): return lax.dot_general(a, b, (dims, ((), ())), preferred_element_type=F32)  35.8 us
    pallas_call x1, Pallas kernels, run_forward(): local_call(attention_forward, (jax.ShapeDtypeStruct((rows, WIDTH), BF), j...  32.5 us
    pallas_call x1, Pallas kernels, expert_backward(): pl.pallas_call(expert_backward_kernel, out_shape=(low, low, jax.ShapeDtyp...  15.4 us
  transfers between devices with their start and end apart: 19, of which 10 were waited for; matrix products, arithmetic and copies ran while one was open for 18% of the time, Pallas kernels for 24%

profile of v1, /device:TPU:8, one launch (start us, length us, event | category | flops | bytes accessed | tf_op | source)
XLA Modules:
  0.0 519.3 jit_solution(2829303374399892196)
XLA Ops:
  9.6 2.1 copy-done.3
  14.5 41.0 %gather_rows.1 = (bf16[8,128,1536]{2,1,0:T(8,128)(2,1)S(1)}, bf16[4,384,384]{2,1,0:T(8,128)(2,1)S(1)}, bf16[4,16,384]{2,1,0:T(8,128)(2,1)S(1)}, bf16[4,384,1536]{2,1,0:T(8,128)(2,1)S(1)}) custom-call(bf16[128,1536]{1,0:T(8,128)(2,1)S(1)} %bitcast.125, bf16[8,384,384]{2,1,0:T(8,128)(2,1)S(1)} %get-tuple-element.79.wp_ref.p0, ...), custom_call_target="tpu_custom_call" | custom-call | tf_op jit(solution)/shard_map/gather_rows/pallas_call | solution.py:511
  55.5 2.2 copy-done.2
  59.4 2.0 copy.104
  72.7 12.7 %gather_keys.1 = bf16[4,1024,128]{2,1,0:T(8,128)(2,1)S(1)} custom-call(bf16[1024,128]{1,0:T(8,128)(2,1)S(1)} %slice.84.kv_ref), custom_call_target="tpu_custom_call" | custom-call | tf_op jit(solution)/shard_map/gather_keys/pallas_call | solution.py:561
  85.7 32.5 %attention_forward.1 = (bf16[1024,192]{1,0:T(8,128)(2,1)S(1)}, f32[16,192]{1,0:T(8,128)S(1)}) custom-call(s32[84]{0:T(128)S(1)} %pad_add_fusion.meta, bf16[1024,192]{1,0:T(8,128)(2,1)S(1)} %slice.83.q_ref, bf16[4096,128]{1,0:T(8,128)(2,1)S(1)} %bitcast.129), custom_call_target="tpu_custom_call" | custom-call | flops 4000000000 | bytes 10000000 | tf_op jit(solution)/shard_map/attention_forward/pallas_call | solution.py:208
  119.1 4.3 all-to-all-start
  125.2 6.3 %all-to-all-done = bf16[8,128,192]{1,2,0:T(8,128)(2,1)S(1)} async-done(((bf16[8,128,192]{1,2,0:T(8,128)(2,1)}), bf16[8,128,192]{1,2,0:T(8,128)(2,1)S(1)}, u32[]{:S(2)}, u32[]{:S(2)}) %all-to-all-start) | async-done | bytes 393248 | tf_op jit(solution)/shard_map/all_to_all | solution.py:678
  131.4 3.2 multiply_reduce_fusion.4
  135.4 1.8 convolution_convert_fusion
  137.3 4.3 all-to-all-start.1
  144.0 3.0 fusion.3
  147.0 12.8 %all-to-all-done.1 = bf16[16,32,1536]{2,1,0:T(8,128)(2,1)} async-done(((bf16[16,32,1536]{2,1,0:T(8,128)(2,1)}), bf16[16,32,1536]{2,1,0:T(8,128)(2,1)}, u32[]{:S(2)}, u32[]{:S(2)}) %all-to-all-start.1) | async-done | bytes 1572896 | tf_op jit(solution)/shard_map/all_to_all | solution.py:678
  159.8 7.9 %all-to-all-start.2 = ((bf16[16,32,1536]{2,1,0:T(8,128)(2,1)}), bf16[16,32,1536]{2,1,0:T(8,128)(2,1)}, u32[]{:S(2)}, u32[]{:S(2)}) async-start(bf16[16,32,1536]{2,1,0:T(8,128)(2,1)} %bitcast.141), calls=%async_computation.2 | async-start | bytes 3145728 | tf_op jit(solution)/shard_map/all_to_all | solution.py:678
  167.7 1.8 collective-permute-start
  169.9 11.0 %expert_forward.1 = (f32[512,1024]{1,0:T(8,128)S(1)}, f32[512,1024]{1,0:T(8,128)S(1)}, bf16[512,1024]{1,0:T(8,128)(2,1)S(1)}, bf16[512,1536]{1,0:T(8,128)(2,1)S(1)}) custom-call(bf16[512,1536]{1,0:T(8,128)(2,1)} %bitcast.17.x_ref, bf16[8,3,384,512]{3,2,1,0:T(8,128)(2,1)} %bitcast.156), custom_call_target="tpu_custom_call" | custom-call | flops 5000000000 | bytes 16000000 | tf_op jit(solution)/shard_map/expert_forward/pallas_call | solution.py:304
  185.6 2.4 all-to-all-done.2
  188.0 6.8 %all-to-all-start.3 = ((bf16[16,32,1536]{2,1,0:T(8,128)(2,1)}), bf16[16,32,1536]{2,1,0:T(8,128)(2,1)}, u32[]{:S(2)}, u32[]{:S(2)}) async-start(bf16[16,32,1536]{2,1,0:T(8,128)(2,1)} %bitcast.128), calls=%async_computation.3 | async-start | bytes 3145728 | tf_op jit(solution)/shard_map/all_to_all | solution.py:678
  198.0 15.4 %expert_backward.1 = (bf16[512,1024]{1,0:T(8,128)(2,1)S(1)}, bf16[512,1024]{1,0:T(8,128)(2,1)S(1)}, bf16[512,1536]{1,0:T(8,128)(2,1)S(1)}) custom-call(bf16[512,1536]{1,0:T(8,128)(2,1)} %bitcast.25.g_ref, bf16[8,3,384,512]{3,2,1,0:T(8,128)(2,1)} %bitcast.157, f32[512,1024]{1,0:T(8,128)S(1)} %copy-done.36, f32[512,1024]{1,0:T(8,128)S(1)} %copy-done.38), custom_call_target="tpu_custom_call" | custom-call | flops 5000000000 | bytes 16000000 | tf_op jit(solution)/shard_map/expert_backward/pallas_call | solution.py:321
  220.4 6.3 %expert_gradients.3 = bf16[2,2,3,384,512]{4,3,2,1,0:T(8,128)(2,1)} custom-call(s32[1]{0:T(128)} %bitcast.33.core_ref, bf16[512,1536]{1,0:T(8,128)(2,1)} %bitcast.17.x_ref, bf16[512,1536]{1,0:T(8,128)(2,1)} %bitcast.25.g_ref, bf16[512,1024]{1,0:T(8,128)(2,1)S(1)} %copy-done.27, bf16[512,1024]{1,0:T(8,128)(2,1)S(1)} %copy-done.30, bf16[512,1024]{1,0:T(8,128)(2,1)S(1)} %copy-done.33), custom_call_target="tpu_custom_call" | custom-call | flops 3000000000 | bytes 8000000 | tf_op jit(solution)/shard_map/expert_gradients/pallas_call | solution.py:340
  227.4 8.4 %all-to-all-start.4 = ((bf16[16,32,1536]{2,1,0:T(8,128)(2,1)}), bf16[16,32,1536]{2,1,0:T(8,128)(2,1)}, u32[]{:S(2)}, u32[]{:S(2)}) async-start(bf16[16,32,1536]{2,1,0:T(8,128)(2,1)} %bitcast.127), calls=%async_computation.4 | async-start | bytes 3145728 | tf_op jit(solution)/shard_map/all_to_all | solution.py:678
  235.8 1.9 fusion.14
  237.8 2.9 fusion.5
  240.8 2.3 fusion.10
  243.1 4.9 expert_gradients.2
  248.0 2.1 copy-done.7
  250.1 6.9 %all-to-all-done.4 = bf16[16,32,1536]{2,1,0:T(8,128)(2,1)} async-done(((bf16[16,32,1536]{2,1,0:T(8,128)(2,1)}), bf16[16,32,1536]{2,1,0:T(8,128)(2,1)}, u32[]{:S(2)}, u32[]{:S(2)}) %all-to-all-start.4) | async-done | bytes 1572896 | tf_op jit(solution)/shard_map/all_to_all | solution.py:678
  257.1 2.8 multiply_reduce_fusion.2
  259.9 2.2 fusion.40
  262.1 4.8 convolution_convert_fusion.3
  267.0 1.9 copy.105
  268.9 4.6 all-to-all-start.5
  273.5 5.3 %add_convert_fusion = bf16[2,2,3,384,512]{4,3,2,1,0:T(8,128)(2,1)S(1)} fusion(bf16[2,2,3,384,512]{4,3,2,1,0:T(8,128)(2,1)} %collective-permute-done.3, bf16[2,2,3,384,512]{4,3,2,1,0:T(8,128)(2,1)} %copy-done.7), kind=kLoop, calls=%fused_computation | loop fusion | flops 9437184 | bytes 14155776 | tf_op jit(solution)/shard_map/convert_element_type | solution.py:791
  278.9 1.9 dynamic-slice_bitcast_fusion
  281.8 2.1 collective-permute-start.5
  284.8 2.0 copy.106
  291.9 37.9 %attention_backward.1 = (bf16[1024,192]{1,0:T(8,128)(2,1)S(1)}, bf16[4096,128]{1,0:T(8,128)(2,1)S(1)}) custom-call(s32[84]{0:T(128)S(1)} %pad_add_fusion.meta, bf16[1024,192]{1,0:T(8,128)(2,1)S(1)} %copy-done.24, bf16[4096,128]{1,0:T(8,128)(2,1)S(1)} %bitcast.130, bf16[1024,192]{1,0:T(8,128)(2,1)S(1)} %copy-done.19, f32[16,192]{1,0:T(8,128)S(1)} %copy-done.40, ...), custom_call_target="tpu_custom_call" | custom-call | flops 4000000000 | bytes 10000000 | tf_op jit(solution)/shard_map/attention_backward/pallas_call | solution.py:219
  331.6 5.4 %all-to-all-start.6 = ((bf16[4,1024,128]{2,1,0:T(8,128)(2,1)}), bf16[4,1024,128]{2,1,0:T(8,128)(2,1)}, u32[]{:S(2)}, u32[]{:S(2)}) async-start(bf16[4,1024,128]{2,1,0:T(8,128)(2,1)} %bitcast.131), calls=%async_computation.6 | async-start | bytes 2097152 | tf_op jit(solution)/shard_map/all_to_all | solution.py:678
  337.1 1.8 convolution_convert_fusion.4
  342.1 7.8 %all-to-all-done.6 = bf16[4,1024,128]{2,1,0:T(8,128)(2,1)} async-done(((bf16[4,1024,128]{2,1,0:T(8,128)(2,1)}), bf16[4,1024,128]{2,1,0:T(8,128)(2,1)}, u32[]{:S(2)}, u32[]{:S(2)}) %all-to-all-start.6) | async-done | bytes 1048608 | tf_op jit(solution)/shard_map/all_to_all | solution.py:678
  349.8 2.1 reduce_sum.175
  352.0 4.3 convolution_convert_fusion.1
  356.3 2.3 copy.109
  358.6 3.6 convolution_convert_fusion.2
  362.3 2.2 copy.117
  365.3 5.2 concatenate.32
  370.5 3.0 copy.113
  373.5 5.8 %all-to-all-start.8 = ((bf16[16,96,640]{2,1,0:T(8,128)(2,1)}), bf16[16,96,640]{2,1,0:T(8,128)(2,1)}, u32[]{:S(2)}, u32[]{:S(2)}) async-start(bf16[16,96,640]{2,1,0:T(8,128)(2,1)} %bitcast.139), calls=%async_computation.8 | async-start | bytes 3932160 | tf_op jit(solution)/shard_map/all_to_all | solution.py:678
  379.3 3.1 fusion.2
  383.5 3.0 collective-permute-start.6
  387.7 2.2 copy.107
  389.9 15.7 %all-to-all-done.8 = bf16[16,96,640]{2,1,0:T(8,128)(2,1)} async-done(((bf16[16,96,640]{2,1,0:T(8,128)(2,1)}), bf16[16,96,640]{2,1,0:T(8,128)(2,1)}, u32[]{:S(2)}, u32[]{:S(2)}) %all-to-all-start.8) | async-done | bytes 1966112 | tf_op jit(solution)/shard_map/all_to_all | solution.py:678
  405.6 6.8 %all-to-all-start.7 = ((bf16[8,128,320]{1,2,0:T(8,128)(2,1)}), bf16[8,128,320]{1,2,0:T(8,128)(2,1)}, u32[]{:S(2)}, u32[]{:S(2)}) async-start(bf16[8,128,320]{1,2,0:T(8,128)(2,1)} %copy.107), calls=%async_computation.7 | async-start | bytes 1310720 | tf_op jit(solution)/shard_map/all_to_all | solution.py:678
  412.4 2.5 reduce_sum.177
  415.9 5.2 %collective-permute-start.4 = (bf16[96,192]{1,0:T(8,128)(2,1)S(1)}, bf16[96,192]{1,0:T(8,128)(2,1)S(1)}, u32[]{:S(2)}, u32[]{:S(2)}) collective-permute-start(bf16[96,192]{1,0:T(8,128)(2,1)S(1)} %slice.90), channel_id=1, source_target_pairs={{0,0},{1,4},{2,8},{3,12},{32,16},{33,20},{34,24},{35,28},{64,32},{... | collective-permute-start | bytes 110600 | tf_op jit(solution)/shard_map/ppermute | solution.py:844
  421.1 14.5 %collective-permute-done.6 = bf16[3,384,512]{2,1,0:T(8,128)(2,1)} collective-permute-done((bf16[3,384,512]{2,1,0:T(8,128)(2,1)}, bf16[3,384,512]{2,1,0:T(8,128)(2,1)}, u32[]{:S(2)}, u32[]{:S(2)}) %collective-permute-start.6) | collective-permute-done | bytes 1179680 | tf_op jit(solution)/shard_map/ppermute | solution.py:799
  435.6 3.4 convert_add_fusion.1
  439.8 3.1 broadcast_in_dim.116
  442.9 11.0 %all-to-all-start.9 = ((bf16[32,96,640]{2,1,0:T(8,128)(2,1)}), bf16[32,96,640]{2,1,0:T(8,128)(2,1)}, u32[]{:S(2)}, u32[]{:S(2)}) async-start(bf16[32,96,640]{2,1,0:T(8,128)(2,1)} %broadcast_in_dim.116), calls=%async_computation.9 | async-start | bytes 7864320 | tf_op jit(solution)/shard_map/all_to_all | solution.py:678
  454.7 2.2 copy.108.d_qkv_ref
  458.1 8.8 %input_gradient.1 = bf16[128,1536]{1,0:T(8,128)(2,1)} custom-call(s32[1]{0:T(128)} %bitcast.29.stream_ref, bf16[8,128,320]{2,1,0:T(8,128)(2,1)S(1)} %copy-done.9, bf16[8,384,384]{2,1,0:T(8,128)(2,1)S(1)} %copy-done.6, bf16[8,384,384]{2,1,0:T(8,128)(2,1)} %collective-permute-done.p1, bf16[8,384,384]{2,1,0:T(8,128)(2,1)} %collective-permute-done.1.p2, ...), custom_call_target="tpu_custom_call" | custom-call | flops 1000000000 | bytes 12000000 | tf_op jit(solution)/shard_map/input_gradient/pallas_call | solution.py:661
  469.3 30.9 %all-to-all-done.9 = bf16[32,96,640]{2,1,0:T(8,128)(2,1)} async-done(((bf16[32,96,640]{2,1,0:T(8,128)(2,1)}), bf16[32,96,640]{2,1,0:T(8,128)(2,1)}, u32[]{:S(2)}, u32[]{:S(2)}) %all-to-all-start.9) | async-done | bytes 3932192 | tf_op jit(solution)/shard_map/all_to_all | solution.py:678
  500.2 7.4 %assemble.1 = (f32[384,2560]{1,0:T(8,128)}, f32[384,1536]{1,0:T(8,128)}, f32[384,128]{1,0:T(8,128)S(1)}) custom-call(bf16[4,8,96,640]{3,2,1,0:T(8,128)(2,1)} %bitcast.52.by_row_ref, bf16[2,4,4,96,640]{4,3,2,1,0:T(8,128)(2,1)} %bitcast.53.by_head_ref), custom_call_target="tpu_custom_call" | custom-call | tf_op jit(solution)/shard_map/assemble/pallas_call | solution.py:371
  507.6 2.7 multiply_reduce_fusion.1
  (233 shorter events, 63.3 us)
Async XLA Ops:
  7.2 78.2 %copy-start = (s32[4,64]{1,0:T(4,128)S(1)}, s32[4,64]{1,0:T(4,128)}, u32[]{:S(2)}) copy-start(s32[4,64]{1,0:T(4,128)} %param.15) | copy-start | bytes 3076
  7.2 152.6 %all-gather.5.cloned.1.call-start = ((), (), s32[]{:S(2)}) async-start(), calls=%async_computation.10 | async-start | bytes 10616832 | tf_op jit(solution)/shard_map/all_gather | solution.py:735
  9.6 2.1 copy-start.3
  14.4 41.1 %copy-start.5 = (bf16[8,384,384]{2,1,0:T(8,128)(2,1)}, bf16[8,384,384]{2,1,0:T(8,128)(2,1)S(1)}, u32[]{:S(2)}) copy-start(bf16[8,384,384]{2,1,0:T(8,128)(2,1)S(1)} %get-tuple-element.79.wp_ref.p0) | copy-start | bytes 7077892
  55.5 2.2 copy-start.2
  61.4 2.4 copy-start.49
  65.1 104.5 %collective-permute-start.1 = (bf16[8,384,384]{2,1,0:T(8,128)(2,1)}, bf16[8,384,384]{2,1,0:T(8,128)(2,1)}, u32[]{:S(2)}, u32[]{:S(2)}) collective-permute-start(bf16[8,384,384]{2,1,0:T(8,128)(2,1)} %copy-done.5), channel_id=1, source_target_pairs={{0,18},{1,19},{2,16},{3,17},{4,22},{5,23},{6,20},{7,21},{8,26},{9,... | collective-permute-start | bytes 7077896 | tf_op jit(solution)/shard_map/ppermute | solution.py:736
  69.3 2.3 copy-start.48
  71.6 46.5 %copy-start.23 = (bf16[1024,192]{1,0:T(8,128)(2,1)}, bf16[1024,192]{1,0:T(8,128)(2,1)S(1)}, u32[]{:S(2)}) copy-start(bf16[1024,192]{1,0:T(8,128)(2,1)S(1)} %slice.83.q_ref) | copy-start | bytes 1179652
  85.3 32.8 %copy-start.13 = (bf16[4,1024,128]{2,1,0:T(8,128)(2,1)}, bf16[4,1024,128]{2,1,0:T(8,128)(2,1)S(1)}, u32[]{:S(2)}) copy-start(bf16[4,1024,128]{2,1,0:T(8,128)(2,1)S(1)} %gather_keys.1) | copy-start | bytes 3145732
  85.7 37.8 %copy-start.71 = (s32[1,128,2]{1,2,0:T(2,128)S(1)}, s32[1,128,2]{1,2,0:T(2,128)}, u32[]{:S(2)}) copy-start(s32[1,128,2]{1,2,0:T(2,128)} %param.16) | copy-start | bytes 3076
  85.7 38.2 %copy-start.55 = (f32[4,384]{1,0:T(4,128)S(1)}, f32[4,384]{1,0:T(4,128)}, u32[]{:S(2)}) copy-start(f32[4,384]{1,0:T(4,128)} %get-tuple-element.146) | copy-start | bytes 18436
  118.2 16.5 %copy-start.18 = (bf16[1024,192]{1,0:T(8,128)(2,1)}, bf16[1024,192]{1,0:T(8,128)(2,1)S(1)}, u32[]{:S(2)}) copy-start(bf16[1024,192]{1,0:T(8,128)(2,1)S(1)} %get-tuple-element.55.o_ref) | copy-start | bytes 1179652
  118.2 16.5 %copy-start.39 = (f32[16,192]{1,0:T(8,128)}, f32[16,192]{1,0:T(8,128)S(1)}, u32[]{:S(2)}) copy-start(f32[16,192]{1,0:T(8,128)S(1)} %get-tuple-element.71.lse_ref) | copy-start | bytes 36868
  119.1 12.3 %all-to-all-start = ((bf16[8,128,192]{1,2,0:T(8,128)(2,1)}), bf16[8,128,192]{1,2,0:T(8,128)(2,1)S(1)}, u32[]{:S(2)}, u32[]{:S(2)}) async-start(bf16[8,128,192]{1,2,0:T(8,128)(2,1)} %copy.98), calls=%async_computation | async-start | bytes 786432 | tf_op jit(solution)/shard_map/all_to_all | solution.py:678
  125.1 18.6 %copy-start.56 = (s32[128]{0:T(128)}, s32[128]{0:T(128)S(1)}, u32[]{:S(2)}) copy-start(s32[128]{0:T(128)S(1)} %get-tuple-element.145) | copy-start | bytes 1540
  125.2 18.6 %copy-start.58 = (s32[128]{0:T(128)}, s32[128]{0:T(128)S(1)}, u32[]{:S(2)}) copy-start(s32[128]{0:T(128)S(1)} %get-tuple-element.144) | copy-start | bytes 1540
  134.7 122.4 %copy-start.41 = (f32[128,1536]{1,0:T(8,128)}, f32[128,1536]{1,0:T(8,128)S(1)}, u32[]{:S(2)}) copy-start(f32[128,1536]{1,0:T(8,128)S(1)} %get-tuple-element.159) | copy-start | bytes 2359300
  135.3 2.0 copy-start.67
  135.4 6.2 %copy-start.45 = (bf16[128,1536]{1,0:T(8,128)(2,1)}, bf16[128,1536]{1,0:T(8,128)(2,1)S(1)}, u32[]{:S(2)}) copy-start(bf16[128,1536]{1,0:T(8,128)(2,1)S(1)} %multiply_convert_fusion) | copy-start | bytes 1179652
  137.3 22.5 %all-to-all-start.1 = ((bf16[16,32,1536]{2,1,0:T(8,128)(2,1)}), bf16[16,32,1536]{2,1,0:T(8,128)(2,1)}, u32[]{:S(2)}, u32[]{:S(2)}) async-start(bf16[16,32,1536]{2,1,0:T(8,128)(2,1)} %bitcast.16), calls=%async_computation.1 | async-start | bytes 3145728 | tf_op jit(solution)/shard_map/all_to_all | solution.py:678
  143.2 16.6 %copy-start.53 = (f32[128,2]{0,1:T(2,128)}, f32[128,2]{0,1:T(2,128)S(1)}, u32[]{:S(2)}) copy-start(f32[128,2]{0,1:T(2,128)S(1)} %select_reduce_fusion.4) | copy-start | bytes 3076
  144.0 23.7 %copy-start.6 = (bf16[8,384,384]{2,1,0:T(8,128)(2,1)S(1)}, bf16[8,384,384]{2,1,0:T(8,128)(2,1)}, u32[]{:S(2)}) copy-start(bf16[8,384,384]{2,1,0:T(8,128)(2,1)} %copy-done.5) | copy-start | bytes 7077892
  159.8 28.2 %all-to-all-start.2 = ((bf16[16,32,1536]{2,1,0:T(8,128)(2,1)}), bf16[16,32,1536]{2,1,0:T(8,128)(2,1)}, u32[]{:S(2)}, u32[]{:S(2)}) async-start(bf16[16,32,1536]{2,1,0:T(8,128)(2,1)} %bitcast.141), calls=%async_computation.2 | async-start | bytes 3145728 | tf_op jit(solution)/shard_map/all_to_all | solution.py:678
  167.7 47.6 %collective-permute-start = (bf16[8,384,384]{2,1,0:T(8,128)(2,1)S(1)}, bf16[8,384,384]{2,1,0:T(8,128)(2,1)}, u32[]{:S(2)}, u32[]{:S(2)}) collective-permute-start(bf16[8,384,384]{2,1,0:T(8,128)(2,1)S(1)} %copy-done.6), channel_id=1, source_target_pairs={{0,1},{1,0},{2,3},{3,2},{4,5},{5,4},{6,7},{7,6},{8,9},{9,8},{10,11... | collective-permute-start | bytes 7077896 | tf_op jit(solution)/shard_map/ppermute | solution.py:739
  169.6 46.9 %collective-permute-start.2 = (bf16[8,384,384]{2,1,0:T(8,128)(2,1)}, bf16[8,384,384]{2,1,0:T(8,128)(2,1)}, u32[]{:S(2)}, u32[]{:S(2)}) collective-permute-start(bf16[8,384,384]{2,1,0:T(8,128)(2,1)} %collective-permute-done.1.p2), channel_id=1, source_target_pairs={{0,1},{1,0},{2,3},{3,2},{4,5},{5,4},{6,7},{7,6},{8,9},{9,8},{10,11... | collective-permute-start | bytes 7077896 | tf_op jit(solution)/shard_map/ppermute | solution.py:741
  188.0 28.7 %all-to-all-start.3 = ((bf16[16,32,1536]{2,1,0:T(8,128)(2,1)}), bf16[16,32,1536]{2,1,0:T(8,128)(2,1)}, u32[]{:S(2)}, u32[]{:S(2)}) async-start(bf16[16,32,1536]{2,1,0:T(8,128)(2,1)} %bitcast.128), calls=%async_computation.3 | async-start | bytes 3145728 | tf_op jit(solution)/shard_map/all_to_all | solution.py:678
  226.7 9.1 %copy-start.57 = (s32[128]{0:T(128)S(1)}, s32[128]{0:T(128)}, u32[]{:S(2)}) copy-start(s32[128]{0:T(128)} %copy-done.56) | copy-start | bytes 1540
  226.7 30.3 %collective-permute-start.3 = (bf16[2,2,3,384,512]{4,3,2,1,0:T(8,128)(2,1)}, bf16[2,2,3,384,512]{4,3,2,1,0:T(8,128)(2,1)}, u32[]{:S(2)}, u32[]{:S(2)}) collective-permute-start(bf16[2,2,3,384,512]{4,3,2,1,0:T(8,128)(2,1)} %expert_gradients.3), channel_id=1, source_target_pairs={{0,1},{1,0},{2,3},{3,2},{4,5},{5,4},{6,7},{7,6},{8,9},{9,8},{10,11... | collective-permute-start | bytes 14155784 | tf_op jit(solution)/shard_map/ppermute | solution.py:788
  227.4 29.6 %all-to-all-start.4 = ((bf16[16,32,1536]{2,1,0:T(8,128)(2,1)}), bf16[16,32,1536]{2,1,0:T(8,128)(2,1)}, u32[]{:S(2)}, u32[]{:S(2)}) async-start(bf16[16,32,1536]{2,1,0:T(8,128)(2,1)} %bitcast.127), calls=%async_computation.4 | async-start | bytes 3145728 | tf_op jit(solution)/shard_map/all_to_all | solution.py:678
  235.8 122.9 %all-gather.7.cloned.1.call-start = ((), (), s32[]{:S(2)}) async-start(), calls=%async_computation.11 | async-start | bytes 3538944 | tf_op jit(solution)/shard_map/all_gather | solution.py:823
  235.8 1.9 copy-start.46
  237.7 3.0 copy-start.54
  237.7 2.9 copy-start.61
  237.8 2.9 copy-start.66
  237.8 3.0 copy-start.63
  237.8 5.3 %copy-start.28 = (bf16[512,1024]{1,0:T(8,128)(2,1)S(1)}, bf16[512,1024]{1,0:T(8,128)(2,1)}, u32[]{:S(2)}) copy-start(bf16[512,1024]{1,0:T(8,128)(2,1)} %copy-done.26) | copy-start | bytes 3145732
  237.8 5.3 %copy-start.31 = (bf16[512,1024]{1,0:T(8,128)(2,1)S(1)}, bf16[512,1024]{1,0:T(8,128)(2,1)}, u32[]{:S(2)}) copy-start(bf16[512,1024]{1,0:T(8,128)(2,1)} %copy-done.29) | copy-start | bytes 3145732
  237.8 5.3 %copy-start.34 = (bf16[512,1024]{1,0:T(8,128)(2,1)S(1)}, bf16[512,1024]{1,0:T(8,128)(2,1)}, u32[]{:S(2)}) copy-start(bf16[512,1024]{1,0:T(8,128)(2,1)} %copy-done.32) | copy-start | bytes 3145732
  240.8 2.3 copy-start.51
  248.0 2.1 copy-start.7
  250.1 9.8 %copy-start.68 = (f32[128]{0:T(128)S(1)}, f32[128]{0:T(128)}, u32[]{:S(2)}) copy-start(f32[128]{0:T(128)} %copy-done.67) | copy-start | bytes 1540
  257.0 2.9 copy-start.47
  257.0 2.9 copy-start.72
  268.9 16.0 %all-to-all-start.5 = ((bf16[8,128,192]{1,2,0:T(8,128)(2,1)}), bf16[8,128,192]{1,2,0:T(8,128)(2,1)}, u32[]{:S(2)}, u32[]{:S(2)}) async-start(bf16[8,128,192]{1,2,0:T(8,128)(2,1)} %bitcast.148), calls=%async_computation.5 | async-start | bytes 786432 | tf_op jit(solution)/shard_map/all_to_all | solution.py:678
  278.9 3.0 copy-start.42
  281.8 97.4 %collective-permute-start.5 = (bf16[2,3,384,512]{3,2,1,0:T(8,128)(2,1)}, bf16[2,3,384,512]{3,2,1,0:T(8,128)(2,1)}, u32[]{:S(2)}, u32[]{:S(2)}) collective-permute-start(bf16[2,3,384,512]{3,2,1,0:T(8,128)(2,1)} %dynamic-slice_bitcast_fusion), channel_id=1, source_target_pairs={{0,4},{4,0},{8,12},{12,8},{16,20},{20,16},{24,28},{28,24},{32,36},... | collective-permute-start | bytes 7077896 | tf_op jit(solution)/shard_map/ppermute | solution.py:793
  291.9 45.2 %copy-start.52 = (bf16[128,16]{0,1:T(8,128)(2,1)S(1)}, bf16[128,16]{0,1:T(8,128)(2,1)}, u32[]{:S(2)}) copy-start(bf16[128,16]{0,1:T(8,128)(2,1)} %copy-done.51) | copy-start | bytes 12292
  331.6 9.0 %copy-start.59 = (bf16[1536]{0:T(1024)(128)(2,1)S(1)}, bf16[1536]{0:T(1024)(128)(2,1)}, u32[]{:S(2)}) copy-start(bf16[1536]{0:T(1024)(128)(2,1)} %get-tuple-element.140) | copy-start | bytes 9220
  331.6 18.2 %all-to-all-start.6 = ((bf16[4,1024,128]{2,1,0:T(8,128)(2,1)}), bf16[4,1024,128]{2,1,0:T(8,128)(2,1)}, u32[]{:S(2)}, u32[]{:S(2)}) async-start(bf16[4,1024,128]{2,1,0:T(8,128)(2,1)} %bitcast.131), calls=%async_computation.6 | async-start | bytes 2097152 | tf_op jit(solution)/shard_map/all_to_all | solution.py:678
  373.5 32.1 %all-to-all-start.8 = ((bf16[16,96,640]{2,1,0:T(8,128)(2,1)}), bf16[16,96,640]{2,1,0:T(8,128)(2,1)}, u32[]{:S(2)}, u32[]{:S(2)}) async-start(bf16[16,96,640]{2,1,0:T(8,128)(2,1)} %bitcast.139), calls=%async_computation.8 | async-start | bytes 3932160 | tf_op jit(solution)/shard_map/all_to_all | solution.py:678
  382.4 5.3 %copy-start.43 = (bf16[2,3,384,512]{3,2,1,0:T(8,128)(2,1)}, bf16[2,3,384,512]{3,2,1,0:T(8,128)(2,1)S(1)}, u32[]{:S(2)}) copy-start(bf16[2,3,384,512]{3,2,1,0:T(8,128)(2,1)S(1)} %fusion.2) | copy-start | bytes 7077892
  382.4 4.1 copy-start.17
  382.4 4.1 copy-start.50
  383.5 52.1 %collective-permute-start.6 = (bf16[3,384,512]{2,1,0:T(8,128)(2,1)}, bf16[3,384,512]{2,1,0:T(8,128)(2,1)}, u32[]{:S(2)}, u32[]{:S(2)}) collective-permute-start(bf16[3,384,512]{2,1,0:T(8,128)(2,1)} %dynamic-slice_bitcast_fusion.1), channel_id=1, source_target_pairs={{0,2},{1,3},{2,0},{3,1},{4,6},{5,7},{6,4},{7,5},{8,10},{9,11},{10,... | collective-permute-start | bytes 3538952 | tf_op jit(solution)/shard_map/ppermute | solution.py:799
  405.6 34.2 %all-to-all-start.7 = ((bf16[8,128,320]{1,2,0:T(8,128)(2,1)}), bf16[8,128,320]{1,2,0:T(8,128)(2,1)}, u32[]{:S(2)}, u32[]{:S(2)}) async-start(bf16[8,128,320]{1,2,0:T(8,128)(2,1)} %copy.107), calls=%async_computation.7 | async-start | bytes 1310720 | tf_op jit(solution)/shard_map/all_to_all | solution.py:678
  415.8 23.2 %slice-start = ((bf16[96,640]{1,0:T(8,128)(2,1)}), bf16[96,128]{1,0:T(8,128)(2,1)S(1)}, s32[]{:S(2)}) async-start(bf16[96,640]{1,0:T(8,128)(2,1)} %reduce_sum.177), calls=%async_computation.12 | async-start | bytes 49152 | tf_op jit(solution)/shard_map/slice | solution.py:845
  415.9 23.2 %slice-start.1 = ((bf16[96,640]{1,0:T(8,128)(2,1)}), bf16[96,320]{1,0:T(8,128)(2,1)S(1)}, s32[]{:S(2)}) async-start(bf16[96,640]{1,0:T(8,128)(2,1)} %reduce_sum.177), calls=%async_computation.13 | async-start | bytes 147456 | tf_op jit(solution)/shard_map/slice | solution.py:845
  415.9 23.2 %collective-permute-start.4 = (bf16[96,192]{1,0:T(8,128)(2,1)S(1)}, bf16[96,192]{1,0:T(8,128)(2,1)S(1)}, u32[]{:S(2)}, u32[]{:S(2)}) collective-permute-start(bf16[96,192]{1,0:T(8,128)(2,1)S(1)} %slice.90), channel_id=1, source_target_pairs={{0,0},{1,4},{2,8},{3,12},{32,16},{33,20},{34,24},{35,28},{64,32},{... | collective-permute-start | bytes 110600 | tf_op jit(solution)/shard_map/ppermute | solution.py:844
  442.9 57.3 %all-to-all-start.9 = ((bf16[32,96,640]{2,1,0:T(8,128)(2,1)}), bf16[32,96,640]{2,1,0:T(8,128)(2,1)}, u32[]{:S(2)}, u32[]{:S(2)}) async-start(bf16[32,96,640]{2,1,0:T(8,128)(2,1)} %broadcast_in_dim.116), calls=%async_computation.9 | async-start | bytes 7864320 | tf_op jit(solution)/shard_map/all_to_all | solution.py:678
  458.1 8.8 %copy-start.44 = (f32[3,384,512]{2,1,0:T(8,128)S(1)}, f32[3,384,512]{2,1,0:T(8,128)}, u32[]{:S(2)}) copy-start(f32[3,384,512]{2,1,0:T(8,128)} %convert_add_fusion.1) | copy-start | bytes 7077892
  500.2 7.4 %copy-start.4 = (f32[384,2560]{1,0:T(8,128)S(1)}, f32[384,2560]{1,0:T(8,128)}, u32[]{:S(2)}) copy-start(f32[384,2560]{1,0:T(8,128)} %qkv_ref.1) | copy-start | bytes 11796484
  507.6 4.9 copy-start.1
  507.6 2.8 copy-start.64
  (30 other events, 32.5 us)
Sparse Core Ops, SparseCore 0:
  65.2 54.0 all-gather.4
  262.2 64.7 all-gather.6

commit v2 on v1

v2 whole, which is shorter than its diff:
```python
import functools

import jax
import jax.numpy as jnp
from jax import lax
from jax.experimental import pallas as pl
from jax.experimental.pallas import tpu as pltpu
from jax.sharding import PartitionSpec as P

QUERY_HEADS = 24
KEY_VALUE_HEADS = 8
HEAD_SIZE = 64
GROUP = QUERY_HEADS // KEY_VALUE_HEADS
TOP = 2
BLOCK = 64
WIDTH = GROUP * HEAD_SIZE
HEAD_COLUMNS = WIDTH + 2 * HEAD_SIZE
CHUNK = 512
LANES = 3
TURN = 256

EPSILON = 1e-05
NEG_BIG = -1e30
BF = jnp.bfloat16
F32 = jnp.float32

def turned(index):
    return index % 4 * 8 + index // 4 % 2 * 4 + index // 8


ROW = [[turned(y * 8 + r) for r in range(8)] for y in range(4)]
OWNERS = [[(2 * e + k) * 4 + w for k in range(2) for w in range(4)] for e in range(16)]
OTHER_HALF = [(c, c ^ 1) for c in range(32)]
OTHER_SIDE = [(w, w ^ 2) for w in range(4)]
OTHER_CORE = [(w, w ^ 1) for w in range(4)]
NEXT_Z = [(c * 4 + w, (c ^ 4) * 4 + (w ^ 2)) for c in range(32) for w in range(4)]
MOVES = [
    (turned(y * 8 + r) * 4 + w, turned((r % 2) * 16 + y * 4 + w) * 4 + r // 2)
    for r in range(8)
    for y in range(4)
    for w in range(4)
]


def dot(a, b, dims=((1,), (0,))):
    return lax.dot_general(a, b, (dims, ((), ())), preferred_element_type=F32)


NT = ((1,), (1,))
TN = ((0,), (0,))


def block_range(meta, b):
    base = meta[BLOCK + b] * BLOCK
    lane = lax.broadcasted_iota(jnp.int32, (1, WIDTH), 1)
    query = base + (lane & (BLOCK - 1))
    start = jnp.zeros((1, WIDTH), jnp.int32)
    first = jnp.int32(0)
    for i in range(3):
        bound = meta[80 + i]
        start = jnp.where(query >= bound, bound, start)
        first = jnp.where(base >= bound, bound, first)
    first = (first // 128) * 128
    count = (base + BLOCK - first + CHUNK - 1) // CHUNK
    return query, start, first, count


def list_work(meta, blocks, block_s, key_s):
    def one(b, n):
        _, _, first, count = block_range(meta, b)

        def put(i, n):
            block_s[n] = b
            key_s[n] = first + i * CHUNK
            return n + 1

        return lax.fori_loop(0, count, put, n)

    total = lax.fori_loop(0, blocks, one, jnp.int32(0))
    for i in range(LANES):
        block_s[total + i] = blocks
        key_s[total + i] = 0
    return (total + LANES - 1) // LANES


def allowed_of(key_start, query, start):
    key = key_start + lax.broadcasted_iota(jnp.int32, (CHUNK, WIDTH), 0)
    return (key <= query) & (key >= start)


def stack_heads(rows):
    return jnp.concatenate([rows[:, g * HEAD_SIZE : (g + 1) * HEAD_SIZE] for g in range(GROUP)], axis=0)


def sort_blocks(meta, kv_ref, sorted_ref):
    total = kv_ref.shape[0]

    def one(p, carry):
        source = pl.multiple_of(meta[p] * BLOCK, BLOCK)
        target = pl.multiple_of(p * BLOCK, BLOCK)
        sorted_ref[pl.ds(target, BLOCK), :] = kv_ref[pl.ds(source, BLOCK), :]
        return carry

    lax.fori_loop(0, total // BLOCK, one, 0, unroll=8)
    sorted_ref[total:, :] = jnp.zeros((CHUNK, sorted_ref.shape[1]), sorted_ref.dtype)


def transpose_all(sorted_ref, turned_ref):
    steps = sorted_ref.shape[0] // TURN

    def one(i, carry):
        at = pl.multiple_of(i * TURN, TURN)
        turned_ref[:, pl.ds(at, TURN)] = sorted_ref[pl.ds(at, TURN), :].T
        return carry

    lax.fori_loop(0, steps, one, 0)


def attention_forward(
    meta, q_ref, kv_ref, o_ref, lse_ref,
    sorted_ref, turned_ref, pad_ref, query_ref, start_ref, top_ref, total_ref, acc_ref, block_s, key_s,
):
    blocks = q_ref.shape[0] // BLOCK
    sort_blocks(meta, kv_ref, sorted_ref)
    transpose_all(sorted_ref, turned_ref)
    share = list_work(meta, blocks, block_s, key_s)
    zeros = jnp.zeros((WIDTH, HEAD_SIZE), BF)
    top_ref[...] = jnp.full(top_ref.shape, NEG_BIG, F32)
    total_ref[...] = jnp.zeros_like(total_ref)
    acc_ref[...] = jnp.zeros_like(acc_ref)
    query_ref[blocks] = jnp.full((1, WIDTH), -1, jnp.int32)
    start_ref[blocks] = jnp.zeros((1, WIDTH), jnp.int32)
    pad_ref[blocks] = jnp.zeros((WIDTH, 2 * HEAD_SIZE), BF)

    def prepare_block(b, carry):
        query_ref[b], start_ref[b], _, _ = block_range(meta, b)
        at = pl.multiple_of(b * BLOCK, BLOCK)
        rows = stack_heads(q_ref[pl.ds(at, BLOCK), :]) * jnp.asarray(HEAD_SIZE**-0.5, BF)
        pad_ref[b] = jnp.concatenate([rows, zeros], axis=1)
        return carry

    lax.fori_loop(0, blocks, prepare_block, 0, unroll=4)

    def work(i, carry):
        blocks_now = [block_s[lane * share + i] for lane in range(LANES)]
        starts_now = [pl.multiple_of(key_s[lane * share + i], 128) for lane in range(LANES)]
        results = []
        for b, key_start in zip(blocks_now, starts_now):
            scores = dot(sorted_ref[pl.ds(key_start, CHUNK), :], pad_ref[b], NT)
            scores = jnp.where(allowed_of(key_start, query_ref[b], start_ref[b]), scores, NEG_BIG)
            top = top_ref[b]
            top_new = jnp.maximum(top, jnp.max(scores, axis=0, keepdims=True))
            weights = jnp.exp(scores - top_new)
            fade = jnp.exp(top - top_new)
            total = total_ref[b] * fade + jnp.sum(weights, axis=0, keepdims=True)
            values = turned_ref[HEAD_SIZE:, pl.ds(key_start, CHUNK)]
            results.append((top_new, total, acc_ref[b] * fade + dot(values, weights.astype(BF))))
        for b, (top, total, acc) in zip(blocks_now, results):
            top_ref[b] = top
            total_ref[b] = total
            acc_ref[b] = acc
        return carry

    lax.fori_loop(0, share, work, 0)

    def finish_block(b, carry):
        at = pl.multiple_of(b * BLOCK, BLOCK)
        total = total_ref[b]
        lse_ref[b] = top_ref[b] + jnp.log(total)
        result = (acc_ref[b] / total).T.astype(BF)
        o_ref[pl.ds(at, BLOCK), :] = jnp.concatenate(
            [result[g * BLOCK : (g + 1) * BLOCK] for g in range(GROUP)], axis=1
        )
        return carry

    lax.fori_loop(0, blocks, finish_block, 0, unroll=4)


def attention_backward(
    meta, q_ref, kv_ref, o_ref, lse_ref, do_ref, dq_ref, dkv_ref,
    sorted_ref, turned_ref, total_ref, both_ref, query_ref, start_ref, delta_ref, acc_ref, block_s, key_s,
):
    blocks = q_ref.shape[0] // BLOCK
    sort_blocks(meta, kv_ref, sorted_ref)
    transpose_all(sorted_ref, turned_ref)
    share = list_work(meta, blocks, block_s, key_s)
    total_ref[...] = jnp.zeros_like(total_ref)
    acc_ref[...] = jnp.zeros_like(acc_ref)
    query_ref[blocks] = jnp.full((1, WIDTH), -1, jnp.int32)
    start_ref[blocks] = jnp.zeros((1, WIDTH), jnp.int32)
    delta_ref[blocks] = jnp.zeros((1, WIDTH), F32)
    both_ref[blocks] = jnp.zeros((2 * WIDTH, 2 * HEAD_SIZE), BF)
    zeros = jnp.zeros((WIDTH, HEAD_SIZE), BF)
    scaling = HEAD_SIZE**-0.5

    def prepare_block(b, carry):
        query_ref[b], start_ref[b], _, _ = block_range(meta, b)
        at = pl.multiple_of(b * BLOCK, BLOCK)
        rows = stack_heads(q_ref[pl.ds(at, BLOCK), :]) * jnp.asarray(scaling, BF)
        grad = stack_heads(do_ref[pl.ds(at, BLOCK), :])
        value = stack_heads(o_ref[pl.ds(at, BLOCK), :])
        delta_ref[b] = jnp.sum((grad.astype(F32) * value.astype(F32)).T, axis=0, keepdims=True)
        both_ref[b, :WIDTH] = jnp.concatenate([rows, zeros], axis=1)
        both_ref[b, WIDTH:] = jnp.concatenate([zeros, grad], axis=1)
        return carry

    lax.fori_loop(0, blocks, prepare_block, 0, unroll=4)

    def work(i, carry):
        blocks_now = [block_s[lane * share + i] for lane in range(LANES)]
        starts_now = [pl.multiple_of(key_s[lane * share + i], 128) for lane in range(LANES)]
        results = []
        for b, key_start in zip(blocks_now, starts_now):
            keys = sorted_ref[pl.ds(key_start, CHUNK), :]
            scores = dot(keys, both_ref[b, :WIDTH], NT)
            d_probs = dot(keys, both_ref[b, WIDTH:], NT)
            allowed = allowed_of(key_start, query_ref[b], start_ref[b])
            probs = jnp.where(allowed, jnp.exp(scores - lse_ref[b]), 0.0)
            d_scores = (probs * (d_probs - delta_ref[b])).astype(BF)
            joined = jnp.concatenate([d_scores, probs.astype(BF)], axis=1)
            turned = turned_ref[:HEAD_SIZE, pl.ds(key_start, CHUNK)]
            results.append((acc_ref[b] + dot(turned, d_scores), dot(joined, both_ref[b])))
        for b, key_start, (acc, d_keys) in zip(blocks_now, starts_now, results):
            acc_ref[b] = acc
            total_ref[pl.ds(key_start, CHUNK), :] += d_keys
        return carry

    lax.fori_loop(0, share, work, 0)

    def finish_block(b, carry):
        at = pl.multiple_of(b * BLOCK, BLOCK)
        result = (acc_ref[b] * scaling).T.astype(BF)
        dq_ref[pl.ds(at, BLOCK), :] = jnp.concatenate(
            [result[g * BLOCK : (g + 1) * BLOCK] for g in range(GROUP)], axis=1
        )
        return carry

    lax.fori_loop(0, blocks, finish_block, 0, unroll=4)

    def back(p, carry):
        target = pl.multiple_of(meta[p] * BLOCK, BLOCK)
        source = pl.multiple_of(p * BLOCK, BLOCK)
        dkv_ref[pl.ds(target, BLOCK), :] = total_ref[pl.ds(source, BLOCK), :].astype(BF)
        return carry

    lax.fori_loop(0, kv_ref.shape[0] // BLOCK, back, 0, unroll=8)


def local_call(kernel, outs, n_vmem, scratch, name):
    return pl.pallas_call(
        kernel,
        out_shape=outs,
        in_specs=[pl.BlockSpec(memory_space=pltpu.SMEM)] + [pl.BlockSpec(memory_space=pltpu.VMEM)] * n_vmem,
        out_specs=tuple(pl.BlockSpec(memory_space=pltpu.VMEM) for _ in outs),
        scratch_shapes=scratch,
        compiler_params=pltpu.CompilerParams(vmem_limit_bytes=40 * 2**20),
        cost_estimate=pl.CostEstimate(flops=4 * 10**9, bytes_accessed=10**7, transcendentals=4 * 10**6),
        name=name,
    )


def work_scratch(rows, keys):
    blocks = rows // BLOCK
    most = blocks * (keys // CHUNK + 1) + LANES
    return [pltpu.SMEM((most,), jnp.int32), pltpu.SMEM((most,), jnp.int32)]


def run_forward(meta, q, kv):
    rows, keys = q.shape[0], kv.shape[0]
    blocks = rows // BLOCK
    line = (blocks + 1, 1, WIDTH)
    return local_call(
        attention_forward,
        (jax.ShapeDtypeStruct((rows, WIDTH), BF), jax.ShapeDtypeStruct(line, F32)),
        2,
        [
            pltpu.VMEM((keys + CHUNK, 2 * HEAD_SIZE), BF),
            pltpu.VMEM((2 * HEAD_SIZE, keys + CHUNK), BF),
            pltpu.VMEM((blocks + 1, WIDTH, 2 * HEAD_SIZE), BF),
            pltpu.VMEM(line, jnp.int32),
            pltpu.VMEM(line, jnp.int32),
            pltpu.VMEM(line, F32),
            pltpu.VMEM(line, F32),
            pltpu.VMEM((blocks + 1, HEAD_SIZE, WIDTH), F32),
        ]
        + work_scratch(rows, keys),
        "attention_forward",
    )(meta, q, kv)


def run_backward(meta, q, kv, o, lse, d_o):
    rows, keys = q.shape[0], kv.shape[0]
    blocks = rows // BLOCK
    line = (blocks + 1, 1, WIDTH)
    return local_call(
        attention_backward,
        (jax.ShapeDtypeStruct((rows, WIDTH), BF), jax.ShapeDtypeStruct((keys, 2 * HEAD_SIZE), BF)),
        5,
        [
            pltpu.VMEM((keys + CHUNK, 2 * HEAD_SIZE), BF),
            pltpu.VMEM((2 * HEAD_SIZE, keys + CHUNK), BF),
            pltpu.VMEM((keys + CHUNK, 2 * HEAD_SIZE), F32),
            pltpu.VMEM((blocks + 1, 2 * WIDTH, 2 * HEAD_SIZE), BF),
            pltpu.VMEM(line, jnp.int32),
            pltpu.VMEM(line, jnp.int32),
            pltpu.VMEM(line, F32),
            pltpu.VMEM((blocks + 1, HEAD_SIZE, WIDTH), F32),
        ]
        + work_scratch(rows, keys),
        "attention_backward",
    )(meta, q, kv, o, lse, d_o)


def exchange_terms_kernel(kv_ref, out_ref, kv_to, out_to, v_kv, v_out, send, recv, local):
    place, stream = turned(lax.axis_index("ctx")), lax.axis_index("wsh")
    y = place // 8
    peers = []
    for k in range(1, 16):
        peers.append(((y + k // 4) % 4, (stream + k % 4) % 4))
    meet([{"ctx": turned(place % 8 + 8 * py), "wsh": pw} for py, pw in peers])
    copies = Copies(send, recv, local)
    for k in (8, 4, 12):
        py, _ = peers[k - 1]
        copies.to(kv_ref.at[py], kv_to.at[y], {"ctx": turned(place % 8 + 8 * py)})
    for py, pw in peers:
        copies.to(out_ref.at[py, pw], out_to.at[y, stream], {"ctx": turned(place % 8 + 8 * py), "wsh": pw})
    copies.keep(kv_ref.at[y], v_kv, kv_to.at[y])
    copies.keep(out_ref.at[y, stream], v_out, out_to.at[y, stream])
    copies.move_kept()
    copies.finish([])


def exchange_terms(kv, out):
    return pl.pallas_call(
        exchange_terms_kernel,
        out_shape=(jax.ShapeDtypeStruct(kv.shape, BF), jax.ShapeDtypeStruct(out.shape, BF)),
        in_specs=[ANY, ANY],
        out_specs=(ANY, ANY),
        scratch_shapes=[
            pltpu.VMEM(kv.shape[1:], BF),
            pltpu.VMEM(out.shape[2:], BF),
            pltpu.SemaphoreType.DMA((18,)),
            pltpu.SemaphoreType.DMA((18,)),
            pltpu.SemaphoreType.DMA((4,)),
        ],
        compiler_params=pltpu.CompilerParams(collective_id=3, has_side_effects=True, vmem_limit_bytes=40 * 2**20),
        name="exchange_terms",
    )(kv, out)


def weight_terms_kernel(act_ref, dq_ref, kv_ref, small_ref, grad_out, term_out, grad_ref):
    rows = dq_ref.shape[0]

    @pl.when(pl.program_id(0) == 0)
    def _():
        total = kv_ref[0].astype(F32)
        for i in range(1, 4):
            total = total + kv_ref[i].astype(F32)
        grad = jnp.concatenate([dq_ref[...], total.astype(BF)], axis=1)
        grad_ref[...] = grad
        padded = jnp.concatenate([grad, jnp.zeros((rows, 64), BF)], axis=1)
        grad_out[...] = padded.reshape(grad_out.shape)

    term = dot(act_ref[...].T, grad_ref[...]).astype(BF)
    term = jnp.concatenate([term, small_ref[...]], axis=1)
    piece = term_out.shape[2]
    for y in range(4):
        term_out[y, 0] = term[y * piece : (y + 1) * piece]


def weight_terms(act, dq, kv, small):
    rows, width = act.shape
    shard = width // 4
    return pl.pallas_call(
        weight_terms_kernel,
        out_shape=(
            jax.ShapeDtypeStruct((8, rows // 8, 384), BF),
            jax.ShapeDtypeStruct((4, 4, shard // 4, 384), BF),
        ),
        grid=(4,),
        in_specs=[
            pl.BlockSpec((rows, shard), lambda w: (0, w)),
            pl.BlockSpec(dq.shape, lambda w: (0, 0)),
            pl.BlockSpec(kv.shape, lambda w: (0, 0, 0)),
            pl.BlockSpec((shard, 64), lambda w: (w, 0)),
        ],
        out_specs=(
            pl.BlockSpec((8, rows // 8, 384), lambda w: (0, 0, 0)),
            pl.BlockSpec((4, 1, shard // 4, 384), lambda w: (0, w, 0, 0)),
        ),
        scratch_shapes=[pltpu.VMEM((rows, HEAD_COLUMNS), BF)],
        compiler_params=pltpu.CompilerParams(vmem_limit_bytes=40 * 2**20),
        cost_estimate=pl.CostEstimate(flops=10**9, bytes_accessed=8 * 10**6, transcendentals=0),
        name="weight_terms",
    )(act, dq, kv, small)


def return_terms_kernel(grad_ref, term_ref, grad_to, term_to, v_grad, v_term, send, recv, local):
    place, stream = turned(lax.axis_index("ctx")), lax.axis_index("wsh")
    y, r = place // 8, place % 8
    peers = [((y + k // 4) % 4, (stream + k % 4) % 4) for k in range(1, 16)]
    in_row = [(r + k) % 8 for k in range(1, 8)]
    meet(
        [{"ctx": turned(r + 8 * py), "wsh": pw} for py, pw in peers] + [{"ctx": turned(8 * y + pr)} for pr in in_row]
    )
    copies = Copies(send, recv, local)
    for py, pw in peers:
        copies.to(term_ref.at[py, pw], term_to.at[y, stream], {"ctx": turned(r + 8 * py), "wsh": pw})
    for pr in in_row:
        copies.to(grad_ref.at[pr], grad_to.at[r], {"ctx": turned(8 * y + pr)})
    copies.keep(grad_ref.at[r], v_grad, grad_to.at[r])
    copies.keep(term_ref.at[y, stream], v_term, term_to.at[y, stream])
    copies.move_kept()
    copies.finish([])


def return_terms(grad, term):
    return pl.pallas_call(
        return_terms_kernel,
        out_shape=(jax.ShapeDtypeStruct(grad.shape, BF), jax.ShapeDtypeStruct(term.shape, BF)),
        in_specs=[ANY, ANY],
        out_specs=(ANY, ANY),
        scratch_shapes=[
            pltpu.VMEM(grad.shape[1:], BF),
            pltpu.VMEM(term.shape[2:], BF),
            pltpu.SemaphoreType.DMA((22,)),
            pltpu.SemaphoreType.DMA((22,)),
            pltpu.SemaphoreType.DMA((4,)),
        ],
        compiler_params=pltpu.CompilerParams(collective_id=4, has_side_effects=True, vmem_limit_bytes=40 * 2**20),
        name="return_terms",
    )(grad, term)


def gather_sums_kernel(term_ref, piece_ref, all_out, own_ref, send, recv, local):
    place = turned(lax.axis_index("ctx"))
    y, r = place // 8, place % 8
    x, z = r % 4, r // 4
    right, left = {"ctx": turned(place - x + (x + 1) % 4)}, {"ctx": turned(place - x + (x + 3) % 4)}
    across = {"ctx": turned(place + 4 - 8 * z)}
    up, down, beyond = ({"ctx": turned((place + 8 * k) % 32)} for k in (1, 3, 2))
    total = term_ref[0, 0].astype(F32)
    for i in range(1, 16):
        total = total + term_ref[i // 4, i % 4].astype(F32)
    own_ref[:, : total.shape[1]] = total.astype(BF)
    own_ref[:, total.shape[1] :] = piece_ref[...]
    meet([right, left, across, up, down, beyond])
    copies = Copies(send, recv, local)
    half = own_ref.shape[0] // 2
    first, last = pl.ds(0, half), pl.ds(half, half)
    r_z = (1 - z) * 4 + x
    r_left, r_right = z * 4 + (x + 3) % 4, z * 4 + (x + 1) % 4
    z_left, z_right = (1 - z) * 4 + (x + 3) % 4, (1 - z) * 4 + (x + 1) % 4
    arrived = []

    def arrive(*which):
        for copy in which:
            copy.wait_recv()
            arrived.append(copy)

    def on(device, *at):
        return copies.to(all_out.at[at], all_out.at[at], device)

    keep = pltpu.make_async_copy(own_ref, all_out.at[y, r], local.at[0])
    keep.start()
    a_right = copies.to(own_ref.at[first], all_out.at[y, r, first], right)
    a_left = copies.to(own_ref.at[first], all_out.at[y, r, first], left)
    a_cross = copies.to(own_ref.at[first], all_out.at[y, r, first], across)
    b_up = copies.to(own_ref.at[last], all_out.at[y, r, last], up)
    b_down = copies.to(own_ref.at[last], all_out.at[y, r, last], down)
    b_beyond = copies.to(own_ref.at[last], all_out.at[y, r, last], beyond)
    keep.wait()
    arrive(a_cross)
    a_z_right = on(right, y, r_z, first)
    a_z_left = on(left, y, r_z, first)
    arrive(a_right)
    a_on = on(right, y, r_left, first)
    arrive(b_up, b_down, b_beyond)
    lower, upper, every = pl.ds(0, 2), pl.ds(2, 2), pl.ds(0, 4)
    b_right = on(right, every, r, last)
    b_left = on(left, every, r, last)
    b_cross = on(across, every, r, last)
    arrive(a_z_left, a_left)
    a_z_on = on(left, y, z_right, first)
    arrive(a_z_right, a_on, a_z_on)
    low_r, high_r = pl.ds(0, 4), pl.ds(4, 4)
    c_up = [on(up, y, low_r, first), on(up, y, high_r, first)]
    c_down = [on(down, y, high_r, first), on(down, y, low_r, first)]
    arrive(b_right)
    on(right, lower, r_left, last)
    arrive(b_left)
    on(left, upper, r_right, last)
    arrive(b_cross)
    b_z_right = on(right, every, r_z, last)
    b_z_left = on(left, every, r_z, last)
    arrive(c_up[0])
    on(up, (y + 3) % 4, low_r, first)
    arrive(c_down[0])
    on(down, (y + 1) % 4, high_r, first)
    arrive(b_z_right)
    on(right, lower, z_left, last)
    arrive(b_z_left)
    on(left, upper, z_right, last)
    copies.finish(arrived)


def gather_sums(term, piece):
    rows, columns = piece.shape[0], term.shape[3] + piece.shape[1]
    vmem = pl.BlockSpec(memory_space=pltpu.VMEM)
    return pl.pallas_call(
        gather_sums_kernel,
        out_shape=jax.ShapeDtypeStruct((4, 8, rows, columns), BF),
        in_specs=[vmem, vmem],
        out_specs=ANY,
        scratch_shapes=[
            pltpu.VMEM((rows, columns), BF),
            pltpu.SemaphoreType.DMA((25,)),
            pltpu.SemaphoreType.DMA((25,)),
            pltpu.SemaphoreType.DMA((1,)),
        ],
        compiler_params=pltpu.CompilerParams(collective_id=5, has_side_effects=True, vmem_limit_bytes=40 * 2**20),
        name="gather_sums",
    )(term, piece)


def assemble_kernel(by_row_ref, by_head_ref, qkv_ref, out_ref, rest_ref):
    heads = [by_row_ref[0, h].astype(F32) for h in range(8)]
    ends = (0, WIDTH, WIDTH + HEAD_SIZE, HEAD_COLUMNS)
    qkv_ref[...] = jnp.concatenate([t[:, a:b] for a, b in zip(ends[:-1], ends[1:]) for t in heads], axis=1)
    tail = heads[0]
    for t in heads[1:]:
        tail = tail + t
    rest_ref[...] = tail[:, HEAD_COLUMNS:384]
    for parity in range(2):
        parts = [by_head_ref[parity, y, 0, :, 384:].astype(F32).T for y in range(4)]
        out_ref[parity * WIDTH : (parity + 1) * WIDTH, :] = jnp.concatenate(parts, axis=1)


def assemble(gathered):
    _, _, piece, columns = gathered.shape
    shard = 4 * piece
    return pl.pallas_call(
        assemble_kernel,
        out_shape=(
            jax.ShapeDtypeStruct((shard, 8 * HEAD_COLUMNS), F32),
            jax.ShapeDtypeStruct((2 * WIDTH, 4 * shard), F32),
            jax.ShapeDtypeStruct((shard, 64), F32),
        ),
        grid=(4,),
        in_specs=[
            pl.BlockSpec((1, 8, piece, columns), lambda i: (i, 0, 0, 0)),
            pl.BlockSpec((2, 4, 1, piece, columns), lambda i: (0, 0, i, 0, 0)),
        ],
        out_specs=(
            pl.BlockSpec((piece, 8 * HEAD_COLUMNS), lambda i: (i, 0)),
            pl.BlockSpec((2 * WIDTH, shard), lambda i: (0, i)),
            pl.BlockSpec((piece, 64), lambda i: (i, 0)),
        ),
        compiler_params=pltpu.CompilerParams(vmem_limit_bytes=40 * 2**20),
        name="assemble",
    )(gathered, gathered.reshape(2, 4, 4, piece, columns))


MESH = pl.DeviceIdType.MESH
ANY = pl.BlockSpec(memory_space=pl.ANY)


class Copies:
    def __init__(self, send, recv, local):
        self.send, self.recv, self.local = send, recv, local
        self.remote_count = self.local_count = 0
        self.started, self.kept = [], []

    def to(self, source, target, device):
        k = self.remote_count
        self.remote_count += 1
        copy = pltpu.make_async_remote_copy(
            source, target, self.send.at[k], self.recv.at[k], device_id=device, device_id_type=MESH
        )
        copy.start()
        self.started.append(copy)
        return copy

    def keep(self, source, middle, target):
        k = self.local_count
        self.local_count += 2
        first = pltpu.make_async_copy(source, middle, self.local.at[k])
        first.start()
        self.kept.append((first, pltpu.make_async_copy(middle, target, self.local.at[k + 1])))

    def move_kept(self):
        for first, second in self.kept:
            first.wait()
            second.start()

    def finish(self, arrived):
        for copy in self.started:
            copy.wait_send()
            if not any(copy is other for other in arrived):
                copy.wait_recv()
        for _, second in self.kept:
            second.wait()


def meet(devices):
    barrier = pltpu.get_barrier_semaphore()
    for device in devices:
        pl.semaphore_signal(barrier, inc=1, device_id=device, device_id_type=MESH)
    pl.semaphore_wait(barrier, len(devices))


def gather_rows_kernel(
    tok_ref, wp_ref, gain_ref, wo_ref, tok_out, wp_out, gain_out, wo_out, v_tok, v_wp, v_gain, v_wo, send, recv, local
):
    place, stream = turned(lax.axis_index("ctx")), lax.axis_index("wsh")
    x, z = place % 4, (place // 4) % 2
    right, left = {"ctx": turned(place - x + (x + 1) % 4)}, {"ctx": turned(place - x + (x + 3) % 4)}
    across = place + 4 - 8 * z
    other = {"wsh": stream + 1 - 2 * (stream % 2)}
    far = {"ctx": turned(across), "wsh": (stream + 2) % 4}
    meet([right, left, {"ctx": turned(across)}, other, far])
    copies = Copies(send, recv, local)
    half = tok_ref.shape[0] // 2
    own, own_z = z * 4 + x, (1 - z) * 4 + x
    left_id, right_id = z * 4 + (x + 3) % 4, z * 4 + (x + 1) % 4
    left_z, right_z = (1 - z) * 4 + (x + 3) % 4, (1 - z) * 4 + (x + 1) % 4

    def rows(ref, h):
        return ref.at[pl.ds(h * half, half)]

    def spot(block, h):
        return tok_out.at[block, pl.ds(h * half, half)]

    head = place % 8
    far_wp = copies.to(wp_ref.at[across % 8], wp_out.at[stream], far)
    far_gain = copies.to(gain_ref, gain_out.at[stream], far)
    cross = [copies.to(rows(tok_ref, h), spot(own, h), {"ctx": turned(across)}) for h in range(2)]
    to_right = [copies.to(rows(tok_ref, h), spot(own, h), right) for h in (0, 1)]
    to_left = [copies.to(rows(tok_ref, h), spot(own, h), left) for h in (1, 0)]
    copies.to(wp_ref.at[head], wp_out.at[stream], other)
    copies.to(gain_ref, gain_out.at[stream], other)
    third = wo_ref.shape[0] // 3
    parts = [pl.ds(i * third, third) for i in range(3)]
    far_wo = [copies.to(wo_ref.at[p], wo_out.at[stream, p], far) for p in parts]
    copies.to(wo_ref, wo_out.at[stream], other)
    copies.keep(tok_ref, v_tok, tok_out.at[own])
    copies.keep(wp_ref.at[head], v_wp, wp_out.at[stream])
    copies.keep(gain_ref, v_gain, gain_out.at[stream])
    copies.keep(wo_ref, v_wo, wo_out.at[stream])
    copies.move_kept()

    arrived = []

    def arrive(copy):
        copy.wait_recv()
        arrived.append(copy)

    far_stream = (stream + 2) % 4
    arrive(far_wp)
    copies.to(wp_out.at[far_stream], wp_out.at[far_stream], other)
    arrive(far_gain)
    copies.to(gain_out.at[far_stream], gain_out.at[far_stream], other)
    arrive(to_right[0])
    copies.to(spot(left_id, 0), spot(left_id, 0), right)
    arrive(to_left[0])
    copies.to(spot(right_id, 1), spot(right_id, 1), left)
    arrive(cross[0])
    arrive(cross[1])
    z_right = [copies.to(spot(own_z, h), spot(own_z, h), right) for h in (0, 1)]
    z_left = [copies.to(spot(own_z, h), spot(own_z, h), left) for h in (1, 0)]
    arrive(z_right[0])
    copies.to(spot(left_z, 0), spot(left_z, 0), right)
    arrive(z_left[0])
    copies.to(spot(right_z, 1), spot(right_z, 1), left)
    for p, copy in zip(parts, far_wo):
        arrive(copy)
        copies.to(wo_out.at[far_stream, p], wo_out.at[far_stream, p], other)
    copies.finish(arrived)


def gather_rows(tok, wp, gain, wo):
    return pl.pallas_call(
        gather_rows_kernel,
        out_shape=(
            jax.ShapeDtypeStruct((8,) + tok.shape, BF),
            jax.ShapeDtypeStruct((4,) + wp.shape[1:], BF),
            jax.ShapeDtypeStruct((4,) + gain.shape, BF),
            jax.ShapeDtypeStruct((4,) + wo.shape, BF),
        ),
        in_specs=[ANY] * 4,
        out_specs=(ANY,) * 4,
        scratch_shapes=[
            pltpu.VMEM(tok.shape, BF),
            pltpu.VMEM(wp.shape[1:], BF),
            pltpu.VMEM(gain.shape, BF),
            pltpu.VMEM(wo.shape, BF),
            pltpu.SemaphoreType.DMA((27,)),
            pltpu.SemaphoreType.DMA((27,)),
            pltpu.SemaphoreType.DMA((8,)),
        ],
        compiler_params=pltpu.CompilerParams(collective_id=1, has_side_effects=True, vmem_limit_bytes=40 * 2**20),
        name="gather_rows",
    )(tok, wp, gain, wo)


def gather_keys_kernel(kv_ref, kv_out, v_kv, send, recv, local):
    place = turned(lax.axis_index("ctx"))
    y = place // 8
    up, down = {"ctx": turned((place + 8) % 32)}, {"ctx": turned((place + 24) % 32)}
    meet([up, down])
    copies = Copies(send, recv, local)
    half = kv_ref.shape[0] // 2

    def rows(h):
        return kv_ref.at[pl.ds(h * half, half)]

    def spot(block, h):
        return kv_out.at[block, pl.ds(h * half, half)]

    to_up = [copies.to(rows(h), spot(y, h), up) for h in (0, 1)]
    to_down = [copies.to(rows(h), spot(y, h), down) for h in (1, 0)]
    copies.keep(kv_ref, v_kv, kv_out.at[y])
    copies.move_kept()
    to_up[0].wait_recv()
    copies.to(spot((y + 3) % 4, 0), spot((y + 3) % 4, 0), up)
    to_down[0].wait_recv()
    copies.to(spot((y + 1) % 4, 1), spot((y + 1) % 4, 1), down)
    copies.finish([to_up[0], to_down[0]])


def gather_keys(kv):
    return pl.pallas_call(
        gather_keys_kernel,
        out_shape=jax.ShapeDtypeStruct((4,) + kv.shape, BF),
        in_specs=[ANY],
        out_specs=ANY,
        scratch_shapes=[
            pltpu.VMEM(kv.shape, BF),
            pltpu.SemaphoreType.DMA((6,)),
            pltpu.SemaphoreType.DMA((6,)),
            pltpu.SemaphoreType.DMA((2,)),
        ],
        compiler_params=pltpu.CompilerParams(collective_id=2, has_side_effects=True, vmem_limit_bytes=40 * 2**20),
        name="gather_keys",
    )(kv)


FF_STEP = 256


def experts_kernel(
    rows_ref, grads_ref, w_ref, back_out, returned_out, terms_out,
    w_v, x_v, g_v, turned_x, turned_g, out_v, d_in_v, acc_v, gate_v, up_v, hidden_v, d_gate_v, d_up_v, sent_v, got_v,
    send, recv, local,
):
    index, stream = lax.axis_index("ctx"), lax.axis_index("wsh")
    x, mine = index % 4, index // 2
    inner = (x + 1) // 2 % 2

    def device(p):
        return {"ctx": p // 2 * 4 + (1 - inner) * (3 * (p % 2)) + inner * (1 + p % 2)}

    peers = [(mine + k) % 16 for k in range(1, 16)]
    core = stream % 2
    other = {"wsh": stream + 1 - 2 * core}
    meet([device(p) for p in peers] + [other])
    copies = Copies(send, recv, local)
    width, rows = turned_x.shape
    quarter = width // 4
    own = []

    def here(source, target):
        copy = pltpu.make_async_copy(source, target, local.at[len(own)])
        copy.start()
        own.append(copy)
        return copy

    came = [copies.to(rows_ref.at[p], x_v.at[mine], device(p)) for p in peers]
    own_x = here(rows_ref.at[mine], x_v.at[mine])
    weights = [
        here(w_ref.at[4 * k + q, m], w_v.at[k, m, pl.ds(q * quarter, quarter)])
        for k in range(2)
        for q in range(4)
        for m in range(3)
    ]
    came_g = [copies.to(grads_ref.at[p], g_v.at[mine], device(p)) for p in peers]
    own_g = here(grads_ref.at[mine], g_v.at[mine])
    arrived = []

    def arrive(several):
        for copy in several:
            copy.wait_recv()
            arrived.append(copy)

    for copy in weights:
        copy.wait()
    arrive(came)
    own_x.wait()
    steps = w_v.shape[3] // FF_STEP
    acc_v[...] = jnp.zeros_like(acc_v)

    def forward(i, carry):
        k, at = i // steps, pl.ds(pl.multiple_of(i % steps * FF_STEP, FF_STEP), FF_STEP)
        inputs = x_v[...].reshape(rows, width)
        gate = dot(inputs, w_v[k, 0, :, at])
        up = dot(inputs, w_v[k, 1, :, at])
        hidden = (gate * jax.nn.sigmoid(gate) * up).astype(BF)
        gate_v[i] = gate
        up_v[i] = up
        hidden_v[k, :, at] = hidden
        acc_v[...] += dot(hidden, w_v[k, 2, :, at], NT)
        return carry

    lax.fori_loop(0, 2 * steps, forward, 0)
    out_v[...] = acc_v[...].astype(BF).reshape(out_v.shape)
    for p in peers:
        copies.to(out_v.at[p], back_out.at[mine], device(p))
    own_back = here(out_v.at[mine], back_out.at[mine])
    for q in range(4):
        at = slice(q * quarter, (q + 1) * quarter)
        turned_x[at, :] = x_v[:, :, at].reshape(rows, quarter).T
    acc_v[...] = jnp.zeros_like(acc_v)
    arrive(came_g)
    own_g.wait()

    def backward(i, carry):
        k, at = i // steps, pl.ds(pl.multiple_of(i % steps * FF_STEP, FF_STEP), FF_STEP)
        d_hidden = dot(g_v[...].reshape(rows, width), w_v[k, 2, :, at])
        gate, up = gate_v[i], up_v[i]
        sigmoid = jax.nn.sigmoid(gate)
        d_gate = (d_hidden * up * sigmoid * (1.0 + gate * (1.0 - sigmoid))).astype(BF)
        d_up = (d_hidden * (gate * sigmoid)).astype(BF)
        d_gate_v[k, :, at] = d_gate
        d_up_v[k, :, at] = d_up
        acc_v[...] += dot(d_gate, w_v[k, 0, :, at], NT) + dot(d_up, w_v[k, 1, :, at], NT)
        return carry

    lax.fori_loop(0, 2 * steps, backward, 0)
    d_in_v[...] = acc_v[...].astype(BF).reshape(d_in_v.shape)
    for p in peers:
        copies.to(d_in_v.at[p], returned_out.at[mine], device(p))
    own_returned = here(d_in_v.at[mine], returned_out.at[mine])
    for q in range(4):
        at = slice(q * quarter, (q + 1) * quarter)
        turned_g[at, :] = g_v[:, :, at].reshape(rows, quarter).T

    def terms(k, z, c):
        at = pl.ds(pl.multiple_of((2 * z + c) * quarter, quarter), quarter)
        part = turned_x[at, :]
        return (
            dot(part, d_gate_v[k]),
            dot(part, d_up_v[k]),
            dot(turned_g[at, :], hidden_v[k]),
        )

    crossing = []
    for z in range(2):

        def other_term(k, carry, z=z):
            for m, term in enumerate(terms(k, z, 1 - core)):
                sent_v[z, k, m] = term.astype(BF)
            return carry

        lax.fori_loop(0, 2, other_term, 0)
        crossing.append(copies.to(sent_v.at[z], got_v.at[z], other))
    for z in range(2):

        def own_term(k, carry, z=z):
            for m, term in enumerate(terms(k, z, core)):
                terms_out[z, k, m] = (term + got_v[z, k, m].astype(F32)).astype(BF)
            return carry

        arrive([crossing[z]])
        lax.fori_loop(0, 2, own_term, 0)
    copies.finish(arrived)
    own_back.wait()
    own_returned.wait()


def experts(send_rows, send_grads, weights):
    groups, capacity, width = send_rows.shape
    rows = groups * capacity
    half = weights.shape[3]
    vmem = pltpu.VMEM
    steps = 2 * half // FF_STEP
    slots = vmem(send_rows.shape, BF)
    terms = (2, 2, 3, width // 4, half)
    return pl.pallas_call(
        experts_kernel,
        out_shape=(
            jax.ShapeDtypeStruct(send_rows.shape, BF),
            jax.ShapeDtypeStruct(send_rows.shape, BF),
            jax.ShapeDtypeStruct(terms, BF),
        ),
        in_specs=[ANY, ANY, ANY],
        out_specs=(ANY, ANY, pl.BlockSpec(memory_space=pltpu.VMEM)),
        scratch_shapes=[
            vmem((2, 3, width, half), BF),
            slots,
            slots,
            vmem((width, rows), BF),
            vmem((width, rows), BF),
            slots,
            slots,
            vmem((rows, width), F32),
            vmem((steps, rows, FF_STEP), F32),
            vmem((steps, rows, FF_STEP), F32),
            vmem((2, rows, half), BF),
            vmem((2, rows, half), BF),
            vmem((2, rows, half), BF),
            vmem(terms, BF),
            vmem(terms, BF),
            pltpu.SemaphoreType.DMA((62,)),
            pltpu.SemaphoreType.DMA((62,)),
            pltpu.SemaphoreType.DMA((28,)),
        ],
        compiler_params=pltpu.CompilerParams(collective_id=6, has_side_effects=True, vmem_limit_bytes=56 * 2**20),
        cost_estimate=pl.CostEstimate(flops=15 * 10**9, bytes_accessed=10**8, transcendentals=10**6),
        name="experts",
    )(send_rows, send_grads, weights)


def prepare_kernel(qkv_ref, router_ref, wo_ref, wp_out, wo_out):
    rows = qkv_ref.shape[0]
    experts = router_ref.shape[1]
    wo_out[...] = wo_ref[...].astype(BF)
    router = router_ref[...].astype(BF)
    tail = jnp.zeros((rows, wp_out.shape[2] - HEAD_COLUMNS - experts), BF)
    k_at, v_at = QUERY_HEADS * HEAD_SIZE, (QUERY_HEADS + KEY_VALUE_HEADS) * HEAD_SIZE
    for h in range(KEY_VALUE_HEADS):
        wp_out[h] = jnp.concatenate(
            [
                qkv_ref[:, h * WIDTH : (h + 1) * WIDTH].astype(BF),
                qkv_ref[:, k_at + h * HEAD_SIZE : k_at + (h + 1) * HEAD_SIZE].astype(BF),
                qkv_ref[:, v_at + h * HEAD_SIZE : v_at + (h + 1) * HEAD_SIZE].astype(BF),
                router,
                tail,
            ],
            axis=1,
        )


def prepare(w_qkv, w_router, w_out):
    shard = w_qkv.shape[0]
    step = shard // 3

    def block(n):
        return pl.BlockSpec((step, n), lambda i: (i, 0))

    return pl.pallas_call(
        prepare_kernel,
        out_shape=(
            jax.ShapeDtypeStruct((KEY_VALUE_HEADS, shard, 384), BF),
            jax.ShapeDtypeStruct(w_out.shape, BF),
        ),
        grid=(3,),
        in_specs=[block(w_qkv.shape[1]), block(w_router.shape[1]), block(w_out.shape[1])],
        out_specs=(
            pl.BlockSpec((KEY_VALUE_HEADS, step, 384), lambda i: (0, i, 0)),
            block(w_out.shape[1]),
        ),
        compiler_params=pltpu.CompilerParams(vmem_limit_bytes=40 * 2**20),
        name="prepare",
    )(w_qkv, w_router, w_out)


def input_gradient_kernel(stream_ref, d_qkv_ref, p0, p1, p2, p3, x_ref, d_mid_ref, gain_ref, out_ref, acc_ref):
    step = pl.program_id(0)
    stream = stream_ref[0]

    @pl.when(step == 0)
    def _():
        acc_ref[...] = jnp.zeros_like(acc_ref)

    grad = d_qkv_ref[0, :, :HEAD_COLUMNS]
    for j, piece in enumerate((p0, p1, p2, p3)):
        acc_ref[stream ^ j] += dot(grad, piece[0, :, :HEAD_COLUMNS], NT)

    @pl.when(step == pl.num_programs(0) - 1)
    def _():
        x = x_ref[...].astype(F32)
        scale = rms_scale(x)
        quarter = acc_ref.shape[2]
        inner = 0.0
        for q in range(4):
            at = slice(q * quarter, (q + 1) * quarter)
            inner += jnp.sum(acc_ref[q] * gain_ref[:, at] * x[:, at], axis=-1, keepdims=True)
        inner = inner * (1.0 / x.shape[1])
        for q in range(4):
            at = slice(q * quarter, (q + 1) * quarter)
            out_ref[:, at] = (
                d_mid_ref[:, at] + scale * (acc_ref[q] * gain_ref[:, at]) - x[:, at] * scale**3 * inner
            ).astype(BF)


def input_gradient(stream, d_qkv, pieces, x, d_middle, gain):
    heads, rows, _ = d_qkv.shape
    width = x.shape[1]

    def whole(a):
        return pl.BlockSpec(a.shape, lambda h, s: (0, 0))

    def by_head(a):
        return pl.BlockSpec((1,) + a.shape[1:], lambda h, s: (h, 0, 0))

    gain = gain.reshape(1, width)
    return pl.pallas_call(
        input_gradient_kernel,
        out_shape=jax.ShapeDtypeStruct(x.shape, BF),
        grid_spec=pltpu.PrefetchScalarGridSpec(
            num_scalar_prefetch=1,
            grid=(heads,),
            in_specs=[by_head(d_qkv)] + [by_head(p) for p in pieces] + [whole(x), whole(d_middle), whole(gain)],
            out_specs=whole(x),
            scratch_shapes=[pltpu.VMEM((4, rows, width // 4), F32)],
        ),
        compiler_params=pltpu.CompilerParams(vmem_limit_bytes=40 * 2**20),
        cost_estimate=pl.CostEstimate(flops=10**9, bytes_accessed=12 * 10**6, transcendentals=0),
        name="input_gradient",
    )(stream.reshape(1).astype(jnp.int32), d_qkv, *pieces, x, d_middle, gain)


def swap(x, groups, axis="ctx"):
    return lax.all_to_all(x, axis, 0, 0, axis_index_groups=groups, tiled=True)


def rms_scale(values):
    return lax.rsqrt(jnp.mean(values * values, axis=-1, keepdims=True) + EPSILON)


def body(
    tokens,
    lengths,
    deal,
    expert_ids,
    gain_attn,
    w_qkv,
    w_out,
    gain_moe,
    w_router,
    w_gate,
    w_up,
    w_down,
    cotangent,
):
    stream = lax.axis_index("wsh")
    index = lax.axis_index("ctx")
    place = turned(index)
    rows, width = tokens.shape[1], tokens.shape[2]
    shard = w_qkv.shape[0]
    experts_count = w_router.shape[1]
    capacity = 2 * rows * TOP // experts_count
    head = place % 8
    head_row = place // 8
    lengths_row = lax.dynamic_index_in_dim(lengths, stream, 0, keepdims=False)
    deal_row = lax.dynamic_index_in_dim(deal, stream, 0, keepdims=False)
    blocks = deal_row.shape[0]
    deal_row = deal_row.reshape(4, 2, 4, 2).transpose(2, 1, 0, 3).reshape(blocks)
    block_ids = jnp.arange(blocks, dtype=jnp.int32)
    inverse = jnp.sum(jnp.where(deal_row[None, :] == block_ids[:, None], block_ids[None, :], 0), axis=1)
    own_blocks = lax.dynamic_slice_in_dim(deal_row, head_row * 16, 16)
    meta = jnp.concatenate([inverse, own_blocks, jnp.cumsum(lengths_row)]).astype(jnp.int32)

    q_columns = QUERY_HEADS * HEAD_SIZE
    by_head, own_out = prepare(w_qkv, w_router, w_out)
    own_gains = jnp.concatenate(
        [gain_attn.astype(BF)[None], gain_moe.astype(BF)[None], jnp.zeros((14, shard), BF)], axis=0
    )
    group_tokens, head_full, gains, full_out = gather_rows(tokens[0], by_head, own_gains, own_out)
    head_full = head_full.reshape(width, -1)
    head_weight = head_full[:, :HEAD_COLUMNS]
    full_router = head_full[:, HEAD_COLUMNS : HEAD_COLUMNS + experts_count]
    gain_first = gains[:, 0].reshape(width).astype(F32)
    gain_second = gains[:, 1].reshape(width).astype(F32)
    full_out = full_out.reshape(q_columns, width)

    w_gate, w_up, w_down, _ = lax.optimization_barrier((w_gate, w_up, w_down, gains))
    expert_shard = jnp.stack([w_gate[0].astype(BF), w_up[0].astype(BF), w_down[0].T.astype(BF)])
    expert_all = lax.all_gather(expert_shard, ("ctx", "wsh"), axis_index_groups=OWNERS)
    far_qkv = lax.ppermute(by_head, ("ctx", "wsh"), NEXT_Z)
    qkv_pieces = [
        by_head,
        lax.ppermute(by_head, "wsh", OTHER_CORE),
        far_qkv,
        lax.ppermute(far_qkv, "wsh", OTHER_CORE),
    ]

    group_x = group_tokens.reshape(8 * rows, width).astype(F32)
    group_act = (group_x * rms_scale(group_x) * gain_first).astype(BF)
    head_qkv = dot(group_act, head_weight).astype(BF)
    kv_all = gather_keys(head_qkv[:, WIDTH:]).reshape(32 * rows, 2 * HEAD_SIZE)
    head_q = head_qkv[:, :WIDTH]
    head_attn, lse = run_forward(meta, head_q, kv_all)
    attn_low = swap(head_attn.reshape(8, rows, WIDTH), ROW).transpose(1, 0, 2).reshape(rows, q_columns)

    x_first = tokens[0].astype(F32)
    middle = x_first + dot(attn_low, full_out)
    scale_second = rms_scale(middle)
    act_moe = (middle * scale_second * gain_second).astype(BF)
    logits = dot(act_moe, full_router)
    choice = expert_ids[0]
    expert_range = jnp.arange(experts_count, dtype=jnp.int32)
    picked_hot = choice[:, :, None] == expert_range[None, None, :]
    picked = jnp.sum(jnp.where(picked_hot, logits[:, None, :], 0.0), axis=-1)
    picked_exp = jnp.exp(picked - jnp.max(picked, axis=-1, keepdims=True))
    gates = picked_exp / jnp.sum(picked_exp, axis=-1, keepdims=True)
    flat_ids = choice.reshape(-1)
    assign_hot = (flat_ids[:, None] == expert_range[None, :]).astype(jnp.int32)
    ranks = jnp.sum((jnp.cumsum(assign_hot, axis=0) - 1) * assign_hot, axis=1)
    slots = (flat_ids * capacity + ranks).reshape(rows, TOP)
    slot_range = jnp.arange(experts_count * capacity, dtype=jnp.int32)
    hot = [slots[:, j][:, None] == slot_range[None, :] for j in range(TOP)]
    hot_low = [h.astype(BF) for h in hot]
    hot_any = hot_low[0] + hot_low[1]
    slot_gate = sum(jnp.sum(jnp.where(hot[j], gates[:, j][:, None], 0.0), axis=0) for j in range(TOP))

    send_rows = dot(hot_any, act_moe, TN).astype(BF).reshape(experts_count, capacity, width)
    send_grads = (slot_gate[:, None] * dot(hot_any, cotangent[0], TN)).astype(BF)
    back_rows, returned, expert_terms = experts(send_rows, send_grads.reshape(experts_count, capacity, width), expert_all)
    back_rows, returned = (r.reshape(-1, width) for r in (back_rows, returned))

    both = [dot(hot_low[j], back_rows) for j in range(TOP)]
    output_rows = (middle + gates[:, :1] * both[0] + gates[:, 1:] * both[1]).astype(BF)
    d_out = cotangent[0].astype(F32)
    d_gates = jnp.stack([jnp.sum(d_out * both[j], axis=-1) for j in range(TOP)], axis=1)
    d_picked = gates * (d_gates - jnp.sum(gates * d_gates, axis=-1, keepdims=True))
    d_logits = jnp.sum(jnp.where(picked_hot, d_picked[:, :, None], 0.0), axis=1).astype(BF)
    d_act_moe = dot(hot_any, returned) + dot(d_logits, full_router, NT)
    d_router_local = dot(act_moe, d_logits, TN)
    d_gain_second = jnp.sum(d_act_moe * middle * scale_second, axis=0)
    scaled = d_act_moe * gain_second
    d_middle = (
        d_out
        + scale_second * scaled
        - middle * scale_second**3 * jnp.mean(scaled * middle, axis=-1, keepdims=True)
    )
    d_branch = d_middle.astype(BF)

    d_attn = dot(d_branch, full_out, NT).astype(BF)
    head_d_attn = swap(d_attn.reshape(rows, 8, WIDTH).transpose(1, 0, 2), ROW).reshape(8 * rows, WIDTH)
    group_branch = lax.all_gather(d_branch, "ctx", axis_index_groups=ROW).reshape(8 * rows, width)
    head_d_attn, expert_terms, qkv_pieces = lax.optimization_barrier((head_d_attn, expert_terms, qkv_pieces))
    side = stream // 2
    recv_terms = lax.ppermute(
        lax.dynamic_index_in_dim(expert_terms, 1 - side, 0, keepdims=False), "wsh", OTHER_SIDE
    )
    keep_terms = lax.dynamic_index_in_dim(expert_terms, side, 0, keepdims=False)
    pending_terms = (keep_terms, recv_terms)
    d_q, d_kv = run_backward(meta, head_q, kv_all, head_attn, lse, head_d_attn)
    out_term = dot(group_branch, head_attn, TN).astype(BF).reshape(4, 4, shard // 4, WIDTH).transpose(1, 0, 2, 3)
    small_term = jnp.concatenate(
        [d_router_local.astype(BF), d_gain_second.astype(BF)[:, None], jnp.zeros((width, 47), BF)], axis=1
    )
    kv_terms, out_terms = exchange_terms(d_kv.reshape(4, 8 * rows, 2 * HEAD_SIZE), out_term)
    (keep_terms, recv_terms), kv_terms = lax.optimization_barrier((pending_terms, kv_terms))
    expert_terms = (keep_terms.astype(F32) + recv_terms.astype(F32)).astype(BF)
    half = index % 2
    keep_terms = lax.dynamic_index_in_dim(expert_terms, half, 0, keepdims=False)
    recv_terms = lax.ppermute(
        lax.dynamic_index_in_dim(expert_terms, 1 - half, 0, keepdims=False), "ctx", OTHER_HALF
    )
    out_piece = lax.ppermute(
        jnp.sum(out_terms.astype(F32), axis=(0, 1)).astype(BF), ("ctx", "wsh"), MOVES
    )
    head_d_qkv, term = weight_terms(group_act, d_q, kv_terms, small_term)
    d_qkv, terms = return_terms(head_d_qkv, term)
    d_tokens = input_gradient(stream, d_qkv, qkv_pieces, tokens[0], d_middle, gain_first)
    terms, recv_terms = lax.optimization_barrier((terms, recv_terms))
    expert_own = keep_terms.astype(F32) + recv_terms.astype(F32)
    d_w_qkv, d_w_out, rest = assemble(gather_sums(terms, out_piece))
    d_gain_first = jnp.sum(d_w_qkv * w_qkv.astype(BF).astype(F32), axis=1) / gain_attn.astype(BF).astype(F32)
    return (
        output_rows[None],
        d_tokens[None],
        d_gain_first,
        d_w_qkv,
        d_w_out,
        rest[:, experts_count],
        rest[:, :experts_count],
        expert_own[0][None],
        expert_own[1][None],
        expert_own[2].T[None],
    )


def solution(mesh):
    placed = (
        P("wsh", "ctx", None),
        P(),
        P(),
        P("wsh", "ctx", None),
        P("wsh"),
        P("wsh", None),
        P("wsh", None),
        P("wsh"),
        P("wsh", None),
        P("ctx", "wsh", None),
        P("ctx", "wsh", None),
        P("ctx", None, "wsh"),
        P("wsh", "ctx", None),
    )
    return jax.shard_map(
        body,
        mesh=mesh,
        in_specs=placed,
        out_specs=(
            P("wsh", "ctx", None),
            P("wsh", "ctx", None),
            P("wsh"),
            P("wsh", None),
            P("wsh", None),
            P("wsh"),
            P("wsh", None),
            P("ctx", "wsh", None),
            P("ctx", "wsh", None),
            P("ctx", None, "wsh"),
        ),
        check_vma=False,
    )
```

time: 528 us -> 482 us (0.913)
  Pallas kernels: 179 us -> 287 us
  waiting for transfers between devices: 98.5 us -> 12.9 us
  starting transfers between devices: 79 us -> 27.8 us
  matrix products: 35.8 us -> 28.4 us
  local copies, waits for them, and re-layouts: 77.6 us -> 70.7 us
    pallas_call x4 -> x5, Pallas kernels: 37.6 us -> 168 us  [the longest x1 75.1 us: experts(): pl.pallas_call(experts_kernel, out_shape=(jax.ShapeDtypeStruct(send_rows....]
    all_to_all x10 -> x2, waiting for transfers between devices: 83.9 us -> 12.8 us  [swap(): return lax.all_to_all(x, axis, 0, 0, axis_index_groups=groups, tiled=True)]
    all_to_all x10 -> x2, starting transfers between devices: 65.3 us -> 12.6 us  [swap(): return lax.all_to_all(x, axis, 0, 0, axis_index_groups=groups, tiled=True)]
    ppermute x1, waiting for transfers between devices: 14.5 us -> 0.01 us  [body(): lax.ppermute(lax.dynamic_index_in_dim(expert_terms, 1 - side, 0, keepdims...]
    pallas_call x1, Pallas kernels: 37.9 us -> 24 us  [run_backward(): local_call(attention_backward, (jax.ShapeDtypeStruct((rows, WIDTH), BF),...]
    pallas_call x1, Pallas kernels: 32.5 us -> 19.8 us  [run_forward(): local_call(attention_forward, (jax.ShapeDtypeStruct((rows, WIDTH), BF), j...]
    concatenate x3 -> x1, local copies, waits for them, and re-layouts: 9.16 us -> 0.59 us  [body(): jnp.concatenate([d_router_local.astype(BF), d_gain_second.astype(BF)[:, N...]
    pallas_call x1, Pallas kernels: 12.7 us -> 21.2 us  [gather_keys(): pl.pallas_call(gather_keys_kernel, out_shape=jax.ShapeDtypeStruct((4,) +...]
  transfers between devices with their start and end apart: 19 -> 10, of which waited for: 10 -> 1; matrix products, arithmetic and copies ran while one was open for 18% -> 18% of each run, Pallas kernels for 24% -> 43%
where the time goes in v2:
time: 482 us; the launch traced here: 475 us
  Pallas kernels  287 us (60%)
  local copies, waits for them, and re-layouts  70.7 us (15%)
  other arithmetic  34.5 us (7%)
  matrix products  28.4 us (6%)
  starting transfers between devices  27.8 us (6%)
  between operations  14.7 us (3%)
  waiting for transfers between devices  12.9 us (3%)
    pallas_call x1, Pallas kernels, experts(): pl.pallas_call(experts_kernel, out_shape=(jax.ShapeDtypeStruct(send_rows....  75.1 us
    pallas_call x1, Pallas kernels, gather_rows(): pl.pallas_call(gather_rows_kernel, out_shape=(jax.ShapeDtypeStruct((8,) +...  39.9 us
    pallas_call x1, Pallas kernels, gather_sums(): pl.pallas_call(gather_sums_kernel, out_shape=jax.ShapeDtypeStruct((4, 8,...  36.6 us
    unnamed x126, local copies, waits for them, and re-layouts  32.3 us
    dot_general x12, matrix products, dot(): return lax.dot_general(a, b, (dims, ((), ())), preferred_element_type=F32)  28.4 us
    pallas_call x1, Pallas kernels, exchange_terms(): pl.pallas_call(exchange_terms_kernel, out_shape=(jax.ShapeDtypeStruct(kv....  26.9 us
    pallas_call x1, Pallas kernels, return_terms(): pl.pallas_call(return_terms_kernel, out_shape=(jax.ShapeDtypeStruct(grad....  26.4 us
    pallas_call x1, Pallas kernels, run_backward(): local_call(attention_backward, (jax.ShapeDtypeStruct((rows, WIDTH), BF),...  24 us
  transfers between devices with their start and end apart: 10, of which 1 were waited for; matrix products, arithmetic and copies ran while one was open for 18% of the time, Pallas kernels for 43%

profile of v2, /device:TPU:8, one launch (start us, length us, event | category | flops | bytes accessed | tf_op | source)
XLA Modules:
  0.0 475.3 jit_solution(9477576061211831986)
XLA Ops:
  9.6 2.1 copy-done.3
  11.7 1.7 copy-done.10
  14.5 39.9 %gather_rows.1 = (bf16[8,128,1536]{2,1,0:T(8,128)(2,1)S(1)}, bf16[4,384,384]{2,1,0:T(8,128)(2,1)S(1)}, bf16[4,16,384]{2,1,0:T(8,128)(2,1)S(1)}, bf16[4,384,1536]{2,1,0:T(8,128)(2,1)S(1)}) custom-call(bf16[128,1536]{1,0:T(8,128)(2,1)S(1)} %bitcast.111, bf16[8,384,384]{2,1,0:T(8,128)(2,1)S(1)} %get-tuple-element.69.wp_ref.p0, ...), custom_call_target="tpu_custom_call" | custom-call | tf_op jit(solution)/shard_map/gather_rows/pallas_call | solution.py:682
  54.4 2.2 copy-done.2
  58.2 2.6 copy.121
  60.8 1.2 convert_element_type.172
  62.1 1.2 convert_element_type.173
  63.3 1.2 pad_maximum_fusion
  64.5 1.8 collective-permute-start.1
  66.2 1.4 convert_reduce_fusion
  69.1 2.8 fusion.1.act_ref
  71.9 1.8 convolution_convert_fusion.4
  76.1 1.3 copy.112
  80.1 21.2 %gather_keys.1 = bf16[4,1024,128]{2,1,0:T(8,128)(2,1)S(1)} custom-call(bf16[1024,128]{1,0:T(8,128)(2,1)S(1)} %copy-done.21), custom_call_target="tpu_custom_call" | custom-call | tf_op jit(solution)/shard_map/gather_keys/pallas_call | solution.py:732
  102.5 1.2 copy-done.17
  103.7 1.1 copy-done.30
  104.9 19.8 %attention_forward.1 = (bf16[1024,192]{1,0:T(8,128)(2,1)S(1)}, f32[17,1,192]{2,1,0:T(1,128)S(1)}) custom-call(s32[84]{0:T(128)S(1)} %pad_add_fusion.meta, bf16[1024,192]{1,0:T(8,128)(2,1)S(1)} %copy-done.30, bf16[4096,128]{1,0:T(8,128)(2,1)S(1)} %bitcast.114), custom_call_target="tpu_custom_call" | custom-call | flops 4000000000 | bytes 10000000 | tf_op jit(solution)/shard_map/attention_forward/pallas_call | solution.py:272
  126.1 2.0 copy.115
  128.1 4.9 %all-to-all-start = ((bf16[8,128,192]{1,2,0:T(8,128)(2,1)}), bf16[8,128,192]{1,2,0:T(8,128)(2,1)}, u32[]{:S(2)}, u32[]{:S(2)}) async-start(bf16[8,128,192]{1,2,0:T(8,128)(2,1)} %copy.115), calls=%async_computation | async-start | bytes 786432 | tf_op jit(solution)/shard_map/all_to_all | solution.py:1024
  134.7 1.5 eq.97
  137.0 1.5 copy.117
  139.1 1.9 reduce-window.20
  140.9 1.5 slice_reduce_fusion.3
  146.3 3.4 multiply_reduce_fusion.4
  151.5 1.5 fusion.11
  155.8 2.9 convolution_convert_fusion
  158.7 2.8 fusion.2
  161.5 75.1 %experts.1 = (bf16[16,32,1536]{2,1,0:T(8,128)(2,1)}, bf16[16,32,1536]{2,1,0:T(8,128)(2,1)}, bf16[2,2,3,384,512]{4,3,2,1,0:T(8,128)(2,1)}) custom-call(bf16[16,32,1536]{2,1,0:T(8,128)(2,1)} %bitcast.128, bf16[16,32,1536]{2,1,0:T(8,128)(2,1)} %bitcast.131, bf16[8,3,384,512]{3,2,1,0:T(8,128)(2,1)} %bitcast.139), custom_call_target="tpu_custom_call" | custom-call | flops 15000000512 | bytes 100000000 | tf_op jit(solution)/shard_map/experts/pallas_call | solution.py:888
  236.7 2.0 fusion.13
  238.8 1.3 fusion.4
  240.2 1.4 fusion.9
  242.7 1.3 fusion.39
  244.7 4.8 %convolution_convert_fusion.2 = bf16[128,1536]{1,0:T(8,128)(2,1)} fusion(bf16[128,1536]{1,0:T(8,128)(2,1)} %get-tuple-element.150, bf16[1536,1536]{1,0:T(8,128)(2,1)} %bitcast.110), kind=kOutput, calls=%fused_computation.12 | convolution fusion | flops 604176384 | bytes 5505024 | tf_op jit(solution)/shard_map/dot_general | solution.py:46
  249.5 1.9 copy.122
  251.4 7.7 %all-to-all-start.1 = ((bf16[8,128,192]{1,2,0:T(8,128)(2,1)}), bf16[8,128,192]{1,2,0:T(8,128)(2,1)}, u32[]{:S(2)}, u32[]{:S(2)}) async-start(bf16[8,128,192]{1,2,0:T(8,128)(2,1)} %bitcast.129), calls=%async_computation.1 | async-start | bytes 786432 | tf_op jit(solution)/shard_map/all_to_all | solution.py:1024
  259.1 12.8 %all-to-all-done.1 = bf16[8,128,192]{1,2,0:T(8,128)(2,1)} async-done(((bf16[8,128,192]{1,2,0:T(8,128)(2,1)}), bf16[8,128,192]{1,2,0:T(8,128)(2,1)}, u32[]{:S(2)}, u32[]{:S(2)}) %all-to-all-start.1) | async-done | bytes 393248 | tf_op jit(solution)/shard_map/all_to_all | solution.py:1024
  271.9 2.0 copy.123
  273.9 5.0 %dynamic-slice_bitcast_fusion = (bf16[2,3,384,512]{3,2,1,0:T(8,128)(2,1)}, bf16[2,3,384,512]{3,2,1,0:T(8,128)(2,1)}) fusion(bf16[2,2,3,384,512]{4,3,2,1,0:T(8,128)(2,1)} %get-tuple-element.62, s32[]{:T(128)S(6)} %select_n.84, s32[]{:T(128)S(6)} %select_n.83), kind=kLoop, calls=%fused_computation.14 | loop fusion | bytes 9437192 | tf_op jit(solution)/shard_map/jit(dynamic_index_in_dim)/squeeze | solution.py:1145
  278.9 3.2 collective-permute-start.3
  282.1 1.2 copy-done.18
  287.2 24.0 %attention_backward.1 = (bf16[1024,192]{1,0:T(8,128)(2,1)S(1)}, bf16[4096,128]{1,0:T(8,128)(2,1)S(1)}) custom-call(s32[84]{0:T(128)S(1)} %pad_add_fusion.meta, bf16[1024,192]{1,0:T(8,128)(2,1)S(1)} %copy-done.31, bf16[4096,128]{1,0:T(8,128)(2,1)S(1)} %bitcast.115, bf16[1024,192]{1,0:T(8,128)(2,1)S(1)} %copy-done.26, f32[17,1,192]{2,1,0:T(1,128)S(1)} %copy-done.34, ...), custom_call_target="tpu_custom_call" | custom-call | flops 4000000000 | bytes 10000000 | tf_op jit(solution)/shard_map/attention_backward/pallas_call | solution.py:295
  313.0 3.6 convolution_convert_fusion.1
  316.7 2.9 reshape.286
  319.6 2.2 copy.124
  321.8 1.1 copy-done.8
  323.0 1.2 copy-done.20
  324.2 26.9 %exchange_terms.1 = (bf16[4,1024,128]{2,1,0:T(8,128)(2,1)S(1)}, bf16[4,4,96,192]{3,2,1,0:T(8,128)(2,1)S(1)}) custom-call(bf16[4,1024,128]{2,1,0:T(8,128)(2,1)S(1)} %bitcast.116, bf16[4,4,96,192]{3,2,1,0:T(8,128)(2,1)S(1)} %bitcast.113), custom_call_target="tpu_custom_call" | custom-call | tf_op jit(solution)/shard_map/exchange_terms/pallas_call | solution.py:334
  351.1 3.8 add_convert_fusion
  354.9 1.2 dynamic-slice_bitcast_fusion.2
  358.0 1.8 convolution_convert_fusion.3
  359.8 1.7 copy.125
  361.8 2.0 maximum_maximum_fusion.small_ref
  363.8 1.9 reduce_sum.164
  365.7 9.6 %collective-permute-start.5 = (bf16[96,192]{1,0:T(8,128)(2,1)}, bf16[96,192]{1,0:T(8,128)(2,1)}, u32[]{:S(2)}, u32[]{:S(2)}) collective-permute-start(bf16[96,192]{1,0:T(8,128)(2,1)} %reduce_sum.164), channel_id=1, source_target_pairs={{0,0},{1,32},{2,64},{3,96},{4,16},{5,48},{6,80},{7,112},{8,4},{9,3... | collective-permute-start | bytes 110600 | tf_op jit(solution)/shard_map/ppermute | solution.py:1162
  376.3 1.2 copy-done.15
  378.6 3.2 weight_terms.1
  381.7 26.4 %return_terms.1 = (bf16[8,128,384]{2,1,0:T(8,128)(2,1)S(1)}, bf16[4,4,96,384]{3,2,1,0:T(8,128)(2,1)S(1)}) custom-call(bf16[8,128,384]{2,1,0:T(8,128)(2,1)S(1)} %get-tuple-element.66.grad_ref, bf16[4,4,96,384]{3,2,1,0:T(8,128)(2,1)S(1)} %get-tuple-element.67.term_ref), custom_call_target="tpu_custom_call" | custom-call | tf_op jit(solution)/shard_map/return_terms/pallas_call | solution.py:418
  409.2 8.8 %input_gradient.1 = bf16[128,1536]{1,0:T(8,128)(2,1)} custom-call(s32[1]{0:T(128)} %bitcast.25.stream_ref, bf16[8,128,384]{2,1,0:T(8,128)(2,1)S(1)} %get-tuple-element.68.d_qkv_ref, bf16[8,384,384]{2,1,0:T(8,128)(2,1)S(1)} %copy-done.6, bf16[8,384,384]{2,1,0:T(8,128)(2,1)} %collective-permute-done.p1, bf16[8,384,384]{2,1,0:T(8,128)(2,1)} %collective-permute-done.1.p2, ...), custom_call_target="tpu_custom_call" | custom-call | flops 1000000000 | bytes 12000000 | tf_op jit(solution)/shard_map/input_gradient/pallas_call | solution.py:1007
  418.0 1.7 convert_add_fusion
  419.7 1.3 slice_bitcast_fusion
  421.1 1.1 copy.128
  422.2 36.6 %gather_sums.1.by_row_ref = bf16[4,8,96,576]{3,2,1,0:T(8,128)(2,1)S(1)} custom-call(bf16[4,4,96,384]{3,2,1,0:T(8,128)(2,1)S(1)} %copy-done.13, bf16[96,192]{1,0:T(8,128)(2,1)} %collective-permute-done.5.piece_ref), custom_call_target="tpu_custom_call" | custom-call | tf_op jit(solution)/shard_map/gather_sums/pallas_call | solution.py:510
  458.8 3.7 assemble.1
  464.1 3.8 multiply_reduce_fusion.1
  (182 shorter events, 40.7 us)
Async XLA Ops:
  7.2 68.2 %copy-start = (s32[4,64]{1,0:T(4,128)S(1)}, s32[4,64]{1,0:T(4,128)}, u32[]{:S(2)}) copy-start(s32[4,64]{1,0:T(4,128)} %param.15) | copy-start | bytes 3076
  7.2 154.3 %all-gather.5.cloned.1.call-start = ((), (), s32[]{:S(2)}) async-start(), calls=%async_computation.2 | async-start | bytes 10616832 | tf_op jit(solution)/shard_map/all_gather | solution.py:1079
  9.6 2.1 copy-start.3
  11.7 1.7 copy-start.10
  13.4 1.1 copy-start.7
  14.4 40.0 %copy-start.5 = (bf16[8,384,384]{2,1,0:T(8,128)(2,1)}, bf16[8,384,384]{2,1,0:T(8,128)(2,1)S(1)}, u32[]{:S(2)}) copy-start(bf16[8,384,384]{2,1,0:T(8,128)(2,1)S(1)} %get-tuple-element.69.wp_ref.p0) | copy-start | bytes 7077892
  54.4 2.2 copy-start.2
  56.6 1.0 copy-start.28
  58.2 10.2 %copy-start.4 = (bf16[8,128,1536]{2,1,0:T(8,128)(2,1)}, bf16[8,128,1536]{2,1,0:T(8,128)(2,1)S(1)}, u32[]{:S(2)}) copy-start(bf16[8,128,1536]{2,1,0:T(8,128)(2,1)S(1)} %get-tuple-element.48) | copy-start | bytes 9437188
  60.8 2.4 copy-start.43
  64.5 179.7 %collective-permute-start.1 = (bf16[8,384,384]{2,1,0:T(8,128)(2,1)}, bf16[8,384,384]{2,1,0:T(8,128)(2,1)}, u32[]{:S(2)}, u32[]{:S(2)}) collective-permute-start(bf16[8,384,384]{2,1,0:T(8,128)(2,1)} %copy-done.5), channel_id=1, source_target_pairs={{0,18},{1,19},{2,16},{3,17},{4,22},{5,23},{6,20},{7,21},{8,26},{9,... | collective-permute-start | bytes 7077896 | tf_op jit(solution)/shard_map/ppermute | solution.py:1080
  69.1 2.8 copy-start.29
  79.1 0.9 copy-start.21
  101.3 1.0 copy-start.16
  102.5 1.2 copy-start.17
  103.7 1.1 copy-start.30
  104.9 28.2 %copy-start.59 = (s32[1,128,2]{1,2,0:T(2,128)S(1)}, s32[1,128,2]{1,2,0:T(2,128)}, u32[]{:S(2)}) copy-start(s32[1,128,2]{1,2,0:T(2,128)} %param.16) | copy-start | bytes 3076
  128.1 18.2 %all-to-all-start = ((bf16[8,128,192]{1,2,0:T(8,128)(2,1)}), bf16[8,128,192]{1,2,0:T(8,128)(2,1)}, u32[]{:S(2)}, u32[]{:S(2)}) async-start(bf16[8,128,192]{1,2,0:T(8,128)(2,1)} %copy.115), calls=%async_computation | async-start | bytes 786432 | tf_op jit(solution)/shard_map/all_to_all | solution.py:1024
  133.0 180.0 %all-gather.7.cloned.1.call-start = ((), (), s32[]{:S(2)}) async-start(), calls=%async_computation.3 | async-start | bytes 3538944 | tf_op jit(solution)/shard_map/all_gather | solution.py:1141
  146.3 6.7 %copy-start.48 = (s32[128,2]{0,1:T(2,128)S(1)}, s32[128,2]{0,1:T(2,128)}, u32[]{:S(2)}) copy-start(s32[128,2]{0,1:T(2,128)} %copy.117) | copy-start | bytes 3076
  149.7 0.9 copy-start.35
  154.9 0.8 copy-start.55
  155.0 0.9 copy-start.57
  161.5 75.2 %copy-start.44 = (s32[128]{0:T(128)S(1)}, s32[128]{0:T(128)}, u32[]{:S(2)}) copy-start(s32[128]{0:T(128)} %get-tuple-element.147) | copy-start | bytes 1540
  161.5 77.1 %copy-start.41 = (bf16[1,128,1536]{2,1,0:T(8,128)(2,1)S(1)}, bf16[1,128,1536]{2,1,0:T(8,128)(2,1)}, u32[]{:S(2)}) copy-start(bf16[1,128,1536]{2,1,0:T(8,128)(2,1)} %param.25) | copy-start | bytes 1179652
  236.6 2.1 copy-start.36
  236.6 2.1 copy-start.40
  236.7 2.1 copy-start.45
  236.7 2.1 copy-start.56
  236.7 2.1 copy-start.58
  238.8 1.3 copy-start.47
  238.8 1.3 copy-start.52
  238.8 1.4 copy-start.49
  238.8 2.8 copy-start.42
  238.8 2.8 copy-start.54
  240.2 2.6 copy-start.60
  244.1 29.8 %collective-permute-start = (bf16[8,384,384]{2,1,0:T(8,128)(2,1)}, bf16[8,384,384]{2,1,0:T(8,128)(2,1)}, u32[]{:S(2)}, u32[]{:S(2)}) collective-permute-start(bf16[8,384,384]{2,1,0:T(8,128)(2,1)} %copy-done.5), channel_id=1, source_target_pairs={{0,1},{1,0},{2,3},{3,2},{4,5},{5,4},{6,7},{7,6},{8,9},{9,8},{10,11... | collective-permute-start | bytes 7077896 | tf_op jit(solution)/shard_map/ppermute | solution.py:1083
  244.2 29.7 %collective-permute-start.2 = (bf16[8,384,384]{2,1,0:T(8,128)(2,1)}, bf16[8,384,384]{2,1,0:T(8,128)(2,1)}, u32[]{:S(2)}, u32[]{:S(2)}) collective-permute-start(bf16[8,384,384]{2,1,0:T(8,128)(2,1)} %collective-permute-done.1.p2), channel_id=1, source_target_pairs={{0,1},{1,0},{2,3},{3,2},{4,5},{5,4},{6,7},{7,6},{8,9},{9,8},{10,11... | collective-permute-start | bytes 7077896 | tf_op jit(solution)/shard_map/ppermute | solution.py:1085
  251.4 20.5 %all-to-all-start.1 = ((bf16[8,128,192]{1,2,0:T(8,128)(2,1)}), bf16[8,128,192]{1,2,0:T(8,128)(2,1)}, u32[]{:S(2)}, u32[]{:S(2)}) async-start(bf16[8,128,192]{1,2,0:T(8,128)(2,1)} %bitcast.129), calls=%async_computation.1 | async-start | bytes 786432 | tf_op jit(solution)/shard_map/all_to_all | solution.py:1024
  278.9 72.1 %collective-permute-start.3 = (bf16[2,3,384,512]{3,2,1,0:T(8,128)(2,1)}, bf16[2,3,384,512]{3,2,1,0:T(8,128)(2,1)}, u32[]{:S(2)}, u32[]{:S(2)}) collective-permute-start(bf16[2,3,384,512]{3,2,1,0:T(8,128)(2,1)} %get-tuple-element.152), channel_id=1, source_target_pairs={{0,2},{1,3},{2,0},{3,1},{4,6},{5,7},{6,4},{7,5},{8,10},{9,11},{10,... | collective-permute-start | bytes 7077896 | tf_op jit(solution)/shard_map/ppermute | solution.py:1144
  282.1 1.2 copy-start.18
  283.3 1.1 copy-start.26
  284.4 1.0 copy-start.27
  285.4 1.0 copy-start.31
  311.2 1.0 copy-start.19
  312.2 0.8 copy-start.23
  321.8 1.1 copy-start.8
  323.0 1.2 copy-start.20
  351.0 3.8 copy-start.14
  351.1 3.8 copy-start.22
  354.9 1.8 copy-start.37
  354.9 6.6 %copy-start.46 = (bf16[1536]{0:T(1024)(128)(2,1)S(1)}, bf16[1536]{0:T(1024)(128)(2,1)}, u32[]{:S(2)}) copy-start(bf16[1536]{0:T(1024)(128)(2,1)} %get-tuple-element.142) | copy-start | bytes 9220
  356.7 61.3 %collective-permute-start.4 = (bf16[3,384,512]{2,1,0:T(8,128)(2,1)}, bf16[3,384,512]{2,1,0:T(8,128)(2,1)}, u32[]{:S(2)}, u32[]{:S(2)}) collective-permute-start(bf16[3,384,512]{2,1,0:T(8,128)(2,1)} %dynamic-slice_bitcast_fusion.2), channel_id=1, source_target_pairs={{0,4},{4,0},{8,12},{12,8},{16,20},{20,16},{24,28},{28,24},{32,36},... | collective-permute-start | bytes 3538952 | tf_op jit(solution)/shard_map/ppermute | solution.py:1159
  365.7 56.5 %collective-permute-start.5 = (bf16[96,192]{1,0:T(8,128)(2,1)}, bf16[96,192]{1,0:T(8,128)(2,1)}, u32[]{:S(2)}, u32[]{:S(2)}) collective-permute-start(bf16[96,192]{1,0:T(8,128)(2,1)} %reduce_sum.164), channel_id=1, source_target_pairs={{0,0},{1,32},{2,64},{3,96},{4,16},{5,48},{6,80},{7,112},{8,4},{9,3... | collective-permute-start | bytes 110600 | tf_op jit(solution)/shard_map/ppermute | solution.py:1162
  375.3 1.0 copy-start.11
  376.3 1.2 copy-start.15
  377.5 1.0 copy-start.24
  378.5 30.7 %copy-start.6 = (bf16[8,384,384]{2,1,0:T(8,128)(2,1)S(1)}, bf16[8,384,384]{2,1,0:T(8,128)(2,1)}, u32[]{:S(2)}) copy-start(bf16[8,384,384]{2,1,0:T(8,128)(2,1)} %copy-done.5) | copy-start | bytes 7077892
  378.6 30.7 %copy-start.9 = (f32[128,1536]{1,0:T(8,128)S(1)}, f32[128,1536]{1,0:T(8,128)}, u32[]{:S(2)}) copy-start(f32[128,1536]{1,0:T(8,128)} %get-tuple-element.151.d_mid_ref) | copy-start | bytes 2359300
  408.1 1.1 copy-start.12
  409.2 8.8 %copy-start.38 = (bf16[2,3,384,512]{3,2,1,0:T(8,128)(2,1)S(1)}, bf16[2,3,384,512]{3,2,1,0:T(8,128)(2,1)}, u32[]{:S(2)}) copy-start(bf16[2,3,384,512]{3,2,1,0:T(8,128)(2,1)} %copy-done.37) | copy-start | bytes 7077892
  419.7 2.5 copy-start.13
  464.1 4.4 copy-start.1
  464.1 3.8 copy-start.50
  (7 other events, 4.7 us)
Sparse Core Ops, SparseCore 0:
  64.6 62.3 all-gather.4
  244.2 51.1 all-gather.6

commit v3 on v2

--- a/solution.py
+++ b/solution.py
@@ -34,13 +34,6 @@
 OTHER_SIDE = [(w, w ^ 2) for w in range(4)]
 OTHER_CORE = [(w, w ^ 1) for w in range(4)]
 NEXT_Z = [(c * 4 + w, (c ^ 4) * 4 + (w ^ 2)) for c in range(32) for w in range(4)]
-MOVES = [
-    (turned(y * 8 + r) * 4 + w, turned((r % 2) * 16 + y * 4 + w) * 4 + r // 2)
-    for r in range(8)
-    for y in range(4)
-    for w in range(4)
-]
-
 
 def dot(a, b, dims=((1,), (0,))):
     return lax.dot_general(a, b, (dims, ((), ())), preferred_element_type=F32)
@@ -311,218 +304,6 @@
     )(meta, q, kv, o, lse, d_o)
 
 
-def exchange_terms_kernel(kv_ref, out_ref, kv_to, out_to, v_kv, v_out, send, recv, local):
-    place, stream = turned(lax.axis_index("ctx")), lax.axis_index("wsh")
-    y = place // 8
-    peers = []
-    for k in range(1, 16):
-        peers.append(((y + k // 4) % 4, (stream + k % 4) % 4))
-    meet([{"ctx": turned(place % 8 + 8 * py), "wsh": pw} for py, pw in peers])
-    copies = Copies(send, recv, local)
-    for k in (8, 4, 12):
-        py, _ = peers[k - 1]
-        copies.to(kv_ref.at[py], kv_to.at[y], {"ctx": turned(place % 8 + 8 * py)})
-    for py, pw in peers:
-        copies.to(out_ref.at[py, pw], out_to.at[y, stream], {"ctx": turned(place % 8 + 8 * py), "wsh": pw})
-    copies.keep(kv_ref.at[y], v_kv, kv_to.at[y])
-    copies.keep(out_ref.at[y, stream], v_out, out_to.at[y, stream])
-    copies.move_kept()
-    copies.finish([])
-
-
-def exchange_terms(kv, out):
-    return pl.pallas_call(
-        exchange_terms_kernel,
-        out_shape=(jax.ShapeDtypeStruct(kv.shape, BF), jax.ShapeDtypeStruct(out.shape, BF)),
-        in_specs=[ANY, ANY],
-        out_specs=(ANY, ANY),
-        scratch_shapes=[
-            pltpu.VMEM(kv.shape[1:], BF),
-            pltpu.VMEM(out.shape[2:], BF),
-            pltpu.SemaphoreType.DMA((18,)),
-            pltpu.SemaphoreType.DMA((18,)),
-            pltpu.SemaphoreType.DMA((4,)),
-        ],
-        compiler_params=pltpu.CompilerParams(collective_id=3, has_side_effects=True, vmem_limit_bytes=40 * 2**20),
-        name="exchange_terms",
-    )(kv, out)
-
-
-def weight_terms_kernel(act_ref, dq_ref, kv_ref, small_ref, grad_out, term_out, grad_ref):
-    rows = dq_ref.shape[0]
-
-    @pl.when(pl.program_id(0) == 0)
-    def _():
-        total = kv_ref[0].astype(F32)
-        for i in range(1, 4):
-            total = total + kv_ref[i].astype(F32)
-        grad = jnp.concatenate([dq_ref[...], total.astype(BF)], axis=1)
-        grad_ref[...] = grad
-        padded = jnp.concatenate([grad, jnp.zeros((rows, 64), BF)], axis=1)
-        grad_out[...] = padded.reshape(grad_out.shape)
-
-    term = dot(act_ref[...].T, grad_ref[...]).astype(BF)
-    term = jnp.concatenate([term, small_ref[...]], axis=1)
-    piece = term_out.shape[2]
-    for y in range(4):
-        term_out[y, 0] = term[y * piece : (y + 1) * piece]
-
-
-def weight_terms(act, dq, kv, small):
-    rows, width = act.shape
-    shard = width // 4
-    return pl.pallas_call(
-        weight_terms_kernel,
-        out_shape=(
-            jax.ShapeDtypeStruct((8, rows // 8, 384), BF),
-            jax.ShapeDtypeStruct((4, 4, shard // 4, 384), BF),
-        ),
-        grid=(4,),
-        in_specs=[
-            pl.BlockSpec((rows, shard), lambda w: (0, w)),
-            pl.BlockSpec(dq.shape, lambda w: (0, 0)),
-            pl.BlockSpec(kv.shape, lambda w: (0, 0, 0)),
-            pl.BlockSpec((shard, 64), lambda w: (w, 0)),
-        ],
-        out_specs=(
-            pl.BlockSpec((8, rows // 8, 384), lambda w: (0, 0, 0)),
-            pl.BlockSpec((4, 1, shard // 4, 384), lambda w: (0, w, 0, 0)),
-        ),
-        scratch_shapes=[pltpu.VMEM((rows, HEAD_COLUMNS), BF)],
-        compiler_params=pltpu.CompilerParams(vmem_limit_bytes=40 * 2**20),
-        cost_estimate=pl.CostEstimate(flops=10**9, bytes_accessed=8 * 10**6, transcendentals=0),
-        name="weight_terms",
-    )(act, dq, kv, small)
-
-
-def return_terms_kernel(grad_ref, term_ref, grad_to, term_to, v_grad, v_term, send, recv, local):
-    place, stream = turned(lax.axis_index("ctx")), lax.axis_index("wsh")
-    y, r = place // 8, place % 8
-    peers = [((y + k // 4) % 4, (stream + k % 4) % 4) for k in range(1, 16)]
-    in_row = [(r + k) % 8 for k in range(1, 8)]
-    meet(
-        [{"ctx": turned(r + 8 * py), "wsh": pw} for py, pw in peers] + [{"ctx": turned(8 * y + pr)} for pr in in_row]
-    )
-    copies = Copies(send, recv, local)
-    for py, pw in peers:
-        copies.to(term_ref.at[py, pw], term_to.at[y, stream], {"ctx": turned(r + 8 * py), "wsh": pw})
-    for pr in in_row:
-        copies.to(grad_ref.at[pr], grad_to.at[r], {"ctx": turned(8 * y + pr)})
-    copies.keep(grad_ref.at[r], v_grad, grad_to.at[r])
-    copies.keep(term_ref.at[y, stream], v_term, term_to.at[y, stream])
-    copies.move_kept()
-    copies.finish([])
-
-
-def return_terms(grad, term):
-    return pl.pallas_call(
-        return_terms_kernel,
-        out_shape=(jax.ShapeDtypeStruct(grad.shape, BF), jax.ShapeDtypeStruct(term.shape, BF)),
-        in_specs=[ANY, ANY],
-        out_specs=(ANY, ANY),
-        scratch_shapes=[
-            pltpu.VMEM(grad.shape[1:], BF),
-            pltpu.VMEM(term.shape[2:], BF),
-            pltpu.SemaphoreType.DMA((22,)),
-            pltpu.SemaphoreType.DMA((22,)),
-            pltpu.SemaphoreType.DMA((4,)),
-        ],
-        compiler_params=pltpu.CompilerParams(collective_id=4, has_side_effects=True, vmem_limit_bytes=40 * 2**20),
-        name="return_terms",
-    )(grad, term)
-
-
-def gather_sums_kernel(term_ref, piece_ref, all_out, own_ref, send, recv, local):
-    place = turned(lax.axis_index("ctx"))
-    y, r = place // 8, place % 8
-    x, z = r % 4, r // 4
-    right, left = {"ctx": turned(place - x + (x + 1) % 4)}, {"ctx": turned(place - x + (x + 3) % 4)}
-    across = {"ctx": turned(place + 4 - 8 * z)}
-    up, down, beyond = ({"ctx": turned((place + 8 * k) % 32)} for k in (1, 3, 2))
-    total = term_ref[0, 0].astype(F32)
-    for i in range(1, 16):
-        total = total + term_ref[i // 4, i % 4].astype(F32)
-    own_ref[:, : total.shape[1]] = total.astype(BF)
-    own_ref[:, total.shape[1] :] = piece_ref[...]
-    meet([right, left, across, up, down, beyond])
-    copies = Copies(send, recv, local)
-    half = own_ref.shape[0] // 2
-    first, last = pl.ds(0, half), pl.ds(half, half)
-    r_z = (1 - z) * 4 + x
-    r_left, r_right = z * 4 + (x + 3) % 4, z * 4 + (x + 1) % 4
-    z_left, z_right = (1 - z) * 4 + (x + 3) % 4, (1 - z) * 4 + (x + 1) % 4
-    arrived = []
-
-    def arrive(*which):
-        for copy in which:
-            copy.wait_recv()
-            arrived.append(copy)
-
-    def on(device, *at):
-        return copies.to(all_out.at[at], all_out.at[at], device)
-
-    keep = pltpu.make_async_copy(own_ref, all_out.at[y, r], local.at[0])
-    keep.start()
-    a_right = copies.to(own_ref.at[first], all_out.at[y, r, first], right)
-    a_left = copies.to(own_ref.at[first], all_out.at[y, r, first], left)
-    a_cross = copies.to(own_ref.at[first], all_out.at[y, r, first], across)
-    b_up = copies.to(own_ref.at[last], all_out.at[y, r, last], up)
-    b_down = copies.to(own_ref.at[last], all_out.at[y, r, last], down)
-    b_beyond = copies.to(own_ref.at[last], all_out.at[y, r, last], beyond)
-    keep.wait()
-    arrive(a_cross)
-    a_z_right = on(right, y, r_z, first)
-    a_z_left = on(left, y, r_z, first)
-    arrive(a_right)
-    a_on = on(right, y, r_left, first)
-    arrive(b_up, b_down, b_beyond)
-    lower, upper, every = pl.ds(0, 2), pl.ds(2, 2), pl.ds(0, 4)
-    b_right = on(right, every, r, last)
-    b_left = on(left, every, r, last)
-    b_cross = on(across, every, r, last)
-    arrive(a_z_left, a_left)
-    a_z_on = on(left, y, z_right, first)
-    arrive(a_z_right, a_on, a_z_on)
-    low_r, high_r = pl.ds(0, 4), pl.ds(4, 4)
-    c_up = [on(up, y, low_r, first), on(up, y, high_r, first)]
-    c_down = [on(down, y, high_r, first), on(down, y, low_r, first)]
-    arrive(b_right)
-    on(right, lower, r_left, last)
-    arrive(b_left)
-    on(left, upper, r_right, last)
-    arrive(b_cross)
-    b_z_right = on(right, every, r_z, last)
-    b_z_left = on(left, every, r_z, last)
-    arrive(c_up[0])
-    on(up, (y + 3) % 4, low_r, first)
-    arrive(c_down[0])
-    on(down, (y + 1) % 4, high_r, first)
-    arrive(b_z_right)
-    on(right, lower, z_left, last)
-    arrive(b_z_left)
-    on(left, upper, z_right, last)
-    copies.finish(arrived)
-
-
-def gather_sums(term, piece):
-    rows, columns = piece.shape[0], term.shape[3] + piece.shape[1]
-    vmem = pl.BlockSpec(memory_space=pltpu.VMEM)
-    return pl.pallas_call(
-        gather_sums_kernel,
-        out_shape=jax.ShapeDtypeStruct((4, 8, rows, columns), BF),
-        in_specs=[vmem, vmem],
-        out_specs=ANY,
-        scratch_shapes=[
-            pltpu.VMEM((rows, columns), BF),
-            pltpu.SemaphoreType.DMA((25,)),
-            pltpu.SemaphoreType.DMA((25,)),
-            pltpu.SemaphoreType.DMA((1,)),
-        ],
-        compiler_params=pltpu.CompilerParams(collective_id=5, has_side_effects=True, vmem_limit_bytes=40 * 2**20),
-        name="gather_sums",
-    )(term, piece)
-
-
 def assemble_kernel(by_row_ref, by_head_ref, qkv_ref, out_ref, rest_ref):
     heads = [by_row_ref[0, h].astype(F32) for h in range(8)]
     ends = (0, WIDTH, WIDTH + HEAD_SIZE, HEAD_COLUMNS)
@@ -532,7 +313,7 @@
         tail = tail + t
     rest_ref[...] = tail[:, HEAD_COLUMNS:384]
     for parity in range(2):
-        parts = [by_head_ref[parity, y, 0, :, 384:].astype(F32).T for y in range(4)]
+        parts = [by_head_ref[y, 0, 1 - parity, :, 384:].astype(F32).T for y in range(4)]
         out_ref[parity * WIDTH : (parity + 1) * WIDTH, :] = jnp.concatenate(parts, axis=1)
 
 
@@ -549,7 +330,7 @@
         grid=(4,),
         in_specs=[
             pl.BlockSpec((1, 8, piece, columns), lambda i: (i, 0, 0, 0)),
-            pl.BlockSpec((2, 4, 1, piece, columns), lambda i: (0, 0, i, 0, 0)),
+            pl.BlockSpec((4, 1, 2, piece, columns), lambda i: (0, i, 0, 0, 0)),
         ],
         out_specs=(
             pl.BlockSpec((piece, 8 * HEAD_COLUMNS), lambda i: (i, 0)),
@@ -558,7 +339,7 @@
         ),
         compiler_params=pltpu.CompilerParams(vmem_limit_bytes=40 * 2**20),
         name="assemble",
-    )(gathered, gathered.reshape(2, 4, 4, piece, columns))
+    )(gathered, gathered.reshape(4, 4, 2, piece, columns))
 
 
 MESH = pl.DeviceIdType.MESH
@@ -749,7 +530,7 @@
 
 
 def experts_kernel(
-    rows_ref, grads_ref, w_ref, back_out, returned_out, terms_out,
+    rows_ref, grads_ref, w_ref, back_out, returned_out, half_send, half_keep, side_send, side_keep,
     w_v, x_v, g_v, turned_x, turned_g, out_v, d_in_v, acc_v, gate_v, up_v, hidden_v, d_gate_v, d_up_v, sent_v, got_v,
     send, recv, local,
 ):
@@ -853,25 +634,28 @@
             dot(turned_g[at, :], hidden_v[k]),
         )
 
+    half, side = index % 2, stream // 2
     crossing = []
-    for z in range(2):
-
-        def other_term(k, carry, z=z):
+    for dz in (1, 0):
+        z = side + dz - 2 * side * dz
+
+        def other_term(k, carry, z=z, dz=dz):
             for m, term in enumerate(terms(k, z, 1 - core)):
-                sent_v[z, k, m] = term.astype(BF)
+                sent_v[dz, k, m] = term.astype(BF)
             return carry
 
         lax.fori_loop(0, 2, other_term, 0)
-        crossing.append(copies.to(sent_v.at[z], got_v.at[z], other))
-    for z in range(2):
-
-        def own_term(k, carry, z=z):
+        crossing.append(copies.to(sent_v.at[dz], got_v.at[dz], other))
+    halfway = quarter // 2
+    for dz, copy in zip((1, 0), crossing):
+        z = side + dz - 2 * side * dz
+        arrive([copy])
+        for dk in (1, 0):
+            k = half + dk - 2 * half * dk
             for m, term in enumerate(terms(k, z, core)):
-                terms_out[z, k, m] = (term + got_v[z, k, m].astype(F32)).astype(BF)
-            return carry
-
-        arrive([crossing[z]])
-        lax.fori_loop(0, 2, own_term, 0)
+                total = (term + got_v[dz, k, m].astype(F32)).astype(BF)
+                (half_send if dk else half_keep)[z, m] = total[:halfway]
+                (side_send if dz else side_keep)[k, m] = total[halfway:]
     copies.finish(arrived)
     own_back.wait()
     own_returned.wait()
@@ -890,10 +674,10 @@
         out_shape=(
             jax.ShapeDtypeStruct(send_rows.shape, BF),
             jax.ShapeDtypeStruct(send_rows.shape, BF),
-            jax.ShapeDtypeStruct(terms, BF),
-        ),
+        )
+        + (jax.ShapeDtypeStruct((2, 3, width // 8, half), BF),) * 4,
         in_specs=[ANY, ANY, ANY],
-        out_specs=(ANY, ANY, pl.BlockSpec(memory_space=pltpu.VMEM)),
+        out_specs=(ANY, ANY) + (pl.BlockSpec(memory_space=pltpu.VMEM),) * 4,
         scratch_shapes=[
             vmem((2, 3, width, half), BF),
             slots,
@@ -964,60 +748,236 @@
     )(w_qkv, w_router, w_out)
 
 
-def input_gradient_kernel(stream_ref, d_qkv_ref, p0, p1, p2, p3, x_ref, d_mid_ref, gain_ref, out_ref, acc_ref):
-    step = pl.program_id(0)
-    stream = stream_ref[0]
-
-    @pl.when(step == 0)
-    def _():
-        acc_ref[...] = jnp.zeros_like(acc_ref)
-
-    grad = d_qkv_ref[0, :, :HEAD_COLUMNS]
-    for j, piece in enumerate((p0, p1, p2, p3)):
-        acc_ref[stream ^ j] += dot(grad, piece[0, :, :HEAD_COLUMNS], NT)
-
-    @pl.when(step == pl.num_programs(0) - 1)
-    def _():
-        x = x_ref[...].astype(F32)
-        scale = rms_scale(x)
-        quarter = acc_ref.shape[2]
-        inner = 0.0
-        for q in range(4):
-            at = slice(q * quarter, (q + 1) * quarter)
-            inner += jnp.sum(acc_ref[q] * gain_ref[:, at] * x[:, at], axis=-1, keepdims=True)
-        inner = inner * (1.0 / x.shape[1])
-        for q in range(4):
-            at = slice(q * quarter, (q + 1) * quarter)
-            out_ref[:, at] = (
-                d_mid_ref[:, at] + scale * (acc_ref[q] * gain_ref[:, at]) - x[:, at] * scale**3 * inner
-            ).astype(BF)
-
-
-def input_gradient(stream, d_qkv, pieces, x, d_middle, gain):
-    heads, rows, _ = d_qkv.shape
-    width = x.shape[1]
-
-    def whole(a):
-        return pl.BlockSpec(a.shape, lambda h, s: (0, 0))
-
-    def by_head(a):
-        return pl.BlockSpec((1,) + a.shape[1:], lambda h, s: (h, 0, 0))
-
-    gain = gain.reshape(1, width)
+def finish_kernel(
+    dq_ref, kv_ref, act_ref, small_ref, out_ref, p0, p1, p2, p3, x_ref, d_mid_ref, gain_ref, d_tokens_ref, all_out,
+    kv_v, out_v, grad_v, grad_to, term_v, term_to, act_t, own_v, w_v, acc_v,
+    send, recv, out_send, out_recv, local,
+):
+    place, stream = turned(lax.axis_index("ctx")), lax.axis_index("wsh")
+    y, r = place // 8, place % 8
+    x, z = r % 4, r // 4
+
+    def at_place(p):
+        return {"ctx": turned(p)}
+
+    right, left = at_place(place - x + (x + 1) % 4), at_place(place - x + (x + 3) % 4)
+    across = at_place(place + 4 - 8 * z)
+    up, down, beyond = (at_place((place + 8 * k) % 32) for k in (1, 3, 2))
+    others = [((y + k // 4) % 4, (stream + k % 4) % 4) for k in range(1, 16)]
+    in_row = [(r + k) % 8 for k in range(1, 8)]
+    served = 2 * stream + 1 - r % 2
+
+    def out_target(p):
+        return {"ctx": turned(p // 4 * 8 + 2 * (p % 4) + 1 - r % 2), "wsh": r // 2}
+
+    barrier = pltpu.get_barrier_semaphore()
+    partners = [{"ctx": turned(r + 8 * py), "wsh": pw} for py, pw in others]
+    partners += [at_place(8 * y + pr) for pr in in_row]
+    sources = [{"ctx": turned(i // 4 * 8 + served), "wsh": i % 4} for i in range(16)]
+    for device in partners + sources:
+        pl.semaphore_signal(barrier, inc=1, device_id=device, device_id_type=MESH)
+    pl.semaphore_wait(barrier, len(partners) + 16)
+
+    copies = Copies(send, recv, local)
+    rows, width = act_ref.shape
+    shard, piece = width // 4, own_v.shape[0]
+    arrived = []
+
+    def arrive(*which):
+        for copy in which:
+            copy.wait_recv()
+            arrived.append(copy)
+
+    own = []
+
+    def here(source, target):
+        copy = pltpu.make_async_copy(source, target, local.at[len(own)])
+        copy.start()
+        own.append(copy)
+        return copy
+
+    kv_came = [
+        copies.to(kv_ref.at[(y + k) % 4], kv_v.at[y], at_place((place + 8 * k) % 32)) for k in (2, 1, 3)
+    ]
+    own_kv = here(kv_ref.at[y], kv_v.at[y])
+    out_copies = []
+    for p in range(16):
+        copy = pltpu.make_async_remote_copy(
+            out_ref.at[pl.ds(p % 4 * shard + p // 4 * piece, piece)],
+            out_v.at[y * 4 + stream],
+            out_send.at[p],
+            out_recv.at[y * 4 + stream],
+            device_id=out_target(p),
+            device_id_type=MESH,
+        )
+        copy.start()
+        out_copies.append(copy)
+    weights = [here(p, w_v.at[j]) for j, p in enumerate((p0, p1, p2, p3))]
+    dq = dq_ref[...]
+    for q in range(4):
+        act_t[q * shard : (q + 1) * shard, :] = act_ref[:, q * shard : (q + 1) * shard].T
+    for q in range(4):
+        term = dot(act_t[q * shard : (q + 1) * shard, :], dq).astype(BF)
+        for i in range(4):
+            term_v[i, q, :, :WIDTH] = term[i * piece : (i + 1) * piece]
+            at = q * shard + i * piece
+            term_v[i, q, :, HEAD_COLUMNS:] = small_ref[at : at + piece, :]
+    own_kv.wait()
+    arrive(*kv_came)
+    total = kv_v[0].astype(F32)
+    for i in range(1, 4):
+        total = total + kv_v[i].astype(F32)
+    kv = total.astype(BF)
+    grad_v[...] = jnp.concatenate([dq, kv, jnp.zeros((rows, 64), BF)], axis=1).reshape(grad_v.shape)
+    grads = [copies.to(grad_v.at[pr], grad_to.at[r], at_place(8 * y + pr)) for pr in in_row]
+    own_grad = here(grad_v.at[r], grad_to.at[r])
+    terms = []
+    for dw in (2, 3, 1, 0):
+        pw = (stream + dw) % 4
+        part = act_t[pl.ds(pl.multiple_of(pw * shard, shard), shard), :]
+        term = dot(part, kv).astype(BF)
+        for i in range(4):
+            term_v[i, pw, :, WIDTH:HEAD_COLUMNS] = term[i * piece : (i + 1) * piece]
+        for dy in (2, 1, 3, 0):
+            py = (y + dy) % 4
+            if dw or dy:
+                device = {"ctx": turned(r + 8 * py), "wsh": pw}
+                terms.append(copies.to(term_v.at[py, pw], term_to.at[y, stream], device))
+    own_term = here(term_v.at[y, stream], term_to.at[y, stream])
+    for i, copy in enumerate(out_copies):
+        pltpu.make_async_remote_copy(
+            out_v.at[i], out_v.at[i], out_send.at[i], out_recv.at[i], device_id=across, device_id_type=MESH
+        ).wait_recv()
+        copy.wait_send()
+    total = out_v[0].astype(F32)
+    for i in range(1, 16):
+        total = total + out_v[i].astype(F32)
+    own_v[:, 384:] = total.astype(BF)
+    own_term.wait()
+    arrive(*terms)
+    total = term_to[0, 0].astype(F32)
+    for i in range(1, 16):
+        total = total + term_to[i // 4, i % 4].astype(F32)
+    own_v[:, :384] = total.astype(BF)
+
+    half = piece // 2
+    first, last = pl.ds(0, half), pl.ds(half, half)
+    r_z = (1 - z) * 4 + x
+    r_left, r_right = z * 4 + (x + 3) % 4, z * 4 + (x + 1) % 4
+    z_left, z_right = (1 - z) * 4 + (x + 3) % 4, (1 - z) * 4 + (x + 1) % 4
+
+    def on(device, *at):
+        return copies.to(all_out.at[at], all_out.at[at], device)
+
+    a_cross = copies.to(own_v.at[first], all_out.at[y, r, first], across)
+    a_right = copies.to(own_v.at[first], all_out.at[y, r, first], right)
+    a_left = copies.to(own_v.at[first], all_out.at[y, r, first], left)
+    b_up = copies.to(own_v.at[last], all_out.at[y, r, last], up)
+    b_down = copies.to(own_v.at[last], all_out.at[y, r, last], down)
+    b_beyond = copies.to(own_v.at[last], all_out.at[y, r, last], beyond)
+    keep = here(own_v, all_out.at[y, r])
+
+    for copy in weights:
+        copy.wait()
+    own_grad.wait()
+    arrive(*grads)
+    acc_v[...] = jnp.zeros_like(acc_v)
+    shards = (stream, stream + 1 - 2 * (stream % 2), (stream + 2) % 4, 3 - stream)
+
+    def heads(start, count):
+        def one(h, carry):
+            grad = grad_to[h][:, :HEAD_COLUMNS]
+            for j in range(4):
+                acc_v[shards[j]] += dot(grad, w_v[j, h][:, :HEAD_COLUMNS], NT)
+            return carry
+
+        lax.fori_loop(start, start + count, one, 0)
+
+    heads(0, 2)
+    keep.wait()
+    arrive(a_cross)
+    a_z_right = on(right, y, r_z, first)
+    a_z_left = on(left, y, r_z, first)
+    arrive(a_right)
+    a_on = on(right, y, r_left, first)
+    arrive(b_up, b_down, b_beyond)
+    lower, upper, every = pl.ds(0, 2), pl.ds(2, 2), pl.ds(0, 4)
+    b_right = on(right, every, r, last)
+    b_left = on(left, every, r, last)
+    b_cross = on(across, every, r, last)
+    heads(2, 2)
+    arrive(a_z_left, a_left)
+    a_z_on = on(left, y, z_right, first)
+    arrive(a_z_right, a_on, a_z_on)
+    low_r, high_r = pl.ds(0, 4), pl.ds(4, 4)
+    c_up = [on(up, y, low_r, first), on(up, y, high_r, first)]
+    c_down = [on(down, y, high_r, first), on(down, y, low_r, first)]
+    heads(4, 2)
+    arrive(b_right)
+    on(right, lower, r_left, last)
+    arrive(b_left)
+    on(left, upper, r_right, last)
+    arrive(b_cross)
+    b_z_right = on(right, every, r_z, last)
+    b_z_left = on(left, every, r_z, last)
+    arrive(c_up[0])
+    on(up, (y + 3) % 4, low_r, first)
+    arrive(c_down[0])
+    on(down, (y + 1) % 4, high_r, first)
+    heads(6, 2)
+    arrive(b_z_right)
+    on(right, lower, z_left, last)
+    arrive(b_z_left)
+    on(left, upper, z_right, last)
+    values = x_ref[...].astype(F32)
+    scale = rms_scale(values)
+    inner = 0.0
+    for q in range(4):
+        at = slice(q * shard, (q + 1) * shard)
+        inner += jnp.sum(acc_v[q] * gain_ref[:, at] * values[:, at], axis=-1, keepdims=True)
+    inner = inner * (1.0 / width)
+    for q in range(4):
+        at = slice(q * shard, (q + 1) * shard)
+        d_tokens_ref[:, at] = (
+            d_mid_ref[:, at] + scale * (acc_v[q] * gain_ref[:, at]) - values[:, at] * scale**3 * inner
+        ).astype(BF)
+    copies.finish(arrived)
+
+
+def finish(dq, kv, act, small, out_term, pieces, x, d_middle, gain):
+    rows, width = act.shape
+    piece = width // 16
+    vmem = pl.BlockSpec(memory_space=pltpu.VMEM)
+    scratch = pltpu.VMEM
     return pl.pallas_call(
-        input_gradient_kernel,
-        out_shape=jax.ShapeDtypeStruct(x.shape, BF),
-        grid_spec=pltpu.PrefetchScalarGridSpec(
-            num_scalar_prefetch=1,
-            grid=(heads,),
-            in_specs=[by_head(d_qkv)] + [by_head(p) for p in pieces] + [whole(x), whole(d_middle), whole(gain)],
-            out_specs=whole(x),
-            scratch_shapes=[pltpu.VMEM((4, rows, width // 4), F32)],
+        finish_kernel,
+        out_shape=(
+            jax.ShapeDtypeStruct(x.shape, BF),
+            jax.ShapeDtypeStruct((4, 8, piece, 384 + WIDTH), BF),
         ),
-        compiler_params=pltpu.CompilerParams(vmem_limit_bytes=40 * 2**20),
-        cost_estimate=pl.CostEstimate(flops=10**9, bytes_accessed=12 * 10**6, transcendentals=0),
-        name="input_gradient",
-    )(stream.reshape(1).astype(jnp.int32), d_qkv, *pieces, x, d_middle, gain)
+        in_specs=[vmem, ANY, vmem, vmem, ANY] + [ANY] * 4 + [vmem] * 3,
+        out_specs=(vmem, ANY),
+        scratch_shapes=[
+            scratch(kv.shape, BF),
+            scratch((16, piece, WIDTH), BF),
+            scratch((8, rows // 8, 384), BF),
+            scratch((8, rows // 8, 384), BF),
+            scratch((4, 4, piece, 384), BF),
+            scratch((4, 4, piece, 384), BF),
+            scratch((width, rows), BF),
+            scratch((piece, 384 + WIDTH), BF),
+            scratch((4,) + pieces[0].shape, BF),
+            scratch((4, rows // 8, width // 4), F32),
+            pltpu.SemaphoreType.DMA((50,)),
+            pltpu.SemaphoreType.DMA((50,)),
+            pltpu.SemaphoreType.DMA((16,)),
+            pltpu.SemaphoreType.DMA((16,)),
+            pltpu.SemaphoreType.DMA((8,)),
+        ],
+        compiler_params=pltpu.CompilerParams(collective_id=3, has_side_effects=True, vmem_limit_bytes=52 * 2**20),
+        cost_estimate=pl.CostEstimate(flops=3 * 10**9, bytes_accessed=10**8, transcendentals=0),
+        name="finish",
+    )(dq, kv, act, small, out_term, *pieces, x, d_middle, gain.reshape(1, width))
 
 
 def swap(x, groups, axis="ctx"):
@@ -1116,7 +1076,7 @@
 
     send_rows = dot(hot_any, act_moe, TN).astype(BF).reshape(experts_count, capacity, width)
     send_grads = (slot_gate[:, None] * dot(hot_any, cotangent[0], TN)).astype(BF)
-    back_rows, returned, expert_terms = experts(send_rows, send_grads.reshape(experts_count, capacity, width), expert_all)
+    back_rows, returned, *expert_terms = experts(send_rows, send_grads.reshape(experts_count, capacity, width), expert_all)
     back_rows, returned = (r.reshape(-1, width) for r in (back_rows, returned))
 
     both = [dot(hot_low[j], back_rows) for j in range(TOP)]
@@ -1140,34 +1100,38 @@
     head_d_attn = swap(d_attn.reshape(rows, 8, WIDTH).transpose(1, 0, 2), ROW).reshape(8 * rows, WIDTH)
     group_branch = lax.all_gather(d_branch, "ctx", axis_index_groups=ROW).reshape(8 * rows, width)
     head_d_attn, expert_terms, qkv_pieces = lax.optimization_barrier((head_d_attn, expert_terms, qkv_pieces))
-    side = stream // 2
-    recv_terms = lax.ppermute(
-        lax.dynamic_index_in_dim(expert_terms, 1 - side, 0, keepdims=False), "wsh", OTHER_SIDE
-    )
-    keep_terms = lax.dynamic_index_in_dim(expert_terms, side, 0, keepdims=False)
-    pending_terms = (keep_terms, recv_terms)
+    half_send, half_keep, side_send, side_keep = expert_terms
+    by_half = (half_keep, lax.ppermute(half_send, "ctx", OTHER_HALF))
+    by_side = (side_keep, lax.ppermute(side_send, "wsh", OTHER_SIDE))
     d_q, d_kv = run_backward(meta, head_q, kv_all, head_attn, lse, head_d_attn)
-    out_term = dot(group_branch, head_attn, TN).astype(BF).reshape(4, 4, shard // 4, WIDTH).transpose(1, 0, 2, 3)
     small_term = jnp.concatenate(
         [d_router_local.astype(BF), d_gain_second.astype(BF)[:, None], jnp.zeros((width, 47), BF)], axis=1
     )
-    kv_terms, out_terms = exchange_terms(d_kv.reshape(4, 8 * rows, 2 * HEAD_SIZE), out_term)
-    (keep_terms, recv_terms), kv_terms = lax.optimization_barrier((pending_terms, kv_terms))
-    expert_terms = (keep_terms.astype(F32) + recv_terms.astype(F32)).astype(BF)
-    half = index % 2
-    keep_terms = lax.dynamic_index_in_dim(expert_terms, half, 0, keepdims=False)
-    recv_terms = lax.ppermute(
-        lax.dynamic_index_in_dim(expert_terms, 1 - half, 0, keepdims=False), "ctx", OTHER_HALF
+    out_term = dot(group_branch, head_attn, TN).astype(BF)
+    by_half, by_side, d_q = lax.optimization_barrier((by_half, by_side, d_q))
+
+    def part_sum(terms, which):
+        return sum(lax.dynamic_index_in_dim(t, which, 0, keepdims=False).astype(F32) for t in terms)
+
+    half, side = index % 2, stream // 2
+    half_got = lax.ppermute(part_sum(by_half, 1 - side).astype(BF), "wsh", OTHER_SIDE)
+    side_got = lax.ppermute(part_sum(by_side, 1 - half).astype(BF), "ctx", OTHER_HALF)
+    d_tokens, gathered = finish(
+        d_q,
+        d_kv.reshape(4, 8 * rows, 2 * HEAD_SIZE),
+        group_act,
+        small_term,
+        out_term,
+        qkv_pieces,
+        tokens[0],
+        d_middle,
+        gain_first,
     )
-    out_piece = lax.ppermute(
-        jnp.sum(out_terms.astype(F32), axis=(0, 1)).astype(BF), ("ctx", "wsh"), MOVES
+    gathered, half_got, side_got = lax.optimization_barrier((gathered, half_got, side_got))
+    expert_own = jnp.concatenate(
+        [part_sum(by_half, side) + half_got.astype(F32), part_sum(by_side, half) + side_got.astype(F32)], axis=1
     )
-    head_d_qkv, term = weight_terms(group_act, d_q, kv_terms, small_term)
-    d_qkv, terms = return_terms(head_d_qkv, term)
-    d_tokens = input_gradient(stream, d_qkv, qkv_pieces, tokens[0], d_middle, gain_first)
-    terms, recv_terms = lax.optimization_barrier((terms, recv_terms))
-    expert_own = keep_terms.astype(F32) + recv_terms.astype(F32)
-    d_w_qkv, d_w_out, rest = assemble(gather_sums(terms, out_piece))
+    d_w_qkv, d_w_out, rest = assemble(gathered)
     d_gain_first = jnp.sum(d_w_qkv * w_qkv.astype(BF).astype(F32), axis=1) / gain_attn.astype(BF).astype(F32)
     return (
         output_rows[None],

time: 482 us -> 421 us (0.87)
  local copies, waits for them, and re-layouts: 70.7 us -> 28.1 us
  blocking collectives: 0 us -> 21.6 us
  starting transfers between devices: 27.8 us -> 10.5 us
  Pallas kernels: 287 us -> 277 us
  other arithmetic: 34.5 us -> 24.7 us
  matrix products: 28.4 us -> 23.1 us
    all_to_all x0 -> x1, blocking collectives: none -> 21.6 us  [swap(): return lax.all_to_all(x, axis, 0, 0, axis_index_groups=groups, tiled=True)]
    unnamed x126 -> x75, local copies, waits for them, and re-layouts: 32.3 us -> 14.7 us
    ppermute x3 -> x4, starting transfers between devices: 12.7 us -> 2.34 us  [the longest x1 1.65 us: body(): lax.ppermute(part_sum(by_side, 1 - half).astype(BF), 'ctx', OTHER_HALF)]
    pallas_call x1, Pallas kernels: 75.1 us -> 83.2 us  [experts(): pl.pallas_call(experts_kernel, out_shape=(jax.ShapeDtypeStruct(send_rows....]
    all_to_all x2 -> x1, waiting for transfers between devices: 12.8 us -> 4.93 us  [swap(): return lax.all_to_all(x, axis, 0, 0, axis_index_groups=groups, tiled=True)]
    all_to_all x2 -> x1, starting transfers between devices: 12.6 us -> 4.93 us  [swap(): return lax.all_to_all(x, axis, 0, 0, axis_index_groups=groups, tiled=True)]
    ppermute x3 -> x4, waiting for transfers between devices: 0.01 us -> 7.22 us  [the longest x1 5.62 us: body(): by_half = (half_keep, lax.ppermute(half_send, 'ctx', OTHER_HALF))]
    squeeze x2 -> x0, local copies, waits for them, and re-layouts: 6.16 us -> none  [the longest x1 4.97 us: body(): lax.dynamic_index_in_dim(expert_terms, 1 - side, 0, keepdims=False)]
  transfers between devices with their start and end apart: 10 -> 10, of which waited for: 1 -> 3; matrix products, arithmetic and copies ran while one was open for 18% -> 11% of each run, Pallas kernels for 43% -> 56%
where the time goes in v3:
time: 421 us; the launch traced here: 413 us
  Pallas kernels  277 us (66%)
  local copies, waits for them, and re-layouts  28.1 us (7%)
  other arithmetic  24.7 us (6%)
  matrix products  23.1 us (5%)
  blocking collectives  21.6 us (5%)
  between operations  15.1 us (4%)
  waiting for transfers between devices  12.2 us (3%)
  starting transfers between devices  10.5 us (2%)
    pallas_call x1, Pallas kernels, finish(): pl.pallas_call(finish_kernel, out_shape=(jax.ShapeDtypeStruct(x.shape, BF...  96.4 us
    pallas_call x1, Pallas kernels, experts(): pl.pallas_call(experts_kernel, out_shape=(jax.ShapeDtypeStruct(send_rows....  83.2 us
    pallas_call x1, Pallas kernels, gather_rows(): pl.pallas_call(gather_rows_kernel, out_shape=(jax.ShapeDtypeStruct((8,) +...  39.9 us
    dot_general x12, matrix products, dot(): return lax.dot_general(a, b, (dims, ((), ())), preferred_element_type=F32)  23.1 us
    all_to_all x1, blocking collectives, swap(): return lax.all_to_all(x, axis, 0, 0, axis_index_groups=groups, tiled=True)  21.6 us
    pallas_call x1, Pallas kernels, gather_keys(): pl.pallas_call(gather_keys_kernel, out_shape=jax.ShapeDtypeStruct((4,) +...  20.2 us
    pallas_call x1, Pallas kernels, run_backward(): local_call(attention_backward, (jax.ShapeDtypeStruct((rows, WIDTH), BF),...  18.2 us
    pallas_call x1, Pallas kernels, run_forward(): local_call(attention_forward, (jax.ShapeDtypeStruct((rows, WIDTH), BF), j...  14.9 us
  transfers between devices with their start and end apart: 10, of which 3 were waited for; matrix products, arithmetic and copies ran while one was open for 11% of the time, Pallas kernels for 56%

profile of v3, /device:TPU:8, one launch (start us, length us, event | category | flops | bytes accessed | tf_op | source)
XLA Modules:
  0.0 412.8 jit_solution(16599212214575295854)
XLA Ops:
  7.2 0.9 copy.113.router_ref
  8.1 0.7 convert_element_type.185
  8.8 0.7 convert_element_type.186
  9.6 2.1 copy-done.3
  11.7 1.7 copy-done.8
  13.4 1.0 prepare.1
  14.5 39.9 %gather_rows.1 = (bf16[8,128,1536]{2,1,0:T(8,128)(2,1)S(1)}, bf16[4,384,384]{2,1,0:T(8,128)(2,1)S(1)}, bf16[4,16,384]{2,1,0:T(8,128)(2,1)S(1)}, bf16[4,384,1536]{2,1,0:T(8,128)(2,1)S(1)}) custom-call(bf16[128,1536]{1,0:T(8,128)(2,1)S(1)} %bitcast.106, bf16[8,384,384]{2,1,0:T(8,128)(2,1)S(1)} %get-tuple-element.76.wp_ref.p0, ...), custom_call_target="tpu_custom_call" | custom-call | tf_op jit(solution)/shard_map/gather_rows/pallas_call | solution.py:463
  54.4 2.2 copy-done.2
  56.6 1.0 copy-done.13
  57.6 0.6 copy-done.18
  58.3 2.0 copy.121
  60.3 1.3 convert_element_type.202
  61.8 1.1 pad_maximum_fusion
  62.9 1.8 collective-permute-start.1
  64.7 1.4 convert_reduce_fusion
  66.2 0.7 reshape.293
  66.9 0.7 multiply_reduce_fusion
  67.6 0.8 fusion.1.act_ref
  68.8 1.8 convolution_convert_fusion.4
  71.1 0.7 fusion.42
  72.0 20.2 %gather_keys.1 = bf16[4,1024,128]{2,1,0:T(8,128)(2,1)S(1)} custom-call(bf16[1024,128]{1,0:T(8,128)(2,1)S(1)} %slice.72.kv_ref), custom_call_target="tpu_custom_call" | custom-call | tf_op jit(solution)/shard_map/gather_keys/pallas_call | solution.py:513
  92.5 14.9 %attention_forward.1 = (bf16[1024,192]{1,0:T(8,128)(2,1)S(1)}, f32[17,1,192]{2,1,0:T(1,128)S(1)}) custom-call(s32[84]{0:T(128)S(1)} %pad_add_fusion.meta, bf16[1024,192]{1,0:T(8,128)(2,1)S(1)} %slice.71.q_ref, bf16[4096,128]{1,0:T(8,128)(2,1)S(1)} %bitcast.109), custom_call_target="tpu_custom_call" | custom-call | flops 4000000000 | bytes 10000000 | tf_op jit(solution)/shard_map/attention_forward/pallas_call | solution.py:265
  107.4 1.0 copy.115
  108.4 4.9 %all-to-all-start = ((bf16[8,128,192]{1,2,0:T(8,128)(2,1)}), bf16[8,128,192]{1,2,0:T(8,128)(2,1)S(1)}, u32[]{:S(2)}, u32[]{:S(2)}) async-start(bf16[8,128,192]{1,2,0:T(8,128)(2,1)} %copy.115), calls=%async_computation | async-start | bytes 786432 | tf_op jit(solution)/shard_map/all_to_all | solution.py:984
  114.0 0.6 reduce-window.20
  115.2 4.9 %all-to-all-done = bf16[8,128,192]{1,2,0:T(8,128)(2,1)S(1)} async-done(((bf16[8,128,192]{1,2,0:T(8,128)(2,1)}), bf16[8,128,192]{1,2,0:T(8,128)(2,1)S(1)}, u32[]{:S(2)}, u32[]{:S(2)}) %all-to-all-start) | async-done | bytes 393248 | tf_op jit(solution)/shard_map/all_to_all | solution.py:984
  120.2 3.3 multiply_reduce_fusion.4
  123.7 0.5 fusion.16
  124.5 1.8 convolution_convert_fusion
  126.3 1.8 fusion.2
  128.2 83.2 %experts.1 = (bf16[16,32,1536]{2,1,0:T(8,128)(2,1)}, bf16[16,32,1536]{2,1,0:T(8,128)(2,1)}, bf16[2,3,192,512]{3,2,1,0:T(8,128)(2,1)}, bf16[2,3,192,512]{3,2,1,0:...) custom-call(bf16[16,32,1536]{2,1,0:T(8,128)(2,1)} %bitcast.123, ...), custom_call_target="tpu_custom_call" | custom-call | flops 15000000512 | bytes 100000000 | tf_op jit(solution)/shard_map/experts/pallas_call | solution.py:672
  211.4 2.0 fusion.18
  213.4 1.3 fusion.4
  215.2 0.6 multiply_reduce_fusion.2
  215.8 2.6 fusion.44
  218.4 1.2 collective-permute-start
  219.7 4.8 %convolution_convert_fusion.2 = bf16[128,1536]{1,0:T(8,128)(2,1)} fusion(bf16[128,1536]{1,0:T(8,128)(2,1)} %get-tuple-element.160, bf16[1536,1536]{1,0:T(8,128)(2,1)} %bitcast.104), kind=kOutput, calls=%fused_computation.15 | convolution fusion | flops 604176384 | bytes 5505024 | tf_op jit(solution)/shard_map/dot_general | solution.py:39
  224.5 1.9 copy.122
  226.5 21.6 %all_to_all.10 = bf16[8,128,192]{1,2,0:T(8,128)(2,1)} all-to-all(bf16[8,128,192]{1,2,0:T(8,128)(2,1)} %bitcast.126), channel_id=1, replica_groups={{0,32,64,96,16,48,80,112},{4,36,68,100,20,52,84,116},{8,40,72,104,24,56..., dimensions={0} | all-to-all | bytes 786432 | tf_op jit(solution)/shard_map/all_to_all | solution.py:984
  248.0 2.0 copy.123
  250.2 0.9 slice_convert_fusion
  251.2 1.2 convolution_convert_fusion.3
  253.1 0.5 copy-done.12
  253.8 18.2 %attention_backward.1 = (bf16[1024,192]{1,0:T(8,128)(2,1)S(1)}, bf16[4096,128]{1,0:T(8,128)(2,1)S(1)}) custom-call(s32[84]{0:T(128)S(1)} %pad_add_fusion.meta, bf16[1024,192]{1,0:T(8,128)(2,1)S(1)} %copy-done.17, bf16[4096,128]{1,0:T(8,128)(2,1)S(1)} %bitcast.110, bf16[1024,192]{1,0:T(8,128)(2,1)S(1)} %get-tuple-element.56.o_ref, ...), custom_call_target="tpu_custom_call" | custom-call | flops 4000000000 | bytes 10000000 | tf_op jit(solution)/shard_map/attention_backward/pallas_call | solution.py:288
  272.0 5.6 %collective-permute-done.3 = bf16[2,3,192,512]{3,2,1,0:T(8,128)(2,1)} collective-permute-done((bf16[2,3,192,512]{3,2,1,0:T(8,128)(2,1)}, bf16[2,3,192,512]{3,2,1,0:T(8,128)(2,1)}, u32[]{:S(2)}, u32[]{:S(2)}) %collective-permute-start.3) | collective-permute-done | bytes 1179680 | tf_op jit(solution)/shard_map/ppermute | solution.py:1104
  277.6 1.6 collective-permute-done.4
  279.2 2.1 fusion.11
  281.3 1.7 collective-permute-start.6
  283.0 2.1 fusion.10
  285.1 0.5 collective-permute-start.5
  285.6 3.5 convolution_convert_fusion.1
  289.1 2.2 copy.126.out_ref
  291.3 96.4 %finish.1 = (bf16[128,1536]{1,0:T(8,128)(2,1)S(1)}, bf16[4,8,96,576]{3,2,1,0:T(8,128)(2,1)}) custom-call(bf16[1024,192]{1,0:T(8,128)(2,1)S(1)} %get-tuple-element.74.dq_ref, bf16[4,1024,128]{2,1,0:T(8,128)(2,1)} %bitcast.108, bf16[1024,1536]{1,0:T(8,128)(2,1)} %copy-done.20, bf16[1536,64]{1,0:T(8,128)(2,1)S(1)} %maximum_maximum_fusion.small_ref, ...), custom_call_target="tpu_custom_call" | custom-call | flops 3000000000 | bytes 100000000 | tf_op jit(solution)/shard_map/finish/pallas_call | solution.py:952
  387.7 1.4 bitcast_add_fusion.1
  389.2 1.3 bitcast_add_fusion
  390.5 1.3 fusion.9
  391.9 1.1 copy.128
  393.0 2.1 copy-done.4
  395.1 3.7 assemble.1
  398.9 0.8 slice_reduce_fusion
  399.7 0.7 copy.127
  400.4 3.8 multiply_reduce_fusion.1
  404.1 0.6 convert_divide_fusion
  404.7 0.7 copy.133
  (126 shorter events, 5.3 us)
Async XLA Ops:
  7.2 63.7 %copy-start = (s32[4,64]{1,0:T(4,128)S(1)}, s32[4,64]{1,0:T(4,128)}, u32[]{:S(2)}) copy-start(s32[4,64]{1,0:T(4,128)} %param.15) | copy-start | bytes 3076
  7.2 121.0 %all-gather.5.cloned.1.call-start = ((), (), s32[]{:S(2)}) async-start(), calls=%async_computation.2 | async-start | bytes 10616832 | tf_op jit(solution)/shard_map/all_gather | solution.py:1039
  9.6 2.1 copy-start.3
  11.7 1.7 copy-start.8
  13.4 1.1 copy-start.7
  14.4 40.0 %copy-start.5 = (bf16[8,384,384]{2,1,0:T(8,128)(2,1)}, bf16[8,384,384]{2,1,0:T(8,128)(2,1)S(1)}, u32[]{:S(2)}) copy-start(bf16[8,384,384]{2,1,0:T(8,128)(2,1)S(1)} %get-tuple-element.76.wp_ref.p0) | copy-start | bytes 7077892
  54.4 2.2 copy-start.2
  56.6 1.0 copy-start.13
  57.6 0.6 copy-start.18
  60.3 1.4 copy-start.31
  60.3 1.5 copy-start.26
  62.9 156.7 %collective-permute-start.1 = (bf16[8,384,384]{2,1,0:T(8,128)(2,1)}, bf16[8,384,384]{2,1,0:T(8,128)(2,1)}, u32[]{:S(2)}, u32[]{:S(2)}) collective-permute-start(bf16[8,384,384]{2,1,0:T(8,128)(2,1)} %copy-done.5), channel_id=1, source_target_pairs={{0,18},{1,19},{2,16},{3,17},{4,22},{5,23},{6,20},{7,21},{8,26},{9,... | collective-permute-start | bytes 7077896 | tf_op jit(solution)/shard_map/ppermute | solution.py:1040
  67.6 1.3 copy-start.14
  68.4 2.3 copy-start.20
  70.8 36.5 %copy-start.16 = (bf16[1024,192]{1,0:T(8,128)(2,1)}, bf16[1024,192]{1,0:T(8,128)(2,1)S(1)}, u32[]{:S(2)}) copy-start(bf16[1024,192]{1,0:T(8,128)(2,1)S(1)} %slice.71.q_ref) | copy-start | bytes 1179652
  92.2 15.2 %copy-start.10 = (bf16[4,1024,128]{2,1,0:T(8,128)(2,1)}, bf16[4,1024,128]{2,1,0:T(8,128)(2,1)S(1)}, u32[]{:S(2)}) copy-start(bf16[4,1024,128]{2,1,0:T(8,128)(2,1)S(1)} %gather_keys.1) | copy-start | bytes 3145732
  107.4 6.1 %copy-start.34 = (s32[1,128,2]{1,2,0:T(2,128)S(1)}, s32[1,128,2]{1,2,0:T(2,128)}, u32[]{:S(2)}) copy-start(s32[1,128,2]{1,2,0:T(2,128)} %param.16) | copy-start | bytes 3076
  107.4 6.5 %copy-start.32 = (f32[4,384]{1,0:T(4,128)S(1)}, f32[4,384]{1,0:T(4,128)}, u32[]{:S(2)}) copy-start(f32[4,384]{1,0:T(4,128)} %get-tuple-element.158) | copy-start | bytes 18436
  108.4 11.8 %all-to-all-start = ((bf16[8,128,192]{1,2,0:T(8,128)(2,1)}), bf16[8,128,192]{1,2,0:T(8,128)(2,1)S(1)}, u32[]{:S(2)}, u32[]{:S(2)}) async-start(bf16[8,128,192]{1,2,0:T(8,128)(2,1)} %copy.115), calls=%async_computation | async-start | bytes 786432 | tf_op jit(solution)/shard_map/all_to_all | solution.py:984
  113.3 172.3 %all-gather.7.cloned.1.call-start = ((), (), s32[]{:S(2)}) async-start(), calls=%async_computation.3 | async-start | bytes 3538944 | tf_op jit(solution)/shard_map/all_gather | solution.py:1101
  120.2 3.5 copy-start.15
  123.5 91.7 %copy-start.19 = (f32[128,1536]{1,0:T(8,128)}, f32[128,1536]{1,0:T(8,128)S(1)}, u32[]{:S(2)}) copy-start(f32[128,1536]{1,0:T(8,128)S(1)} %get-tuple-element.171) | copy-start | bytes 2359300
  123.7 4.5 %copy-start.21 = (bf16[128,1536]{1,0:T(8,128)(2,1)}, bf16[128,1536]{1,0:T(8,128)(2,1)S(1)}, u32[]{:S(2)}) copy-start(bf16[128,1536]{1,0:T(8,128)(2,1)S(1)} %multiply_convert_fusion) | copy-start | bytes 1179652
  124.2 2.1 copy-start.23
  211.4 2.0 copy-start.22
  211.4 2.0 copy-start.24
  213.4 1.8 copy-start.25
  215.8 2.6 copy-start.6
  218.4 31.6 %collective-permute-start = (bf16[8,384,384]{2,1,0:T(8,128)(2,1)S(1)}, bf16[8,384,384]{2,1,0:T(8,128)(2,1)}, u32[]{:S(2)}, u32[]{:S(2)}) collective-permute-start(bf16[8,384,384]{2,1,0:T(8,128)(2,1)S(1)} %copy-done.6), channel_id=1, source_target_pairs={{0,1},{1,0},{2,3},{3,2},{4,5},{5,4},{6,7},{7,6},{8,9},{9,8},{10,11... | collective-permute-start | bytes 7077896 | tf_op jit(solution)/shard_map/ppermute | solution.py:1043
  219.6 30.4 %collective-permute-start.2 = (bf16[8,384,384]{2,1,0:T(8,128)(2,1)}, bf16[8,384,384]{2,1,0:T(8,128)(2,1)}, u32[]{:S(2)}, u32[]{:S(2)}) collective-permute-start(bf16[8,384,384]{2,1,0:T(8,128)(2,1)} %collective-permute-done.1.p2), channel_id=1, source_target_pairs={{0,1},{1,0},{2,3},{3,2},{4,5},{5,4},{6,7},{7,6},{8,9},{9,8},{10,11... | collective-permute-start | bytes 7077896 | tf_op jit(solution)/shard_map/ppermute | solution.py:1045
  250.0 3.1 copy-start.11
  250.0 27.6 %collective-permute-start.3 = (bf16[2,3,192,512]{3,2,1,0:T(8,128)(2,1)}, bf16[2,3,192,512]{3,2,1,0:T(8,128)(2,1)}, u32[]{:S(2)}, u32[]{:S(2)}) collective-permute-start(bf16[2,3,192,512]{3,2,1,0:T(8,128)(2,1)} %get-tuple-element.68), channel_id=1, source_target_pairs={{0,4},{4,0},{8,12},{12,8},{16,20},{20,16},{24,28},{28,24},{32,36},... | collective-permute-start | bytes 3538952 | tf_op jit(solution)/shard_map/ppermute | solution.py:1104
  250.1 29.1 %collective-permute-start.4 = (bf16[2,3,192,512]{3,2,1,0:T(8,128)(2,1)}, bf16[2,3,192,512]{3,2,1,0:T(8,128)(2,1)}, u32[]{:S(2)}, u32[]{:S(2)}) collective-permute-start(bf16[2,3,192,512]{3,2,1,0:T(8,128)(2,1)} %get-tuple-element.70), channel_id=1, source_target_pairs={{0,2},{1,3},{2,0},{3,1},{4,6},{5,7},{6,4},{7,5},{8,10},{9,11},{10,... | collective-permute-start | bytes 3538952 | tf_op jit(solution)/shard_map/ppermute | solution.py:1105
  252.6 1.0 copy-start.12
  252.6 1.2 copy-start.17
  253.8 25.5 %copy-start.27 = (bf16[2,3,192,512]{3,2,1,0:T(8,128)(2,1)S(1)}, bf16[2,3,192,512]{3,2,1,0:T(8,128)(2,1)}, u32[]{:S(2)}) copy-start(bf16[2,3,192,512]{3,2,1,0:T(8,128)(2,1)} %get-tuple-element.84) | copy-start | bytes 3538948
  272.0 13.1 %copy-start.9 = (bf16[4096,128]{1,0:T(8,128)(2,1)}, bf16[4096,128]{1,0:T(8,128)(2,1)S(1)}, u32[]{:S(2)}) copy-start(bf16[4096,128]{1,0:T(8,128)(2,1)S(1)} %get-tuple-element.75) | copy-start | bytes 3145732
  272.0 10.9 %copy-start.29 = (bf16[2,3,192,512]{3,2,1,0:T(8,128)(2,1)S(1)}, bf16[2,3,192,512]{3,2,1,0:T(8,128)(2,1)}, u32[]{:S(2)}) copy-start(bf16[2,3,192,512]{3,2,1,0:T(8,128)(2,1)} %get-tuple-element.82) | copy-start | bytes 3538948
  281.3 106.4 %collective-permute-start.6 = (bf16[3,192,512]{2,1,0:T(8,128)(2,1)}, bf16[3,192,512]{2,1,0:T(8,128)(2,1)S(1)}, u32[]{:S(2)}, u32[]{:S(2)}) collective-permute-start(bf16[3,192,512]{2,1,0:T(8,128)(2,1)} %fusion.11), channel_id=1, source_target_pairs={{0,4},{4,0},{8,12},{12,8},{16,20},{20,16},{24,28},{28,24},{32,36},... | collective-permute-start | bytes 1769480 | tf_op jit(solution)/shard_map/ppermute | solution.py:1118
  285.1 102.7 %collective-permute-start.5 = (bf16[3,192,512]{2,1,0:T(8,128)(2,1)}, bf16[3,192,512]{2,1,0:T(8,128)(2,1)S(1)}, u32[]{:S(2)}, u32[]{:S(2)}) collective-permute-start(bf16[3,192,512]{2,1,0:T(8,128)(2,1)} %fusion.10), channel_id=1, source_target_pairs={{0,2},{1,3},{2,0},{3,1},{4,6},{5,7},{6,4},{7,5},{8,10},{9,11},{10,... | collective-permute-start | bytes 1769480 | tf_op jit(solution)/shard_map/ppermute | solution.py:1117
  291.3 96.4 %copy-start.30 = (bf16[2,3,192,512]{3,2,1,0:T(8,128)(2,1)S(1)}, bf16[2,3,192,512]{3,2,1,0:T(8,128)(2,1)}, u32[]{:S(2)}) copy-start(bf16[2,3,192,512]{3,2,1,0:T(8,128)(2,1)} %get-tuple-element.82) | copy-start | bytes 3538948
  387.7 1.5 copy-start.28
  393.0 2.1 copy-start.4
  400.4 3.8 copy-start.33
  400.4 5.1 %copy-start.1 = (s32[4,64]{1,0:T(4,128)S(1)}, s32[4,64]{1,0:T(4,128)}, u32[]{:S(2)}) copy-start(s32[4,64]{1,0:T(4,128)} %param.15) | copy-start | bytes 3076
Sparse Core Ops, SparseCore 0:
  63.1 60.6 all-gather.4
  218.5 49.0 all-gather.6

commit v4 on v3

--- a/solution.py
+++ b/solution.py
@@ -304,42 +304,36 @@
     )(meta, q, kv, o, lse, d_o)
 
 
-def assemble_kernel(by_row_ref, by_head_ref, qkv_ref, out_ref, rest_ref):
-    heads = [by_row_ref[0, h].astype(F32) for h in range(8)]
+def assemble_kernel(pieces_ref, qkv_ref, out_ref, rest_ref):
+    parts = [pieces_ref[0, i].astype(F32) for i in range(8)]
     ends = (0, WIDTH, WIDTH + HEAD_SIZE, HEAD_COLUMNS)
-    qkv_ref[...] = jnp.concatenate([t[:, a:b] for a, b in zip(ends[:-1], ends[1:]) for t in heads], axis=1)
-    tail = heads[0]
-    for t in heads[1:]:
+    qkv_ref[...] = jnp.concatenate([t[:, a:b] for a, b in zip(ends[:-1], ends[1:]) for t in parts], axis=1)
+    out_ref[...] = jnp.concatenate([t[:, 384:] for t in parts], axis=1)
+    tail = parts[0]
+    for t in parts[1:]:
         tail = tail + t
     rest_ref[...] = tail[:, HEAD_COLUMNS:384]
-    for parity in range(2):
-        parts = [by_head_ref[y, 0, 1 - parity, :, 384:].astype(F32).T for y in range(4)]
-        out_ref[parity * WIDTH : (parity + 1) * WIDTH, :] = jnp.concatenate(parts, axis=1)
 
 
 def assemble(gathered):
     _, _, piece, columns = gathered.shape
-    shard = 4 * piece
+
+    def by_rows(n):
+        return pl.BlockSpec((piece, n), lambda i: (i, 0))
+
     return pl.pallas_call(
         assemble_kernel,
         out_shape=(
-            jax.ShapeDtypeStruct((shard, 8 * HEAD_COLUMNS), F32),
-            jax.ShapeDtypeStruct((2 * WIDTH, 4 * shard), F32),
-            jax.ShapeDtypeStruct((shard, 64), F32),
+            jax.ShapeDtypeStruct((4 * piece, 8 * HEAD_COLUMNS), F32),
+            jax.ShapeDtypeStruct((4 * piece, 8 * WIDTH), F32),
+            jax.ShapeDtypeStruct((4 * piece, 64), F32),
         ),
         grid=(4,),
-        in_specs=[
-            pl.BlockSpec((1, 8, piece, columns), lambda i: (i, 0, 0, 0)),
-            pl.BlockSpec((4, 1, 2, piece, columns), lambda i: (0, i, 0, 0, 0)),
-        ],
-        out_specs=(
-            pl.BlockSpec((piece, 8 * HEAD_COLUMNS), lambda i: (i, 0)),
-            pl.BlockSpec((2 * WIDTH, shard), lambda i: (0, i)),
-            pl.BlockSpec((piece, 64), lambda i: (i, 0)),
-        ),
+        in_specs=[pl.BlockSpec((1, 8, piece, columns), lambda i: (i, 0, 0, 0))],
+        out_specs=(by_rows(8 * HEAD_COLUMNS), by_rows(8 * WIDTH), by_rows(64)),
         compiler_params=pltpu.CompilerParams(vmem_limit_bytes=40 * 2**20),
         name="assemble",
-    )(gathered, gathered.reshape(4, 4, 2, piece, columns))
+    )(gathered)
 
 
 MESH = pl.DeviceIdType.MESH
@@ -350,7 +344,7 @@
     def __init__(self, send, recv, local):
         self.send, self.recv, self.local = send, recv, local
         self.remote_count = self.local_count = 0
-        self.started, self.kept = [], []
+        self.started, self.kept, self.left = [], [], []
 
     def to(self, source, target, device):
         k = self.remote_count
@@ -374,9 +368,15 @@
             first.wait()
             second.start()
 
+    def sent(self, several):
+        for copy in several:
+            copy.wait_send()
+            self.left.append(copy)
+
     def finish(self, arrived):
         for copy in self.started:
-            copy.wait_send()
+            if not any(copy is other for other in self.left):
+                copy.wait_send()
             if not any(copy is other for other in arrived):
                 copy.wait_recv()
         for _, second in self.kept:
@@ -529,26 +529,31 @@
 FF_STEP = 256
 
 
-def experts_kernel(
-    rows_ref, grads_ref, w_ref, back_out, returned_out, half_send, half_keep, side_send, side_keep,
-    w_v, x_v, g_v, turned_x, turned_g, out_v, d_in_v, acc_v, gate_v, up_v, hidden_v, d_gate_v, d_up_v, sent_v, got_v,
-    send, recv, local,
+def middle_kernel(
+    attn_ref, x_ref, cot_ref, wo_ref, head_ref, gain_ref, choice_ref, slot_ref, slot_t_ref, w_ref,
+    out_ref, d_mid_ref, small_ref, d_attn_to, branch_to, half_out, side_out,
+    attn_v, wo_v, w_v, x_v, g_v, turned_x, turned_g, out_v, d_in_v, back_v, returned_v, acc_v, gate_v, up_v,
+    hidden_v, d_gate_v, d_up_v, got_v, half_got, side_got, mid_v, act_v, d_attn_v, branch_v, send, recv, local,
 ):
     index, stream = lax.axis_index("ctx"), lax.axis_index("wsh")
-    x, mine = index % 4, index // 2
-    inner = (x + 1) // 2 % 2
+    place, mine = turned(index), index // 2
+    y, r = place // 8, place % 8
+    inner = (index % 4 + 1) // 2 % 2
 
     def device(p):
         return {"ctx": p // 2 * 4 + (1 - inner) * (3 * (p % 2)) + inner * (1 + p % 2)}
 
     peers = [(mine + k) % 16 for k in range(1, 16)]
-    core = stream % 2
+    in_row = [(r + k) % 8 for k in range(1, 8)]
+    core, half, side = stream % 2, index % 2, stream // 2
     other = {"wsh": stream + 1 - 2 * core}
-    meet([device(p) for p in peers] + [other])
+    other_half, other_side = {"ctx": index + 1 - 2 * half}, {"wsh": (stream + 2) % 4}
+    meet([device(p) for p in peers] + [other, other_half, other_side])
     copies = Copies(send, recv, local)
     width, rows = turned_x.shape
+    tokens = x_ref.shape[0]
     quarter = width // 4
-    own = []
+    own, arrived = [], []
 
     def here(source, target):
         copy = pltpu.make_async_copy(source, target, local.at[len(own)])
@@ -556,22 +561,47 @@
         own.append(copy)
         return copy
 
-    came = [copies.to(rows_ref.at[p], x_v.at[mine], device(p)) for p in peers]
-    own_x = here(rows_ref.at[mine], x_v.at[mine])
+    def arrive(several):
+        for copy in several:
+            copy.wait_recv()
+            arrived.append(copy)
+
+    attn_came = [copies.to(attn_ref.at[pr], attn_v.at[r], {"ctx": turned(8 * y + pr)}) for pr in in_row]
+    own_attn = here(attn_ref.at[r], attn_v.at[r])
+    own_wo = here(wo_ref, wo_v)
     weights = [
         here(w_ref.at[4 * k + q, m], w_v.at[k, m, pl.ds(q * quarter, quarter)])
         for k in range(2)
         for q in range(4)
         for m in range(3)
     ]
-    came_g = [copies.to(grads_ref.at[p], g_v.at[mine], device(p)) for p in peers]
-    own_g = here(grads_ref.at[mine], g_v.at[mine])
-    arrived = []
-
-    def arrive(several):
-        for copy in several:
-            copy.wait_recv()
-            arrived.append(copy)
+    lanes = lax.broadcasted_iota(jnp.int32, (tokens, 64), 1)
+    chosen = [choice_ref[:, j : j + 1] == lanes for j in range(TOP)]
+    slot_rows = lax.broadcasted_iota(jnp.int32, (rows, tokens), 0)
+    to_slot = [jnp.where(slot_t_ref[j : j + 1, :] == slot_rows, 1.0, 0.0).astype(BF) for j in range(TOP)]
+    own_attn.wait()
+    own_wo.wait()
+    arrive(attn_came)
+    middle = x_ref[...].astype(F32)
+    for i in range(4):
+        pair = jnp.concatenate([attn_v[2 * i], attn_v[2 * i + 1]], axis=1)
+        middle += dot(pair, wo_v[i * quarter : (i + 1) * quarter, :])
+    mid_v[...] = middle
+    scale = rms_scale(middle)
+    act = (middle * scale * gain_ref[...]).astype(BF)
+    act_v[...] = act
+    out_v[...] = dot(to_slot[0] + to_slot[1], act).astype(BF).reshape(out_v.shape)
+    came = [copies.to(out_v.at[p], x_v.at[mine], device(p)) for p in peers]
+    own_x = here(out_v.at[mine], x_v.at[mine])
+    logits = dot(act, head_ref[:, HEAD_COLUMNS:])
+    picked = [jnp.sum(jnp.where(c, logits, 0.0), axis=-1, keepdims=True) for c in chosen]
+    top = jnp.maximum(picked[0], picked[1])
+    powers = [jnp.exp(p - top) for p in picked]
+    gates = [p / (powers[0] + powers[1]) for p in powers]
+    gated = jnp.concatenate([(g * cot_ref[...].astype(F32)).astype(BF) for g in gates], axis=0)
+    d_in_v[...] = dot(jnp.concatenate(to_slot, axis=1), gated).astype(BF).reshape(d_in_v.shape)
+    came_g = [copies.to(d_in_v.at[p], g_v.at[mine], device(p)) for p in peers]
+    own_g = here(d_in_v.at[mine], g_v.at[mine])
 
     for copy in weights:
         copy.wait()
@@ -593,10 +623,10 @@
         return carry
 
     lax.fori_loop(0, 2 * steps, forward, 0)
+    copies.sent(came)
     out_v[...] = acc_v[...].astype(BF).reshape(out_v.shape)
-    for p in peers:
-        copies.to(out_v.at[p], back_out.at[mine], device(p))
-    own_back = here(out_v.at[mine], back_out.at[mine])
+    outs = [copies.to(out_v.at[p], back_v.at[mine], device(p)) for p in peers]
+    own_back = here(out_v.at[mine], back_v.at[mine])
     for q in range(4):
         at = slice(q * quarter, (q + 1) * quarter)
         turned_x[at, :] = x_v[:, :, at].reshape(rows, quarter).T
@@ -617,10 +647,10 @@
         return carry
 
     lax.fori_loop(0, 2 * steps, backward, 0)
+    copies.sent(came_g)
     d_in_v[...] = acc_v[...].astype(BF).reshape(d_in_v.shape)
-    for p in peers:
-        copies.to(d_in_v.at[p], returned_out.at[mine], device(p))
-    own_returned = here(d_in_v.at[mine], returned_out.at[mine])
+    returns = [copies.to(d_in_v.at[p], returned_v.at[mine], device(p)) for p in peers]
+    own_returned = here(d_in_v.at[mine], returned_v.at[mine])
     for q in range(4):
         at = slice(q * quarter, (q + 1) * quarter)
         turned_g[at, :] = g_v[:, :, at].reshape(rows, quarter).T
@@ -634,74 +664,149 @@
             dot(turned_g[at, :], hidden_v[k]),
         )
 
-    half, side = index % 2, stream // 2
     crossing = []
     for dz in (1, 0):
         z = side + dz - 2 * side * dz
 
         def other_term(k, carry, z=z, dz=dz):
+            at = pl.ds(pl.multiple_of((2 * dz + k) * quarter, quarter), quarter)
             for m, term in enumerate(terms(k, z, 1 - core)):
-                sent_v[dz, k, m] = term.astype(BF)
+                w_v[0, m, at] = term.astype(BF)
             return carry
 
         lax.fori_loop(0, 2, other_term, 0)
-        crossing.append(copies.to(sent_v.at[dz], got_v.at[dz], other))
+        at = pl.ds(2 * dz * quarter, 2 * quarter)
+        crossing.append(copies.to(w_v.at[0, :, at], got_v.at[:, at], other))
     halfway = quarter // 2
     for dz, copy in zip((1, 0), crossing):
         z = side + dz - 2 * side * dz
         arrive([copy])
         for dk in (1, 0):
             k = half + dk - 2 * half * dk
+            got_at = pl.ds(pl.multiple_of((2 * dz + k) * quarter, quarter), quarter)
+            z_at = pl.ds(pl.multiple_of(z * halfway, halfway), halfway)
+            k_at = pl.ds(pl.multiple_of(quarter + k * halfway, halfway), halfway)
             for m, term in enumerate(terms(k, z, core)):
-                total = (term + got_v[dz, k, m].astype(F32)).astype(BF)
-                (half_send if dk else half_keep)[z, m] = total[:halfway]
-                (side_send if dz else side_keep)[k, m] = total[halfway:]
+                total = (term + got_v[m, got_at].astype(F32)).astype(BF)
+                if dk:
+                    w_v[1, m, z_at] = total[:halfway]
+                else:
+                    half_out[m, z] = total[:halfway]
+                if dz:
+                    w_v[1, m, k_at] = total[halfway:]
+                else:
+                    side_out[m, k] = total[halfway:]
+    first = copies.to(w_v.at[1, :, pl.ds(0, quarter)], half_got, other_half)
+    second = copies.to(w_v.at[1, :, pl.ds(quarter, quarter)], side_got, other_side)
+
+    slot_lanes = lax.broadcasted_iota(jnp.int32, (tokens, rows), 1)
+    of_slot = [jnp.where(slot_ref[:, j : j + 1] == slot_lanes, 1.0, 0.0).astype(BF) for j in range(TOP)]
+    own_back.wait()
+    arrive(outs)
+    back = back_v[...].reshape(rows, width)
+    d_out = cot_ref[...].astype(F32)
+    total = mid_v[...]
+    d_gates = []
+    for j in range(TOP):
+        both = dot(of_slot[j], back)
+        total += gates[j] * both
+        d_gates.append(jnp.sum(d_out * both, axis=-1, keepdims=True))
+    out_ref[...] = total.astype(BF)
+    inner_sum = gates[0] * d_gates[0] + gates[1] * d_gates[1]
+    d_logits = 0.0
+    for j in range(TOP):
+        d_logits += jnp.where(chosen[j], gates[j] * (d_gates[j] - inner_sum), 0.0)
+    d_logits = d_logits.astype(BF)
+    own_returned.wait()
+    arrive(returns)
+    d_act = dot(of_slot[0] + of_slot[1], returned_v[...].reshape(rows, width))
+    d_act += dot(d_logits, head_ref[:, HEAD_COLUMNS:], NT)
+    middle = mid_v[...]
+    normed = middle * scale
+    spot = jnp.where(lanes == 16, 1.0, 0.0).astype(BF)
+    small_ref[...] = (dot(act_v[...].T, d_logits) + dot((d_act * normed).astype(BF).T, spot)).astype(BF)
+    scaled = d_act * gain_ref[...]
+    d_mid = d_out + scale * (scaled - normed * scale * jnp.mean(scaled * middle, axis=-1, keepdims=True))
+    d_mid_ref[...] = d_mid
+    d_branch = d_mid.astype(BF)
+    for i in range(8):
+        branch_v[i] = d_branch[:, i * WIDTH : (i + 1) * WIDTH]
+    to_row = [copies.to(branch_v.at[pr], branch_to.at[r], {"ctx": turned(8 * y + pr)}) for pr in in_row]
+    for i in range(4):
+        pair = dot(d_branch, wo_v[i * quarter : (i + 1) * quarter, :], NT).astype(BF)
+        d_attn_v[2 * i] = pair[:, :WIDTH]
+        d_attn_v[2 * i + 1] = pair[:, WIDTH:]
+    to_row += [copies.to(d_attn_v.at[pr], d_attn_to.at[r], {"ctx": turned(8 * y + pr)}) for pr in in_row]
+    own_row = [here(branch_v.at[r], branch_to.at[r]), here(d_attn_v.at[r], d_attn_to.at[r])]
+    arrive([first, second])
+    for m in range(3):
+        for i in range(2):
+            at = slice(i * halfway, (i + 1) * halfway)
+            half_out[m, i] = (half_out[m, i].astype(F32) + half_got[m, at].astype(F32)).astype(BF)
+            side_out[m, i] = (side_out[m, i].astype(F32) + side_got[m, at].astype(F32)).astype(BF)
     copies.finish(arrived)
-    own_back.wait()
-    own_returned.wait()
-
-
-def experts(send_rows, send_grads, weights):
-    groups, capacity, width = send_rows.shape
-    rows = groups * capacity
-    half = weights.shape[3]
+    own_back = own_row
+    for copy in own_back:
+        copy.wait()
+
+
+def run_middle(attn, x, cotangent, w_out, head_full, gain, choice, slots, weights):
+    _, tokens, _ = attn.shape
+    width = x.shape[1]
+    groups, capacity = 16, 2 * TOP * tokens // 16
+    rows, half, quarter = groups * capacity, weights.shape[3], width // 4
+    steps = 2 * half // FF_STEP
     vmem = pltpu.VMEM
-    steps = 2 * half // FF_STEP
-    slots = vmem(send_rows.shape, BF)
-    terms = (2, 2, 3, width // 4, half)
+    whole = pl.BlockSpec(memory_space=pltpu.VMEM)
+    slot_rows = vmem((groups, capacity, width), BF)
+    wide, low = vmem((steps, rows, FF_STEP), F32), vmem((2, rows, half), BF)
+    part = jax.ShapeDtypeStruct((3, 2, quarter // 2, half), BF)
     return pl.pallas_call(
-        experts_kernel,
+        middle_kernel,
         out_shape=(
-            jax.ShapeDtypeStruct(send_rows.shape, BF),
-            jax.ShapeDtypeStruct(send_rows.shape, BF),
-        )
-        + (jax.ShapeDtypeStruct((2, 3, width // 8, half), BF),) * 4,
-        in_specs=[ANY, ANY, ANY],
-        out_specs=(ANY, ANY) + (pl.BlockSpec(memory_space=pltpu.VMEM),) * 4,
+            jax.ShapeDtypeStruct(x.shape, BF),
+            jax.ShapeDtypeStruct(x.shape, F32),
+            jax.ShapeDtypeStruct((width, 64), BF),
+            jax.ShapeDtypeStruct(attn.shape, BF),
+            jax.ShapeDtypeStruct(attn.shape, BF),
+            part,
+            part,
+        ),
+        in_specs=[ANY, whole, whole, ANY, whole, whole, whole, whole, whole, ANY],
+        out_specs=(whole, whole, whole, ANY, ANY, whole, whole),
         scratch_shapes=[
+            vmem(attn.shape, BF),
+            vmem(w_out.shape, BF),
             vmem((2, 3, width, half), BF),
-            slots,
-            slots,
+            slot_rows,
+            slot_rows,
             vmem((width, rows), BF),
             vmem((width, rows), BF),
-            slots,
-            slots,
+            slot_rows,
+            slot_rows,
+            slot_rows,
+            slot_rows,
             vmem((rows, width), F32),
-            vmem((steps, rows, FF_STEP), F32),
-            vmem((steps, rows, FF_STEP), F32),
-            vmem((2, rows, half), BF),
-            vmem((2, rows, half), BF),
-            vmem((2, rows, half), BF),
-            vmem(terms, BF),
-            vmem(terms, BF),
-            pltpu.SemaphoreType.DMA((62,)),
-            pltpu.SemaphoreType.DMA((62,)),
-            pltpu.SemaphoreType.DMA((28,)),
+            wide,
+            wide,
+            low,
+            low,
+            low,
+            vmem((3, width, half), BF),
+            vmem((3, quarter, half), BF),
+            vmem((3, quarter, half), BF),
+            vmem(x.shape, F32),
+            vmem(x.shape, BF),
+            vmem(attn.shape, BF),
+            vmem(attn.shape, BF),
+            pltpu.SemaphoreType.DMA((85,)),
+            pltpu.SemaphoreType.DMA((85,)),
+            pltpu.SemaphoreType.DMA((32,)),
         ],
-        compiler_params=pltpu.CompilerParams(collective_id=6, has_side_effects=True, vmem_limit_bytes=56 * 2**20),
+        compiler_params=pltpu.CompilerParams(collective_id=6, has_side_effects=True, vmem_limit_bytes=60 * 2**20),
         cost_estimate=pl.CostEstimate(flops=15 * 10**9, bytes_accessed=10**8, transcendentals=10**6),
-        name="experts",
-    )(send_rows, send_grads, weights)
+        name="middle",
+    )(attn, x, cotangent, w_out, head_full, gain.reshape(1, width), choice, slots, slots.T, weights)
 
 
 def prepare_kernel(qkv_ref, router_ref, wo_ref, wp_out, wo_out):
@@ -749,9 +854,9 @@
 
 
 def finish_kernel(
-    dq_ref, kv_ref, act_ref, small_ref, out_ref, p0, p1, p2, p3, x_ref, d_mid_ref, gain_ref, d_tokens_ref, all_out,
-    kv_v, out_v, grad_v, grad_to, term_v, term_to, act_t, own_v, w_v, acc_v,
-    send, recv, out_send, out_recv, local,
+    dq_ref, kv_ref, act_ref, small_ref, attn_ref, branch_ref, p0, p1, p2, p3, x_ref, d_mid_ref, gain_ref,
+    d_tokens_ref, all_out, kv_v, grad_v, grad_to, term_v, term_to, out_v, out_to, attn_v, act_t, own_v, w_v, acc_v,
+    send, recv, local,
 ):
     place, stream = turned(lax.axis_index("ctx")), lax.axis_index("wsh")
     y, r = place // 8, place % 8
@@ -765,19 +870,7 @@
     up, down, beyond = (at_place((place + 8 * k) % 32) for k in (1, 3, 2))
     others = [((y + k // 4) % 4, (stream + k % 4) % 4) for k in range(1, 16)]
     in_row = [(r + k) % 8 for k in range(1, 8)]
-    served = 2 * stream + 1 - r % 2
-
-    def out_target(p):
-        return {"ctx": turned(p // 4 * 8 + 2 * (p % 4) + 1 - r % 2), "wsh": r // 2}
-
-    barrier = pltpu.get_barrier_semaphore()
-    partners = [{"ctx": turned(r + 8 * py), "wsh": pw} for py, pw in others]
-    partners += [at_place(8 * y + pr) for pr in in_row]
-    sources = [{"ctx": turned(i // 4 * 8 + served), "wsh": i % 4} for i in range(16)]
-    for device in partners + sources:
-        pl.semaphore_signal(barrier, inc=1, device_id=device, device_id_type=MESH)
-    pl.semaphore_wait(barrier, len(partners) + 16)
-
+    meet([{"ctx": turned(r + 8 * py), "wsh": pw} for py, pw in others] + [at_place(8 * y + pr) for pr in in_row])
     copies = Copies(send, recv, local)
     rows, width = act_ref.shape
     shard, piece = width // 4, own_v.shape[0]
@@ -800,18 +893,18 @@
         copies.to(kv_ref.at[(y + k) % 4], kv_v.at[y], at_place((place + 8 * k) % 32)) for k in (2, 1, 3)
     ]
     own_kv = here(kv_ref.at[y], kv_v.at[y])
-    out_copies = []
-    for p in range(16):
-        copy = pltpu.make_async_remote_copy(
-            out_ref.at[pl.ds(p % 4 * shard + p // 4 * piece, piece)],
-            out_v.at[y * 4 + stream],
-            out_send.at[p],
-            out_recv.at[y * 4 + stream],
-            device_id=out_target(p),
-            device_id_type=MESH,
-        )
-        copy.start()
-        out_copies.append(copy)
+    r_z = (1 - z) * 4 + x
+    r_left, r_right = z * 4 + (x + 3) % 4, z * 4 + (x + 1) % 4
+    z_left, z_right = (1 - z) * 4 + (x + 3) % 4, (1 - z) * 4 + (x + 1) % 4
+    front, rear = pl.ds(0, 4), pl.ds(4, 4)
+
+    def pass_on(device, *at):
+        return copies.to(attn_v.at[at], attn_v.at[at], device)
+
+    attn_cross = copies.to(attn_ref, attn_v.at[r], across)
+    attn_right = copies.to(attn_ref, attn_v.at[r], right)
+    attn_left = copies.to(attn_ref, attn_v.at[r], left)
+    own_attn = here(attn_ref, attn_v.at[r])
     weights = [here(p, w_v.at[j]) for j, p in enumerate((p0, p1, p2, p3))]
     dq = dq_ref[...]
     for q in range(4):
@@ -822,6 +915,12 @@
             term_v[i, q, :, :WIDTH] = term[i * piece : (i + 1) * piece]
             at = q * shard + i * piece
             term_v[i, q, :, HEAD_COLUMNS:] = small_ref[at : at + piece, :]
+    arrive(attn_cross)
+    attn_far = [pass_on(right, r_z), pass_on(left, r_z)]
+    arrive(attn_right)
+    attn_on = [pass_on(right, r_left, front)]
+    arrive(attn_left)
+    attn_on.append(pass_on(left, r_right, rear))
     own_kv.wait()
     arrive(*kv_came)
     total = kv_v[0].astype(F32)
@@ -844,27 +943,38 @@
                 device = {"ctx": turned(r + 8 * py), "wsh": pw}
                 terms.append(copies.to(term_v.at[py, pw], term_to.at[y, stream], device))
     own_term = here(term_v.at[y, stream], term_to.at[y, stream])
-    for i, copy in enumerate(out_copies):
-        pltpu.make_async_remote_copy(
-            out_v.at[i], out_v.at[i], out_send.at[i], out_recv.at[i], device_id=across, device_id_type=MESH
-        ).wait_recv()
-        copy.wait_send()
-    total = out_v[0].astype(F32)
-    for i in range(1, 16):
-        total = total + out_v[i].astype(F32)
-    own_v[:, 384:] = total.astype(BF)
+    arrive(attn_far[0])
+    attn_on.append(pass_on(right, z_left, front))
+    arrive(attn_far[1])
+    attn_on.append(pass_on(left, z_right, rear))
+    own_attn.wait()
+    arrive(*attn_on)
+    branch = branch_ref[...]
+    for h in range(8):
+        term = dot(attn_v[h].reshape(rows, WIDTH).T, branch).astype(BF)
+        for i in range(2):
+            n = 2 * h + i
+            out_v[n % 4, n // 4] = term[i * piece : (i + 1) * piece]
+    outs = []
+    for k in (8, 4, 12, 10, 6, 14, 2, 9, 5, 13, 1, 11, 7, 15, 3):
+        py, pw = others[k - 1]
+        outs.append(copies.to(out_v.at[py, pw], out_to.at[y, stream], {"ctx": turned(r + 8 * py), "wsh": pw}))
+    own_out = here(out_v.at[y, stream], out_to.at[y, stream])
     own_term.wait()
     arrive(*terms)
     total = term_to[0, 0].astype(F32)
     for i in range(1, 16):
         total = total + term_to[i // 4, i % 4].astype(F32)
     own_v[:, :384] = total.astype(BF)
+    own_out.wait()
+    arrive(*outs)
+    total = out_to[0, 0].astype(F32)
+    for i in range(1, 16):
+        total = total + out_to[i // 4, i % 4].astype(F32)
+    own_v[:, 384:] = total.astype(BF)
 
     half = piece // 2
     first, last = pl.ds(0, half), pl.ds(half, half)
-    r_z = (1 - z) * 4 + x
-    r_left, r_right = z * 4 + (x + 3) % 4, z * 4 + (x + 1) % 4
-    z_left, z_right = (1 - z) * 4 + (x + 3) % 4, (1 - z) * 4 + (x + 1) % 4
 
     def on(device, *at):
         return copies.to(all_out.at[at], all_out.at[at], device)
@@ -944,7 +1054,7 @@
     copies.finish(arrived)
 
 
-def finish(dq, kv, act, small, out_term, pieces, x, d_middle, gain):
+def finish(dq, kv, act, small, attn, branch, pieces, x, d_middle, gain):
     rows, width = act.shape
     piece = width // 16
     vmem = pl.BlockSpec(memory_space=pltpu.VMEM)
@@ -955,29 +1065,29 @@
             jax.ShapeDtypeStruct(x.shape, BF),
             jax.ShapeDtypeStruct((4, 8, piece, 384 + WIDTH), BF),
         ),
-        in_specs=[vmem, ANY, vmem, vmem, ANY] + [ANY] * 4 + [vmem] * 3,
+        in_specs=[vmem, ANY, vmem, vmem, ANY, vmem] + [ANY] * 4 + [vmem] * 3,
         out_specs=(vmem, ANY),
         scratch_shapes=[
             scratch(kv.shape, BF),
-            scratch((16, piece, WIDTH), BF),
             scratch((8, rows // 8, 384), BF),
             scratch((8, rows // 8, 384), BF),
             scratch((4, 4, piece, 384), BF),
             scratch((4, 4, piece, 384), BF),
+            scratch((4, 4, piece, WIDTH), BF),
+            scratch((4, 4, piece, WIDTH), BF),
+            scratch((8,) + attn.shape, BF),
             scratch((width, rows), BF),
             scratch((piece, 384 + WIDTH), BF),
             scratch((4,) + pieces[0].shape, BF),
             scratch((4, rows // 8, width // 4), F32),
-            pltpu.SemaphoreType.DMA((50,)),
-            pltpu.SemaphoreType.DMA((50,)),
-            pltpu.SemaphoreType.DMA((16,)),
-            pltpu.SemaphoreType.DMA((16,)),
-            pltpu.SemaphoreType.DMA((8,)),
+            pltpu.SemaphoreType.DMA((74,)),
+            pltpu.SemaphoreType.DMA((74,)),
+            pltpu.SemaphoreType.DMA((10,)),
         ],
         compiler_params=pltpu.CompilerParams(collective_id=3, has_side_effects=True, vmem_limit_bytes=52 * 2**20),
         cost_estimate=pl.CostEstimate(flops=3 * 10**9, bytes_accessed=10**8, transcendentals=0),
         name="finish",
-    )(dq, kv, act, small, out_term, *pieces, x, d_middle, gain.reshape(1, width))
+    )(dq, kv, act, small, attn, branch, *pieces, x, d_middle, gain.reshape(1, width))
 
 
 def swap(x, groups, axis="ctx"):
@@ -1037,13 +1147,6 @@
     w_gate, w_up, w_down, _ = lax.optimization_barrier((w_gate, w_up, w_down, gains))
     expert_shard = jnp.stack([w_gate[0].astype(BF), w_up[0].astype(BF), w_down[0].T.astype(BF)])
     expert_all = lax.all_gather(expert_shard, ("ctx", "wsh"), axis_index_groups=OWNERS)
-    far_qkv = lax.ppermute(by_head, ("ctx", "wsh"), NEXT_Z)
-    qkv_pieces = [
-        by_head,
-        lax.ppermute(by_head, "wsh", OTHER_CORE),
-        far_qkv,
-        lax.ppermute(far_qkv, "wsh", OTHER_CORE),
-    ]
 
     group_x = group_tokens.reshape(8 * rows, width).astype(F32)
     group_act = (group_x * rms_scale(group_x) * gain_first).astype(BF)
@@ -1051,77 +1154,37 @@
     kv_all = gather_keys(head_qkv[:, WIDTH:]).reshape(32 * rows, 2 * HEAD_SIZE)
     head_q = head_qkv[:, :WIDTH]
     head_attn, lse = run_forward(meta, head_q, kv_all)
-    attn_low = swap(head_attn.reshape(8, rows, WIDTH), ROW).transpose(1, 0, 2).reshape(rows, q_columns)
-
-    x_first = tokens[0].astype(F32)
-    middle = x_first + dot(attn_low, full_out)
-    scale_second = rms_scale(middle)
-    act_moe = (middle * scale_second * gain_second).astype(BF)
-    logits = dot(act_moe, full_router)
-    choice = expert_ids[0]
+    by_head, head_attn = lax.optimization_barrier((by_head, head_attn))
+    far_qkv = lax.ppermute(by_head, ("ctx", "wsh"), NEXT_Z)
+    near_qkv = lax.ppermute(by_head, "wsh", OTHER_CORE)
+    head_blocks = head_attn.reshape(8, rows, WIDTH)
+    flat_ids = expert_ids[0].reshape(-1)
     expert_range = jnp.arange(experts_count, dtype=jnp.int32)
-    picked_hot = choice[:, :, None] == expert_range[None, None, :]
-    picked = jnp.sum(jnp.where(picked_hot, logits[:, None, :], 0.0), axis=-1)
-    picked_exp = jnp.exp(picked - jnp.max(picked, axis=-1, keepdims=True))
-    gates = picked_exp / jnp.sum(picked_exp, axis=-1, keepdims=True)
-    flat_ids = choice.reshape(-1)
     assign_hot = (flat_ids[:, None] == expert_range[None, :]).astype(jnp.int32)
     ranks = jnp.sum((jnp.cumsum(assign_hot, axis=0) - 1) * assign_hot, axis=1)
     slots = (flat_ids * capacity + ranks).reshape(rows, TOP)
-    slot_range = jnp.arange(experts_count * capacity, dtype=jnp.int32)
-    hot = [slots[:, j][:, None] == slot_range[None, :] for j in range(TOP)]
-    hot_low = [h.astype(BF) for h in hot]
-    hot_any = hot_low[0] + hot_low[1]
-    slot_gate = sum(jnp.sum(jnp.where(hot[j], gates[:, j][:, None], 0.0), axis=0) for j in range(TOP))
-
-    send_rows = dot(hot_any, act_moe, TN).astype(BF).reshape(experts_count, capacity, width)
-    send_grads = (slot_gate[:, None] * dot(hot_any, cotangent[0], TN)).astype(BF)
-    back_rows, returned, *expert_terms = experts(send_rows, send_grads.reshape(experts_count, capacity, width), expert_all)
-    back_rows, returned = (r.reshape(-1, width) for r in (back_rows, returned))
-
-    both = [dot(hot_low[j], back_rows) for j in range(TOP)]
-    output_rows = (middle + gates[:, :1] * both[0] + gates[:, 1:] * both[1]).astype(BF)
-    d_out = cotangent[0].astype(F32)
-    d_gates = jnp.stack([jnp.sum(d_out * both[j], axis=-1) for j in range(TOP)], axis=1)
-    d_picked = gates * (d_gates - jnp.sum(gates * d_gates, axis=-1, keepdims=True))
-    d_logits = jnp.sum(jnp.where(picked_hot, d_picked[:, :, None], 0.0), axis=1).astype(BF)
-    d_act_moe = dot(hot_any, returned) + dot(d_logits, full_router, NT)
-    d_router_local = dot(act_moe, d_logits, TN)
-    d_gain_second = jnp.sum(d_act_moe * middle * scale_second, axis=0)
-    scaled = d_act_moe * gain_second
-    d_middle = (
-        d_out
-        + scale_second * scaled
-        - middle * scale_second**3 * jnp.mean(scaled * middle, axis=-1, keepdims=True)
+    output_rows, d_middle, small_term, head_d_attn, branch_part, half_sum, side_sum = run_middle(
+        head_blocks, tokens[0], cotangent[0], full_out, head_full, gain_second, expert_ids[0], slots, expert_all
     )
-    d_branch = d_middle.astype(BF)
-
-    d_attn = dot(d_branch, full_out, NT).astype(BF)
-    head_d_attn = swap(d_attn.reshape(rows, 8, WIDTH).transpose(1, 0, 2), ROW).reshape(8 * rows, WIDTH)
-    group_branch = lax.all_gather(d_branch, "ctx", axis_index_groups=ROW).reshape(8 * rows, width)
-    head_d_attn, expert_terms, qkv_pieces = lax.optimization_barrier((head_d_attn, expert_terms, qkv_pieces))
-    half_send, half_keep, side_send, side_keep = expert_terms
-    by_half = (half_keep, lax.ppermute(half_send, "ctx", OTHER_HALF))
-    by_side = (side_keep, lax.ppermute(side_send, "wsh", OTHER_SIDE))
+    head_d_attn = head_d_attn.reshape(8 * rows, WIDTH)
+    head_d_attn, far_qkv, near_qkv = lax.optimization_barrier((head_d_attn, far_qkv, near_qkv))
+    qkv_pieces = [by_head, near_qkv, far_qkv, lax.ppermute(far_qkv, "wsh", OTHER_CORE)]
+
+    half, side = index % 2, stream // 2
+
+    def part_of(terms, which):
+        return lax.dynamic_index_in_dim(terms, which, 1, keepdims=False)
+
+    half_got = lax.ppermute(part_of(half_sum, 1 - side), "wsh", OTHER_SIDE)
+    side_got = lax.ppermute(part_of(side_sum, 1 - half), "ctx", OTHER_HALF)
     d_q, d_kv = run_backward(meta, head_q, kv_all, head_attn, lse, head_d_attn)
-    small_term = jnp.concatenate(
-        [d_router_local.astype(BF), d_gain_second.astype(BF)[:, None], jnp.zeros((width, 47), BF)], axis=1
-    )
-    out_term = dot(group_branch, head_attn, TN).astype(BF)
-    by_half, by_side, d_q = lax.optimization_barrier((by_half, by_side, d_q))
-
-    def part_sum(terms, which):
-        return sum(lax.dynamic_index_in_dim(t, which, 0, keepdims=False).astype(F32) for t in terms)
-
-    half, side = index % 2, stream // 2
-    half_got = lax.ppermute(part_sum(by_half, 1 - side).astype(BF), "wsh", OTHER_SIDE)
-    side_got = lax.ppermute(part_sum(by_side, 1 - half).astype(BF), "ctx", OTHER_HALF)
     d_tokens, gathered = finish(
         d_q,
         d_kv.reshape(4, 8 * rows, 2 * HEAD_SIZE),
         group_act,
         small_term,
-        out_term,
+        head_blocks,
+        branch_part.reshape(8 * rows, WIDTH),
         qkv_pieces,
         tokens[0],
         d_middle,
@@ -1129,7 +1192,11 @@
     )
     gathered, half_got, side_got = lax.optimization_barrier((gathered, half_got, side_got))
     expert_own = jnp.concatenate(
-        [part_sum(by_half, side) + half_got.astype(F32), part_sum(by_side, half) + side_got.astype(F32)], axis=1
+        [
+            part_of(half_sum, side).astype(F32) + half_got.astype(F32),
+            part_of(side_sum, half).astype(F32) + side_got.astype(F32),
+        ],
+        axis=1,
     )
     d_w_qkv, d_w_out, rest = assemble(gathered)
     d_gain_first = jnp.sum(d_w_qkv * w_qkv.astype(BF).astype(F32), axis=1) / gain_attn.astype(BF).astype(F32)

time: 421 us -> 404 us (0.960); the launches traced: 413 us -> 401 us
  Pallas kernels: 277 us -> 328 us
  blocking collectives: 21.6 us -> 0 us
  matrix products: 23.1 us -> 1.78 us
  other arithmetic: 24.7 us -> 14.4 us
  waiting for transfers between devices: 12.2 us -> 5.57 us
    pallas_call x2, Pallas kernels: 86.9 us -> 128 us  [the longest x1 125 us: run_middle(): pl.pallas_call(middle_kernel, out_shape=(jax.ShapeDtypeStruct(x.shape, BF...]
    all_to_all x1 -> x0, blocking collectives: 21.6 us -> none  [swap(): return lax.all_to_all(x, axis, 0, 0, axis_index_groups=groups, tiled=True)]
    dot_general x12 -> x1, matrix products: 23.1 us -> 1.78 us  [dot(): return lax.dot_general(a, b, (dims, ((), ())), preferred_element_type=F32)]
    ppermute x5 -> x3, waiting for transfers between devices: 7.22 us -> 0.01 us  [the longest x1 0.01 us: body(): near_qkv = lax.ppermute(by_head, 'wsh', OTHER_CORE)]
    convert_element_type x4 -> x0, other arithmetic: 6.9 us -> none  [the longest x1 2.6 us: body(): d_branch = d_middle.astype(BF)]
    unnamed x75 -> x66, local copies, waits for them, and re-layouts: 14.7 us -> 20.6 us
    all_gather x1, waiting for transfers between devices: 0.01 us -> 5.54 us  [body(): lax.all_gather(expert_shard, ('ctx', 'wsh'), axis_index_groups=OWNERS)]
    all_to_all x1 -> x0, waiting for transfers between devices: 4.93 us -> none  [swap(): return lax.all_to_all(x, axis, 0, 0, axis_index_groups=groups, tiled=True)]
  transfers between devices with their start and end apart: 10 -> 6, of which waited for: 3 -> 1; matrix products, arithmetic and copies ran while one was open for 11% -> 3% of each run, Pallas kernels for 56% -> 71%
where the time goes in v4:
time: 404 us; the launch traced here: 401 us
  Pallas kernels  328 us (81%)
  local copies, waits for them, and re-layouts  29.9 us (7%)
  between operations  14.5 us (4%)
  other arithmetic  14.4 us (4%)
  starting transfers between devices  6.89 us (2%)
  waiting for transfers between devices  5.57 us (1%)
    pallas_call x1, Pallas kernels, run_middle(): pl.pallas_call(middle_kernel, out_shape=(jax.ShapeDtypeStruct(x.shape, BF...  125 us
    pallas_call x1, Pallas kernels, finish(): pl.pallas_call(finish_kernel, out_shape=(jax.ShapeDtypeStruct(x.shape, BF...  101 us
    pallas_call x1, Pallas kernels, gather_rows(): pl.pallas_call(gather_rows_kernel, out_shape=(jax.ShapeDtypeStruct((8,) +...  39.9 us
    pallas_call x1, Pallas kernels, run_backward(): local_call(attention_backward, (jax.ShapeDtypeStruct((rows, WIDTH), BF),...  21.4 us
    unnamed x66, local copies, waits for them, and re-layouts  20.6 us
    pallas_call x1, Pallas kernels, gather_keys(): pl.pallas_call(gather_keys_kernel, out_shape=jax.ShapeDtypeStruct((4,) +...  19.1 us
    pallas_call x1, Pallas kernels, run_forward(): local_call(attention_forward, (jax.ShapeDtypeStruct((rows, WIDTH), BF), j...  17.3 us
  transfers between devices with their start and end apart: 6, of which 1 were waited for; matrix products, arithmetic and copies ran while one was open for 3% of the time, Pallas kernels for 71%

profile of v4, /device:TPU:8, one launch (start us, length us, event | category | flops | bytes accessed | tf_op | source)
XLA Modules:
  0.0 401.1 jit_solution(9529373309472861199)
XLA Ops:
  7.2 0.7 convert_element_type.104
  7.9 0.7 convert_element_type.103
  8.6 0.9 copy.62.router_ref
  9.7 2.1 copy-done.2
  11.8 1.7 copy-done.7
  13.4 1.0 prepare.1
  14.5 39.9 %gather_rows.1 = (bf16[8,128,1536]{2,1,0:T(8,128)(2,1)S(1)}, bf16[4,384,384]{2,1,0:T(8,128)(2,1)S(1)}, bf16[4,16,384]{2,1,0:T(8,128)(2,1)S(1)}, bf16[4,384,1536]{2,1,0:T(8,128)(2,1)S(1)}) custom-call(bf16[128,1536]{1,0:T(8,128)(2,1)S(1)} %bitcast.71, bf16[8,384,384]{2,1,0:T(8,128)(2,1)S(1)} %get-tuple-element.57.wp_ref.p0, ...), custom_call_target="tpu_custom_call" | custom-call | tf_op jit(solution)/shard_map/gather_rows/pallas_call | solution.py:463
  54.5 0.6 copy-done.16
  55.1 2.2 copy-done.17
  57.3 1.1 copy-done.18
  58.4 0.8 convert_element_type.116
  59.2 2.0 copy.69
  61.3 2.3 pad_maximum_fusion
  63.6 0.8 fusion.11
  64.4 0.7 multiply_reduce_fusion
  65.1 0.8 fusion.1.act_ref
  65.9 0.5 copy-done.19
  66.4 1.8 convolution_convert_fusion
  68.2 0.1 slice.50.kv_ref
  68.3 0.8 slice.49.q_ref
  69.2 0.7 fusion.10
  69.9 0.2 reduce-window.19
  70.0 0.1 reshape.150
  70.2 0.1 eq.44
  70.3 19.1 %gather_keys.1 = bf16[4,1024,128]{2,1,0:T(8,128)(2,1)S(1)} custom-call(bf16[1024,128]{1,0:T(8,128)(2,1)S(1)} %slice.50.kv_ref), custom_call_target="tpu_custom_call" | custom-call | tf_op jit(solution)/shard_map/gather_keys/pallas_call | solution.py:513
  89.5 0.1 select_reduce_fusion
  89.7 1.1 copy-done.13
  90.8 17.3 %attention_forward.1 = (bf16[1024,192]{1,0:T(8,128)(2,1)S(1)}, f32[17,1,192]{2,1,0:T(1,128)S(1)}) custom-call(s32[84]{0:T(128)S(1)} %pad_add_fusion.meta, bf16[1024,192]{1,0:T(8,128)(2,1)S(1)} %copy-done.13, bf16[4096,128]{1,0:T(8,128)(2,1)S(1)} %bitcast.74), custom_call_target="tpu_custom_call" | custom-call | flops 4000000000 | bytes 10000000 | tf_op jit(solution)/shard_map/attention_forward/pallas_call | solution.py:265
  108.1 0.8 copy-done.11
  108.9 3.4 collective-permute-start
  112.4 0.1 copy.65
  112.5 0.1 eq.52
  112.6 0.1 eq.48
  112.8 0.6 reduce-window.20
  113.4 0.2 slice_reduce_fusion.1
  113.7 0.1 reduce_sum.41
  113.9 0.8 copy.71.slot_ref
  114.7 0.7 copy.70.choice_ref
  115.4 0.8 slice_convert_fusion
  116.2 0.6 convert.6.gain_ref
  116.8 5.5 %all-gather.3.cloned.1.call-done = bf16[24,384,512]{2,1,0:T(8,128)(2,1)} async-done(((bf16[3,384,512]{2,1,0:T(8,128)(2,1)}), bf16[24,384,512]{2,1,0:T(8,128)(2,1)}) %all-gather.3.cloned.1.call-update) | async-done | bytes 9437200 | tf_op jit(solution)/shard_map/all_gather | solution.py:1149
  122.4 124.9 %middle.1 = (bf16[128,1536]{1,0:T(8,128)(2,1)}, f32[128,1536]{1,0:T(8,128)}, bf16[1536,64]{1,0:T(8,128)(2,1)}, bf16[8,128,192]{2,1,0:T(8,128)(2,1)}, bf16[8,128,...) custom-call(bf16[8,128,192]{2,1,0:T(8,128)(2,1)} %bitcast.77, ...), custom_call_target="tpu_custom_call" | custom-call | flops 15000000512 | bytes 100000000 | tf_op jit(solution)/shard_map/middle/pallas_call | solution.py:764
  247.3 0.6 collective-permute-start.2
  247.9 1.1 dynamic-slice_bitcast_fusion
  249.0 0.7 collective-permute-start.4
  249.7 1.1 dynamic-slice_bitcast_fusion.1
  250.8 2.1 collective-permute-start.3
  252.9 1.0 copy-done.12
  254.0 1.0 copy-done.14
  255.0 21.4 %attention_backward.1 = (bf16[1024,192]{1,0:T(8,128)(2,1)S(1)}, bf16[4096,128]{1,0:T(8,128)(2,1)S(1)}) custom-call(s32[84]{0:T(128)S(1)} %pad_add_fusion.meta, bf16[1024,192]{1,0:T(8,128)(2,1)S(1)} %copy-done.14, bf16[4096,128]{1,0:T(8,128)(2,1)S(1)} %bitcast.75, bf16[1024,192]{1,0:T(8,128)(2,1)S(1)} %copy-done.12, ...), custom_call_target="tpu_custom_call" | custom-call | flops 4000000000 | bytes 10000000 | tf_op jit(solution)/shard_map/attention_backward/pallas_call | solution.py:288
  276.4 1.0 copy-done.10
  277.5 101.0 %finish.1 = (bf16[128,1536]{1,0:T(8,128)(2,1)S(1)}, bf16[4,8,96,576]{3,2,1,0:T(8,128)(2,1)}) custom-call(bf16[1024,192]{1,0:T(8,128)(2,1)S(1)} %get-tuple-element.59.dq_ref, bf16[4,1024,128]{2,1,0:T(8,128)(2,1)} %bitcast.73, bf16[1024,1536]{1,0:T(8,128)(2,1)} %copy-done.21, bf16[1536,64]{1,0:T(8,128)(2,1)S(1)} %copy-done.15, bf16[8,128,192]{2,1,0:T(8,128)(2,1)} %bitcast.78, ...), custom_call_target="tpu_custom_call" | custom-call | flops 3000000000 | bytes 100000000 | tf_op jit(solution)/shard_map/finish/pallas_call | solution.py:1062
  378.5 0.4 convert_add_fusion
  378.9 1.3 fusion.5
  380.2 1.1 copy.74
  381.4 2.1 copy-done.6
  383.5 3.4 assemble.1
  386.9 1.0 copy-done.3
  387.9 2.8 multiply_reduce_fusion.1
  390.6 0.6 convert_divide_fusion
  391.2 0.8 slice_reduce_fusion
  392.0 0.7 copy.73
  392.8 0.7 copy.82
  393.5 0.7 copy.83
  (73 shorter events, 0.8 us)
Async XLA Ops:
  7.2 62.0 %copy-start = (s32[4,64]{1,0:T(4,128)S(1)}, s32[4,64]{1,0:T(4,128)}, u32[]{:S(2)}) copy-start(s32[4,64]{1,0:T(4,128)} %param.15) | copy-start | bytes 3076
  7.2 115.2 %all-gather.3.cloned.1.call-start = ((), (), s32[]{:S(2)}) async-start(), calls=%async_computation | async-start | bytes 10616832 | tf_op jit(solution)/shard_map/all_gather | solution.py:1149
  9.7 2.1 copy-start.2
  11.8 1.7 copy-start.7
  13.4 1.0 copy-start.8
  14.4 44.0 %copy-start.4 = (bf16[8,384,384]{2,1,0:T(8,128)(2,1)}, bf16[8,384,384]{2,1,0:T(8,128)(2,1)S(1)}, u32[]{:S(2)}) copy-start(bf16[8,384,384]{2,1,0:T(8,128)(2,1)S(1)} %get-tuple-element.57.wp_ref.p0) | copy-start | bytes 7077892
  14.5 43.9 %copy-start.24 = (f32[1,384,512]{2,1,0:T(8,128)S(1)}, f32[1,384,512]{2,1,0:T(8,128)}, u32[]{:S(2)}) copy-start(f32[1,384,512]{2,1,0:T(8,128)} %param.22) | copy-start | bytes 2359300
  14.5 43.9 %copy-start.25 = (f32[1,384,512]{2,1,0:T(8,128)S(1)}, f32[1,384,512]{2,1,0:T(8,128)}, u32[]{:S(2)}) copy-start(f32[1,384,512]{2,1,0:T(8,128)} %param.23) | copy-start | bytes 2359300
  54.4 0.6 copy-start.16
  55.1 2.2 copy-start.17
  57.3 1.1 copy-start.18
  65.1 1.3 copy-start.19
  65.9 2.3 copy-start.21
  89.7 1.1 copy-start.13
  90.8 18.1 %copy-start.5 = (bf16[8,384,384]{2,1,0:T(8,128)(2,1)S(1)}, bf16[8,384,384]{2,1,0:T(8,128)(2,1)}, u32[]{:S(2)}) copy-start(bf16[8,384,384]{2,1,0:T(8,128)(2,1)} %copy-done.4) | copy-start | bytes 7077892
  90.8 21.6 %copy-start.27 = (s32[1,128,2]{1,2,0:T(2,128)S(1)}, s32[1,128,2]{1,2,0:T(2,128)}, u32[]{:S(2)}) copy-start(s32[1,128,2]{1,2,0:T(2,128)} %param.16) | copy-start | bytes 3076
  108.1 0.8 copy-start.11
  108.9 138.4 %collective-permute-start.1 = (bf16[8,384,384]{2,1,0:T(8,128)(2,1)S(1)}, bf16[8,384,384]{2,1,0:T(8,128)(2,1)}, u32[]{:S(2)}, u32[]{:S(2)}) collective-permute-start(bf16[8,384,384]{2,1,0:T(8,128)(2,1)S(1)} %copy-done.5), channel_id=1, source_target_pairs={{0,1},{1,0},{2,3},{3,2},{4,5},{5,4},{6,7},{7,6},{8,9},{9,8},{10,11... | collective-permute-start | bytes 7077896 | tf_op jit(solution)/shard_map/ppermute | solution.py:1159
  108.9 138.4 %collective-permute-start = (bf16[8,384,384]{2,1,0:T(8,128)(2,1)S(1)}, bf16[8,384,384]{2,1,0:T(8,128)(2,1)}, u32[]{:S(2)}, u32[]{:S(2)}) collective-permute-start(bf16[8,384,384]{2,1,0:T(8,128)(2,1)S(1)} %copy-done.5), channel_id=1, source_target_pairs={{0,18},{1,19},{2,16},{3,17},{4,22},{5,23},{6,20},{7,21},{8,26},{9,... | collective-permute-start | bytes 7077896 | tf_op jit(solution)/shard_map/ppermute | solution.py:1158
  113.9 8.5 %copy-start.29 = (s32[128,2]{0,1:T(2,128)}, s32[128,2]{0,1:T(2,128)S(1)}, u32[]{:S(2)}) copy-start(s32[128,2]{0,1:T(2,128)S(1)} %multiply_add_fusion) | copy-start | bytes 3076
  247.3 5.6 %copy-start.20 = (bf16[8,128,192]{2,1,0:T(8,128)(2,1)S(1)}, bf16[8,128,192]{2,1,0:T(8,128)(2,1)}, u32[]{:S(2)}) copy-start(bf16[8,128,192]{2,1,0:T(8,128)(2,1)} %get-tuple-element.56) | copy-start | bytes 1179652
  247.3 30.1 %collective-permute-start.2 = (bf16[8,384,384]{2,1,0:T(8,128)(2,1)}, bf16[8,384,384]{2,1,0:T(8,128)(2,1)}, u32[]{:S(2)}, u32[]{:S(2)}) collective-permute-start(bf16[8,384,384]{2,1,0:T(8,128)(2,1)} %collective-permute-done.p2), channel_id=1, source_target_pairs={{0,1},{1,0},{2,3},{3,2},{4,5},{5,4},{6,7},{7,6},{8,9},{9,8},{10,11... | collective-permute-start | bytes 7077896 | tf_op jit(solution)/shard_map/ppermute | solution.py:1171
  249.0 129.4 %collective-permute-start.4 = (bf16[3,192,512]{2,1,0:T(8,128)(2,1)S(1)}, bf16[3,192,512]{2,1,0:T(8,128)(2,1)S(1)}, u32[]{:S(2)}, u32[]{:S(2)}) collective-permute-start(bf16[3,192,512]{2,1,0:T(8,128)(2,1)S(1)} %dynamic-slice_bitcast_fusion), channel_id=1, source_target_pairs={{0,4},{4,0},{8,12},{12,8},{16,20},{20,16},{24,28},{28,24},{32,36},... | collective-permute-start | bytes 1769480 | tf_op jit(solution)/shard_map/ppermute | solution.py:1179
  250.8 127.7 %collective-permute-start.3 = (bf16[3,192,512]{2,1,0:T(8,128)(2,1)S(1)}, bf16[3,192,512]{2,1,0:T(8,128)(2,1)S(1)}, u32[]{:S(2)}, u32[]{:S(2)}) collective-permute-start(bf16[3,192,512]{2,1,0:T(8,128)(2,1)S(1)} %dynamic-slice_bitcast_fusion.1), channel_id=1, source_target_pairs={{0,2},{1,3},{2,0},{3,1},{4,6},{5,7},{6,4},{7,5},{8,10},{9,11},{10,... | collective-permute-start | bytes 1769480 | tf_op jit(solution)/shard_map/ppermute | solution.py:1178
  252.9 1.0 copy-start.12
  254.0 1.0 copy-start.14
  255.0 22.4 %copy-start.9 = (bf16[1,128,1536]{2,1,0:T(8,128)(2,1)S(1)}, bf16[1,128,1536]{2,1,0:T(8,128)(2,1)}, u32[]{:S(2)}) copy-start(bf16[1,128,1536]{2,1,0:T(8,128)(2,1)} %param.13) | copy-start | bytes 1179652
  255.0 22.4 %copy-start.15 = (bf16[1536,64]{1,0:T(8,128)(2,1)S(1)}, bf16[1536,64]{1,0:T(8,128)(2,1)}, u32[]{:S(2)}) copy-start(bf16[1536,64]{1,0:T(8,128)(2,1)} %get-tuple-element.61.small_ref) | copy-start | bytes 589828
  276.4 1.0 copy-start.10
  277.4 101.1 %copy-start.22 = (bf16[3,2,192,512]{3,2,1,0:T(8,128)(2,1)S(1)}, bf16[3,2,192,512]{3,2,1,0:T(8,128)(2,1)}, u32[]{:S(2)}) copy-start(bf16[3,2,192,512]{3,2,1,0:T(8,128)(2,1)} %get-tuple-element.68) | copy-start | bytes 3538948
  277.5 101.1 %copy-start.23 = (bf16[3,2,192,512]{3,2,1,0:T(8,128)(2,1)S(1)}, bf16[3,2,192,512]{3,2,1,0:T(8,128)(2,1)}, u32[]{:S(2)}) copy-start(bf16[3,2,192,512]{3,2,1,0:T(8,128)(2,1)} %get-tuple-element.69) | copy-start | bytes 3538948
  381.4 2.1 copy-start.6
  383.5 4.3 %copy-start.3 = (f32[384,2560]{1,0:T(8,128)S(1)}, f32[384,2560]{1,0:T(8,128)}, u32[]{:S(2)}) copy-start(f32[384,2560]{1,0:T(8,128)} %qkv_ref.1) | copy-start | bytes 11796484
  387.8 2.8 copy-start.28
  387.9 4.9 %copy-start.26 = (bf16[128,1536]{1,0:T(8,128)(2,1)S(1)}, bf16[128,1536]{1,0:T(8,128)(2,1)}, u32[]{:S(2)}) copy-start(bf16[128,1536]{1,0:T(8,128)(2,1)} %get-tuple-element.54) | copy-start | bytes 1179652
  387.9 6.4 %copy-start.1 = (s32[4,64]{1,0:T(4,128)S(1)}, s32[4,64]{1,0:T(4,128)}, u32[]{:S(2)}) copy-start(s32[4,64]{1,0:T(4,128)} %param.15) | copy-start | bytes 3076
Sparse Core Ops, SparseCore 0:
  63.7 58.6 all-gather.2

commit v5 on v4

--- a/solution.py
+++ b/solution.py
@@ -304,18 +304,21 @@
     )(meta, q, kv, o, lse, d_o)
 
 
-def assemble_kernel(pieces_ref, qkv_ref, out_ref, rest_ref):
+def assemble_kernel(pieces_ref, weight_ref, qkv_ref, out_ref, rest_ref):
     parts = [pieces_ref[0, i].astype(F32) for i in range(8)]
     ends = (0, WIDTH, WIDTH + HEAD_SIZE, HEAD_COLUMNS)
-    qkv_ref[...] = jnp.concatenate([t[:, a:b] for a, b in zip(ends[:-1], ends[1:]) for t in parts], axis=1)
+    d_qkv = jnp.concatenate([t[:, a:b] for a, b in zip(ends[:-1], ends[1:]) for t in parts], axis=1)
+    qkv_ref[...] = d_qkv
+    gain_part = jnp.sum(d_qkv * weight_ref[...].astype(BF).astype(F32), axis=1, keepdims=True)
     out_ref[...] = jnp.concatenate([t[:, 384:] for t in parts], axis=1)
     tail = parts[0]
     for t in parts[1:]:
         tail = tail + t
-    rest_ref[...] = tail[:, HEAD_COLUMNS:384]
-
-
-def assemble(gathered):
+    lane = lax.broadcasted_iota(jnp.int32, rest_ref.shape, 1)
+    rest_ref[...] = jnp.where(lane == 17, gain_part, tail[:, HEAD_COLUMNS:384])
+
+
+def assemble(gathered, weight):
     _, _, piece, columns = gathered.shape
 
     def by_rows(n):
@@ -329,11 +332,11 @@
             jax.ShapeDtypeStruct((4 * piece, 64), F32),
         ),
         grid=(4,),
-        in_specs=[pl.BlockSpec((1, 8, piece, columns), lambda i: (i, 0, 0, 0))],
+        in_specs=[pl.BlockSpec((1, 8, piece, columns), lambda i: (i, 0, 0, 0)), by_rows(weight.shape[1])],
         out_specs=(by_rows(8 * HEAD_COLUMNS), by_rows(8 * WIDTH), by_rows(64)),
         compiler_params=pltpu.CompilerParams(vmem_limit_bytes=40 * 2**20),
         name="assemble",
-    )(gathered)
+    )(gathered, weight)
 
 
 MESH = pl.DeviceIdType.MESH
@@ -809,10 +812,13 @@
     )(attn, x, cotangent, w_out, head_full, gain.reshape(1, width), choice, slots, slots.T, weights)
 
 
-def prepare_kernel(qkv_ref, router_ref, wo_ref, wp_out, wo_out):
+def prepare_kernel(qkv_ref, router_ref, wo_ref, gate_ref, up_ref, down_ref, wp_out, wo_out, expert_out):
     rows = qkv_ref.shape[0]
     experts = router_ref.shape[1]
     wo_out[...] = wo_ref[...].astype(BF)
+    expert_out[0] = gate_ref[0].astype(BF)
+    expert_out[1] = up_ref[0].astype(BF)
+    expert_out[2] = down_ref[0].T.astype(BF)
     router = router_ref[...].astype(BF)
     tail = jnp.zeros((rows, wp_out.shape[2] - HEAD_COLUMNS - experts), BF)
     k_at, v_at = QUERY_HEADS * HEAD_SIZE, (QUERY_HEADS + KEY_VALUE_HEADS) * HEAD_SIZE
@@ -829,8 +835,8 @@
         )
 
 
-def prepare(w_qkv, w_router, w_out):
-    shard = w_qkv.shape[0]
+def prepare(w_qkv, w_router, w_out, w_gate, w_up, w_down):
+    shard, half = w_gate.shape[1:]
     step = shard // 3
 
     def block(n):
@@ -841,16 +847,25 @@
         out_shape=(
             jax.ShapeDtypeStruct((KEY_VALUE_HEADS, shard, 384), BF),
             jax.ShapeDtypeStruct(w_out.shape, BF),
+            jax.ShapeDtypeStruct((3, shard, half), BF),
         ),
         grid=(3,),
-        in_specs=[block(w_qkv.shape[1]), block(w_router.shape[1]), block(w_out.shape[1])],
+        in_specs=[
+            block(w_qkv.shape[1]),
+            block(w_router.shape[1]),
+            block(w_out.shape[1]),
+            pl.BlockSpec((1, step, half), lambda i: (0, i, 0)),
+            pl.BlockSpec((1, step, half), lambda i: (0, i, 0)),
+            pl.BlockSpec((1, half, step), lambda i: (0, 0, i)),
+        ],
         out_specs=(
             pl.BlockSpec((KEY_VALUE_HEADS, step, 384), lambda i: (0, i, 0)),
             block(w_out.shape[1]),
+            pl.BlockSpec((3, step, half), lambda i: (0, i, 0)),
         ),
         compiler_params=pltpu.CompilerParams(vmem_limit_bytes=40 * 2**20),
         name="prepare",
-    )(w_qkv, w_router, w_out)
+    )(w_qkv, w_router, w_out, w_gate, w_up, w_down)
 
 
 def finish_kernel(
@@ -1132,7 +1147,7 @@
     meta = jnp.concatenate([inverse, own_blocks, jnp.cumsum(lengths_row)]).astype(jnp.int32)
 
     q_columns = QUERY_HEADS * HEAD_SIZE
-    by_head, own_out = prepare(w_qkv, w_router, w_out)
+    by_head, own_out, expert_shard = prepare(w_qkv, w_router, w_out, w_gate, w_up, w_down)
     own_gains = jnp.concatenate(
         [gain_attn.astype(BF)[None], gain_moe.astype(BF)[None], jnp.zeros((14, shard), BF)], axis=0
     )
@@ -1144,8 +1159,7 @@
     gain_second = gains[:, 1].reshape(width).astype(F32)
     full_out = full_out.reshape(q_columns, width)
 
-    w_gate, w_up, w_down, _ = lax.optimization_barrier((w_gate, w_up, w_down, gains))
-    expert_shard = jnp.stack([w_gate[0].astype(BF), w_up[0].astype(BF), w_down[0].T.astype(BF)])
+    expert_shard, gains = lax.optimization_barrier((expert_shard, gains))
     expert_all = lax.all_gather(expert_shard, ("ctx", "wsh"), axis_index_groups=OWNERS)
 
     group_x = group_tokens.reshape(8 * rows, width).astype(F32)
@@ -1198,8 +1212,8 @@
         ],
         axis=1,
     )
-    d_w_qkv, d_w_out, rest = assemble(gathered)
-    d_gain_first = jnp.sum(d_w_qkv * w_qkv.astype(BF).astype(F32), axis=1) / gain_attn.astype(BF).astype(F32)
+    d_w_qkv, d_w_out, rest = assemble(gathered, w_qkv)
+    d_gain_first = rest[:, experts_count + 1] / gain_attn.astype(BF).astype(F32)
     return (
         output_rows[None],
         d_tokens[None],

time: 404 us -> 401 us (level)
  other arithmetic: 14.4 us -> 7.61 us
    unnamed x66 -> x68, local copies, waits for them, and re-layouts: 20.6 us -> 25.9 us
where the time goes in v5:
time: 401 us; the launch traced here: 398 us
  Pallas kernels  327 us (82%)
  local copies, waits for them, and re-layouts  33.7 us (8%)
  between operations  14.4 us (4%)
  waiting for transfers between devices  8.58 us (2%)
  other arithmetic  7.61 us (2%)
  starting transfers between devices  4.42 us (1%)
    pallas_call x1, Pallas kernels, run_middle(): pl.pallas_call(middle_kernel, out_shape=(jax.ShapeDtypeStruct(x.shape, BF...  125 us
    pallas_call x1, Pallas kernels, finish(): pl.pallas_call(finish_kernel, out_shape=(jax.ShapeDtypeStruct(x.shape, BF...  101 us
    pallas_call x1, Pallas kernels, gather_rows(): pl.pallas_call(gather_rows_kernel, out_shape=(jax.ShapeDtypeStruct((8,) +...  39.9 us
    unnamed x68, local copies, waits for them, and re-layouts  25.9 us
    pallas_call x1, Pallas kernels, run_backward(): local_call(attention_backward, (jax.ShapeDtypeStruct((rows, WIDTH), BF),...  21.4 us
    pallas_call x1, Pallas kernels, gather_keys(): pl.pallas_call(gather_keys_kernel, out_shape=jax.ShapeDtypeStruct((4,) +...  18.3 us
    pallas_call x1, Pallas kernels, run_forward(): local_call(attention_forward, (jax.ShapeDtypeStruct((rows, WIDTH), BF), j...  17.3 us
    all_gather x1, waiting for transfers between devices, body(): lax.all_gather(expert_shard, ('ctx', 'wsh'), axis_index_groups=OWNERS)  8.55 us
  transfers between devices with their start and end apart: 6, of which 1 were waited for; matrix products, arithmetic and copies ran while one was open for 3% of the time, Pallas kernels for 71%

profile of v5, /device:TPU:8, one launch (start us, length us, event | category | flops | bytes accessed | tf_op | source)
XLA Modules:
  0.0 397.9 jit_solution(1334356572439717931)
XLA Ops:
  7.2 0.7 convert_element_type.81
  7.9 0.7 convert_element_type.80
  8.6 0.9 copy.55.router_ref
  9.6 0.1 maximum_maximum_fusion.gain_ref
  9.7 2.1 copy-done.2
  11.8 1.7 copy-done.7
  13.4 1.1 copy-done.12
  14.6 1.1 copy-done.13
  15.7 1.1 copy-done.14
  16.8 1.3 prepare.1
  18.1 39.9 %gather_rows.1 = (bf16[8,128,1536]{2,1,0:T(8,128)(2,1)S(1)}, bf16[4,384,384]{2,1,0:T(8,128)(2,1)S(1)}, bf16[4,16,384]{2,1,0:T(8,128)(2,1)S(1)}, bf16[4,384,1536]{2,1,0:T(8,128)(2,1)S(1)}) custom-call(bf16[128,1536]{1,0:T(8,128)(2,1)S(1)} %bitcast.65, bf16[8,384,384]{2,1,0:T(8,128)(2,1)S(1)} %get-tuple-element.55.wp_ref.p0, ...), custom_call_target="tpu_custom_call" | custom-call | tf_op jit(solution)/shard_map/gather_rows/pallas_call | solution.py:466
  58.1 1.4 copy-done.4
  59.5 2.2 copy-done.20
  61.7 1.1 copy-done.21
  62.9 0.7 multiply_reduce_fusion
  63.6 0.8 fusion.1.act_ref
  64.4 0.5 copy-done.22
  64.9 1.8 convolution_convert_fusion
  66.7 0.1 slice.54.kv_ref
  66.8 0.8 slice.53.q_ref
  67.7 0.7 fusion.10
  68.4 0.2 reduce-window.19
  68.6 0.1 reshape.149
  68.7 0.1 eq.44
  68.8 18.3 %gather_keys.1 = bf16[4,1024,128]{2,1,0:T(8,128)(2,1)S(1)} custom-call(bf16[1024,128]{1,0:T(8,128)(2,1)S(1)} %slice.54.kv_ref), custom_call_target="tpu_custom_call" | custom-call | tf_op jit(solution)/shard_map/gather_keys/pallas_call | solution.py:516
  87.2 0.1 select_reduce_fusion
  87.3 0.1 pad_add_fusion.meta
  87.4 1.1 copy-done.17
  88.4 17.3 %attention_forward.1 = (bf16[1024,192]{1,0:T(8,128)(2,1)S(1)}, f32[17,1,192]{2,1,0:T(1,128)S(1)}) custom-call(s32[84]{0:T(128)S(1)} %pad_add_fusion.meta, bf16[1024,192]{1,0:T(8,128)(2,1)S(1)} %copy-done.17, bf16[4096,128]{1,0:T(8,128)(2,1)S(1)} %bitcast.68), custom_call_target="tpu_custom_call" | custom-call | flops 4000000000 | bytes 10000000 | tf_op jit(solution)/shard_map/attention_forward/pallas_call | solution.py:265
  105.8 0.8 copy-done.15
  106.6 0.9 collective-permute-start.1
  107.5 0.1 copy.58
  107.6 0.1 eq.52
  107.7 0.7 eq.48
  108.4 0.6 reduce-window.20
  109.0 0.2 slice_reduce_fusion.2
  109.2 0.8 fusion.7
  110.0 0.1 reduce_sum.32
  110.2 0.8 copy.63.slot_ref
  111.0 0.7 copy.62.choice_ref
  111.7 0.6 convert.6.gain_ref
  112.3 8.6 %all-gather.3.cloned.1.call-done = bf16[24,384,512]{2,1,0:T(8,128)(2,1)} async-done(((bf16[3,384,512]{2,1,0:T(8,128)(2,1)}), bf16[24,384,512]{2,1,0:T(8,128)(2,1)}) %all-gather.3.cloned.1.call-update) | async-done | bytes 9437200 | tf_op jit(solution)/shard_map/all_gather | solution.py:1163
  120.9 124.8 %middle.1 = (bf16[128,1536]{1,0:T(8,128)(2,1)}, f32[128,1536]{1,0:T(8,128)}, bf16[1536,64]{1,0:T(8,128)(2,1)}, bf16[8,128,192]{2,1,0:T(8,128)(2,1)}, bf16[8,128,...) custom-call(bf16[8,128,192]{2,1,0:T(8,128)(2,1)} %bitcast.70, ...), custom_call_target="tpu_custom_call" | custom-call | flops 15000000512 | bytes 100000000 | tf_op jit(solution)/shard_map/middle/pallas_call | solution.py:767
  245.8 0.7 collective-permute-start.2
  246.5 1.1 dynamic-slice_bitcast_fusion
  247.6 0.7 collective-permute-start.4
  248.3 1.1 dynamic-slice_bitcast_fusion.1
  249.4 2.1 collective-permute-start.3
  251.5 1.0 copy-done.16
  252.5 1.0 copy-done.18
  253.5 21.4 %attention_backward.1 = (bf16[1024,192]{1,0:T(8,128)(2,1)S(1)}, bf16[4096,128]{1,0:T(8,128)(2,1)S(1)}) custom-call(s32[84]{0:T(128)S(1)} %pad_add_fusion.meta, bf16[1024,192]{1,0:T(8,128)(2,1)S(1)} %copy-done.18, bf16[4096,128]{1,0:T(8,128)(2,1)S(1)} %bitcast.69, bf16[1024,192]{1,0:T(8,128)(2,1)S(1)} %copy-done.16, ...), custom_call_target="tpu_custom_call" | custom-call | flops 4000000000 | bytes 10000000 | tf_op jit(solution)/shard_map/attention_backward/pallas_call | solution.py:288
  274.9 1.0 copy-done.11
  275.9 100.8 %finish.1 = (bf16[128,1536]{1,0:T(8,128)(2,1)S(1)}, bf16[4,8,96,576]{3,2,1,0:T(8,128)(2,1)}) custom-call(bf16[1024,192]{1,0:T(8,128)(2,1)S(1)} %get-tuple-element.57.dq_ref, bf16[4,1024,128]{2,1,0:T(8,128)(2,1)} %bitcast.67, bf16[1024,1536]{1,0:T(8,128)(2,1)} %copy-done.24, bf16[1536,64]{1,0:T(8,128)(2,1)S(1)} %copy-done.19, bf16[8,128,192]{2,1,0:T(8,128)(2,1)} %bitcast.71, ...), custom_call_target="tpu_custom_call" | custom-call | flops 3000000000 | bytes 100000000 | tf_op jit(solution)/shard_map/finish/pallas_call | solution.py:1077
  376.8 0.4 convert_add_fusion
  377.1 1.3 fusion.5
  378.5 1.1 copy.66
  379.6 2.1 copy-done.3
  381.7 2.1 copy-done.6
  383.9 3.5 assemble.1
  387.4 0.8 slice_reduce_fusion
  388.2 0.6 convert_divide_fusion
  388.8 0.7 copy.65
  389.5 0.7 copy.74
  390.3 0.7 copy.75
  (70 shorter events, 0.5 us)
Async XLA Ops:
  7.2 60.5 %copy-start = (s32[4,64]{1,0:T(4,128)S(1)}, s32[4,64]{1,0:T(4,128)}, u32[]{:S(2)}) copy-start(s32[4,64]{1,0:T(4,128)} %param.15) | copy-start | bytes 3076
  7.2 113.7 %all-gather.3.cloned.1.call-start = ((), (), s32[]{:S(2)}) async-start(), calls=%async_computation | async-start | bytes 10616832 | tf_op jit(solution)/shard_map/all_gather | solution.py:1163
  9.7 2.1 copy-start.2
  11.8 1.7 copy-start.7
  13.4 1.1 copy-start.12
  14.6 1.1 copy-start.13
  15.7 1.1 copy-start.14
  16.8 1.3 copy-start.8
  18.1 40.0 %copy-start.10 = (bf16[3,384,512]{2,1,0:T(8,128)(2,1)}, bf16[3,384,512]{2,1,0:T(8,128)(2,1)S(1)}, u32[]{:S(2)}) copy-start(bf16[3,384,512]{2,1,0:T(8,128)(2,1)S(1)} %get-tuple-element.51) | copy-start | bytes 3538948
  58.1 1.4 copy-start.4
  59.5 2.2 copy-start.20
  61.7 1.1 copy-start.21
  63.6 1.3 copy-start.22
  64.4 2.3 copy-start.24
  87.4 1.1 copy-start.17
  88.4 18.1 %copy-start.5 = (bf16[8,384,384]{2,1,0:T(8,128)(2,1)S(1)}, bf16[8,384,384]{2,1,0:T(8,128)(2,1)}, u32[]{:S(2)}) copy-start(bf16[8,384,384]{2,1,0:T(8,128)(2,1)} %copy-done.4) | copy-start | bytes 7077892
  88.4 19.0 %copy-start.28 = (s32[1,128,2]{1,2,0:T(2,128)S(1)}, s32[1,128,2]{1,2,0:T(2,128)}, u32[]{:S(2)}) copy-start(s32[1,128,2]{1,2,0:T(2,128)} %param.16) | copy-start | bytes 3076
  105.8 0.8 copy-start.15
  106.6 139.2 %collective-permute-start.1 = (bf16[8,384,384]{2,1,0:T(8,128)(2,1)S(1)}, bf16[8,384,384]{2,1,0:T(8,128)(2,1)}, u32[]{:S(2)}, u32[]{:S(2)}) collective-permute-start(bf16[8,384,384]{2,1,0:T(8,128)(2,1)S(1)} %copy-done.5), channel_id=1, source_target_pairs={{0,1},{1,0},{2,3},{3,2},{4,5},{5,4},{6,7},{7,6},{8,9},{9,8},{10,11... | collective-permute-start | bytes 7077896 | tf_op jit(solution)/shard_map/ppermute | solution.py:1173
  107.5 138.3 %collective-permute-start = (bf16[8,384,384]{2,1,0:T(8,128)(2,1)S(1)}, bf16[8,384,384]{2,1,0:T(8,128)(2,1)}, u32[]{:S(2)}, u32[]{:S(2)}) collective-permute-start(bf16[8,384,384]{2,1,0:T(8,128)(2,1)S(1)} %copy-done.5), channel_id=1, source_target_pairs={{0,18},{1,19},{2,16},{3,17},{4,22},{5,23},{6,20},{7,21},{8,26},{9,... | collective-permute-start | bytes 7077896 | tf_op jit(solution)/shard_map/ppermute | solution.py:1172
  110.2 10.7 %copy-start.30 = (s32[128,2]{0,1:T(2,128)}, s32[128,2]{0,1:T(2,128)S(1)}, u32[]{:S(2)}) copy-start(s32[128,2]{0,1:T(2,128)S(1)} %multiply_add_fusion) | copy-start | bytes 3076
  245.8 5.7 %copy-start.23 = (bf16[8,128,192]{2,1,0:T(8,128)(2,1)S(1)}, bf16[8,128,192]{2,1,0:T(8,128)(2,1)}, u32[]{:S(2)}) copy-start(bf16[8,128,192]{2,1,0:T(8,128)(2,1)} %get-tuple-element.54) | copy-start | bytes 1179652
  245.8 30.1 %collective-permute-start.2 = (bf16[8,384,384]{2,1,0:T(8,128)(2,1)}, bf16[8,384,384]{2,1,0:T(8,128)(2,1)}, u32[]{:S(2)}, u32[]{:S(2)}) collective-permute-start(bf16[8,384,384]{2,1,0:T(8,128)(2,1)} %collective-permute-done.p2), channel_id=1, source_target_pairs={{0,1},{1,0},{2,3},{3,2},{4,5},{5,4},{6,7},{7,6},{8,9},{9,8},{10,11... | collective-permute-start | bytes 7077896 | tf_op jit(solution)/shard_map/ppermute | solution.py:1185
  247.6 129.1 %collective-permute-start.4 = (bf16[3,192,512]{2,1,0:T(8,128)(2,1)S(1)}, bf16[3,192,512]{2,1,0:T(8,128)(2,1)S(1)}, u32[]{:S(2)}, u32[]{:S(2)}) collective-permute-start(bf16[3,192,512]{2,1,0:T(8,128)(2,1)S(1)} %dynamic-slice_bitcast_fusion), channel_id=1, source_target_pairs={{0,4},{4,0},{8,12},{12,8},{16,20},{20,16},{24,28},{28,24},{32,36},... | collective-permute-start | bytes 1769480 | tf_op jit(solution)/shard_map/ppermute | solution.py:1193
  249.4 127.3 %collective-permute-start.3 = (bf16[3,192,512]{2,1,0:T(8,128)(2,1)S(1)}, bf16[3,192,512]{2,1,0:T(8,128)(2,1)S(1)}, u32[]{:S(2)}, u32[]{:S(2)}) collective-permute-start(bf16[3,192,512]{2,1,0:T(8,128)(2,1)S(1)} %dynamic-slice_bitcast_fusion.1), channel_id=1, source_target_pairs={{0,2},{1,3},{2,0},{3,1},{4,6},{5,7},{6,4},{7,5},{8,10},{9,11},{10,... | collective-permute-start | bytes 1769480 | tf_op jit(solution)/shard_map/ppermute | solution.py:1192
  251.5 1.0 copy-start.16
  252.5 1.0 copy-start.18
  253.5 22.4 %copy-start.9 = (bf16[1,128,1536]{2,1,0:T(8,128)(2,1)S(1)}, bf16[1,128,1536]{2,1,0:T(8,128)(2,1)}, u32[]{:S(2)}) copy-start(bf16[1,128,1536]{2,1,0:T(8,128)(2,1)} %param.13) | copy-start | bytes 1179652
  253.5 22.4 %copy-start.19 = (bf16[1536,64]{1,0:T(8,128)(2,1)S(1)}, bf16[1536,64]{1,0:T(8,128)(2,1)}, u32[]{:S(2)}) copy-start(bf16[1536,64]{1,0:T(8,128)(2,1)} %get-tuple-element.59.small_ref) | copy-start | bytes 589828
  274.9 1.0 copy-start.11
  275.9 100.8 %copy-start.25 = (bf16[3,2,192,512]{3,2,1,0:T(8,128)(2,1)S(1)}, bf16[3,2,192,512]{3,2,1,0:T(8,128)(2,1)}, u32[]{:S(2)}) copy-start(bf16[3,2,192,512]{3,2,1,0:T(8,128)(2,1)} %get-tuple-element.66) | copy-start | bytes 3538948
  275.9 100.8 %copy-start.26 = (bf16[3,2,192,512]{3,2,1,0:T(8,128)(2,1)S(1)}, bf16[3,2,192,512]{3,2,1,0:T(8,128)(2,1)}, u32[]{:S(2)}) copy-start(bf16[3,2,192,512]{3,2,1,0:T(8,128)(2,1)} %get-tuple-element.67) | copy-start | bytes 3538948
  379.6 2.1 copy-start.3
  381.7 2.1 copy-start.6
  383.9 4.4 %copy-start.29 = (f32[384]{0:T(512)S(1)}, f32[384]{0:T(512)}, u32[]{:S(2)}) copy-start(f32[384]{0:T(512)} %param.17) | copy-start | bytes 4612
  383.9 5.7 %copy-start.27 = (bf16[128,1536]{1,0:T(8,128)(2,1)S(1)}, bf16[128,1536]{1,0:T(8,128)(2,1)}, u32[]{:S(2)}) copy-start(bf16[128,1536]{1,0:T(8,128)(2,1)} %get-tuple-element.52) | copy-start | bytes 1179652
  383.9 7.2 %copy-start.1 = (s32[4,64]{1,0:T(4,128)S(1)}, s32[4,64]{1,0:T(4,128)}, u32[]{:S(2)}) copy-start(s32[4,64]{1,0:T(4,128)} %param.15) | copy-start | bytes 3076
Sparse Core Ops, SparseCore 0:
  62.9 57.9 all-gather.2

commit v6 on v5

--- a/solution.py
+++ b/solution.py
@@ -396,13 +396,15 @@
 def gather_rows_kernel(
     tok_ref, wp_ref, gain_ref, wo_ref, tok_out, wp_out, gain_out, wo_out, v_tok, v_wp, v_gain, v_wo, send, recv, local
 ):
-    place, stream = turned(lax.axis_index("ctx")), lax.axis_index("wsh")
+    index, stream = lax.axis_index("ctx"), lax.axis_index("wsh")
+    place, parity = turned(index), index % 2
+    beside = {"ctx": index + 1 - 2 * parity}
     x, z = place % 4, (place // 4) % 2
     right, left = {"ctx": turned(place - x + (x + 1) % 4)}, {"ctx": turned(place - x + (x + 3) % 4)}
     across = place + 4 - 8 * z
     other = {"wsh": stream + 1 - 2 * (stream % 2)}
     far = {"ctx": turned(across), "wsh": (stream + 2) % 4}
-    meet([right, left, {"ctx": turned(across)}, other, far])
+    meet([right, left, {"ctx": turned(across)}, other, far, beside])
     copies = Copies(send, recv, local)
     half = tok_ref.shape[0] // 2
     own, own_z = z * 4 + x, (1 - z) * 4 + x
@@ -423,8 +425,12 @@
     to_left = [copies.to(rows(tok_ref, h), spot(own, h), left) for h in (1, 0)]
     copies.to(wp_ref.at[head], wp_out.at[stream], other)
     copies.to(gain_ref, gain_out.at[stream], other)
-    third = wo_ref.shape[0] // 3
-    parts = [pl.ds(i * third, third) for i in range(3)]
+    part = wo_ref.shape[0] // 4
+
+    def half_of(side):
+        return [pl.ds(pl.multiple_of((2 * side + i) * part, part), part) for i in range(2)]
+
+    parts, rest = half_of(parity), half_of(1 - parity)
     far_wo = [copies.to(wo_ref.at[p], wo_out.at[stream, p], far) for p in parts]
     copies.to(wo_ref, wo_out.at[stream], other)
     copies.keep(tok_ref, v_tok, tok_out.at[own])
@@ -452,11 +458,21 @@
     arrive(cross[1])
     z_right = [copies.to(spot(own_z, h), spot(own_z, h), right) for h in (0, 1)]
     z_left = [copies.to(spot(own_z, h), spot(own_z, h), left) for h in (1, 0)]
+    beside_wo = []
+
+    def hand_on(i):
+        at = wo_out.at[far_stream, parts[i]]
+        arrive(far_wo[i])
+        beside_wo.append(copies.to(at, at, beside))
+        copies.to(at, at, other)
+
+    hand_on(0)
     arrive(z_right[0])
     copies.to(spot(left_z, 0), spot(left_z, 0), right)
     arrive(z_left[0])
     copies.to(spot(right_z, 1), spot(right_z, 1), left)
-    for p, copy in zip(parts, far_wo):
+    hand_on(1)
+    for p, copy in zip(rest, beside_wo):
         arrive(copy)
         copies.to(wo_out.at[far_stream, p], wo_out.at[far_stream, p], other)
     copies.finish(arrived)
@@ -478,8 +494,8 @@
             pltpu.VMEM(wp.shape[1:], BF),
             pltpu.VMEM(gain.shape, BF),
             pltpu.VMEM(wo.shape, BF),
-            pltpu.SemaphoreType.DMA((27,)),
-            pltpu.SemaphoreType.DMA((27,)),
+            pltpu.SemaphoreType.DMA((29,)),
+            pltpu.SemaphoreType.DMA((29,)),
             pltpu.SemaphoreType.DMA((8,)),
         ],
         compiler_params=pltpu.CompilerParams(collective_id=1, has_side_effects=True, vmem_limit_bytes=40 * 2**20),

time: 401 us -> 397 us (0.990)
    pallas_call x1, Pallas kernels: 39.9 us -> 34.8 us  [gather_rows(): pl.pallas_call(gather_rows_kernel, out_shape=(jax.ShapeDtypeStruct((8,) +...]
  transfers between devices with their start and end apart: 6 -> 6, of which waited for: 1 -> 1; matrix products, arithmetic and copies ran while one was open for 3% -> 3% of each run, Pallas kernels for 71% -> 72%
where the time goes in v6:
time: 397 us; the launch traced here: 395 us
  Pallas kernels  326 us (82%)
  local copies, waits for them, and re-layouts  33.7 us (8%)
  between operations  14.5 us (4%)
  waiting for transfers between devices  7.72 us (2%)
  other arithmetic  7.61 us (2%)
    pallas_call x1, Pallas kernels, run_middle(): pl.pallas_call(middle_kernel, out_shape=(jax.ShapeDtypeStruct(x.shape, BF...  124 us
    pallas_call x1, Pallas kernels, finish(): pl.pallas_call(finish_kernel, out_shape=(jax.ShapeDtypeStruct(x.shape, BF...  101 us
    pallas_call x1, Pallas kernels, gather_rows(): pl.pallas_call(gather_rows_kernel, out_shape=(jax.ShapeDtypeStruct((8,) +...  34.8 us
    unnamed x68, local copies, waits for them, and re-layouts  25.9 us
    pallas_call x1, Pallas kernels, run_backward(): local_call(attention_backward, (jax.ShapeDtypeStruct((rows, WIDTH), BF),...  24.3 us
    pallas_call x1, Pallas kernels, run_forward(): local_call(attention_forward, (jax.ShapeDtypeStruct((rows, WIDTH), BF), j...  19.8 us
    pallas_call x1, Pallas kernels, gather_keys(): pl.pallas_call(gather_keys_kernel, out_shape=jax.ShapeDtypeStruct((4,) +...  17.3 us
  transfers between devices with their start and end apart: 6, of which 1 were waited for; matrix products, arithmetic and copies ran while one was open for 3% of the time, Pallas kernels for 72%

profile of v6, /device:TPU:8, one launch (start us, length us, event | category | flops | bytes accessed | tf_op | source)
XLA Modules:
  0.0 395.2 jit_solution(6722462199641925966)
XLA Ops:
  7.2 0.7 convert_element_type.81
  7.9 0.7 convert_element_type.80
  8.6 0.9 copy.55.router_ref
  9.6 0.1 maximum_maximum_fusion.gain_ref
  9.7 2.1 copy-done.2
  11.8 1.7 copy-done.7
  13.4 1.1 copy-done.12
  14.6 1.1 copy-done.13
  15.7 1.1 copy-done.14
  16.8 1.3 prepare.1
  18.1 34.8 %gather_rows.1 = (bf16[8,128,1536]{2,1,0:T(8,128)(2,1)S(1)}, bf16[4,384,384]{2,1,0:T(8,128)(2,1)S(1)}, bf16[4,16,384]{2,1,0:T(8,128)(2,1)S(1)}, bf16[4,384,1536]{2,1,0:T(8,128)(2,1)S(1)}) custom-call(bf16[128,1536]{1,0:T(8,128)(2,1)S(1)} %bitcast.65, bf16[8,384,384]{2,1,0:T(8,128)(2,1)S(1)} %get-tuple-element.55.wp_ref.p0, ...), custom_call_target="tpu_custom_call" | custom-call | tf_op jit(solution)/shard_map/gather_rows/pallas_call | solution.py:482
  53.0 1.4 copy-done.4
  54.4 2.2 copy-done.20
  56.6 1.1 copy-done.21
  57.8 0.7 multiply_reduce_fusion
  58.5 0.8 fusion.1.act_ref
  59.3 0.5 copy-done.22
  59.8 1.8 convolution_convert_fusion
  61.6 0.1 slice.54.kv_ref
  61.7 0.8 slice.53.q_ref
  62.6 0.7 fusion.10
  63.3 0.2 reduce-window.19
  63.4 0.1 reshape.149
  63.6 0.1 eq.44
  63.7 17.3 %gather_keys.1 = bf16[4,1024,128]{2,1,0:T(8,128)(2,1)S(1)} custom-call(bf16[1024,128]{1,0:T(8,128)(2,1)S(1)} %slice.54.kv_ref), custom_call_target="tpu_custom_call" | custom-call | tf_op jit(solution)/shard_map/gather_keys/pallas_call | solution.py:532
  80.9 0.1 dynamic_slice.25
  81.0 0.1 select_reduce_fusion
  81.1 0.1 pad_add_fusion.meta
  81.2 1.1 copy-done.17
  82.3 19.8 %attention_forward.1 = (bf16[1024,192]{1,0:T(8,128)(2,1)S(1)}, f32[17,1,192]{2,1,0:T(1,128)S(1)}) custom-call(s32[84]{0:T(128)S(1)} %pad_add_fusion.meta, bf16[1024,192]{1,0:T(8,128)(2,1)S(1)} %copy-done.17, bf16[4096,128]{1,0:T(8,128)(2,1)S(1)} %bitcast.68), custom_call_target="tpu_custom_call" | custom-call | flops 4000000000 | bytes 10000000 | tf_op jit(solution)/shard_map/attention_forward/pallas_call | solution.py:265
  102.1 0.8 copy-done.15
  102.9 0.1 copy.58
  103.0 0.1 eq.52
  103.2 0.7 eq.48
  103.9 0.6 reduce-window.20
  104.5 0.2 slice_reduce_fusion.2
  104.7 0.8 fusion.7
  105.5 0.1 reduce_sum.32
  105.7 0.8 copy.63.slot_ref
  106.4 0.7 copy.62.choice_ref
  107.2 0.6 convert.6.gain_ref
  107.8 7.7 %all-gather.3.cloned.1.call-done = bf16[24,384,512]{2,1,0:T(8,128)(2,1)} async-done(((bf16[3,384,512]{2,1,0:T(8,128)(2,1)}), bf16[24,384,512]{2,1,0:T(8,128)(2,1)}) %all-gather.3.cloned.1.call-update) | async-done | bytes 9437200 | tf_op jit(solution)/shard_map/all_gather | solution.py:1179
  115.5 123.9 %middle.1 = (bf16[128,1536]{1,0:T(8,128)(2,1)}, f32[128,1536]{1,0:T(8,128)}, bf16[1536,64]{1,0:T(8,128)(2,1)}, bf16[8,128,192]{2,1,0:T(8,128)(2,1)}, bf16[8,128,...) custom-call(bf16[8,128,192]{2,1,0:T(8,128)(2,1)} %bitcast.70, ...), custom_call_target="tpu_custom_call" | custom-call | flops 15000000512 | bytes 100000000 | tf_op jit(solution)/shard_map/middle/pallas_call | solution.py:783
  239.4 0.2 collective-permute-start.2
  239.6 1.1 dynamic-slice_bitcast_fusion
  240.7 1.6 collective-permute-start.4
  242.3 1.1 dynamic-slice_bitcast_fusion.1
  243.4 2.1 collective-permute-start.3
  245.5 1.0 copy-done.16
  246.6 1.0 copy-done.18
  247.6 24.3 %attention_backward.1 = (bf16[1024,192]{1,0:T(8,128)(2,1)S(1)}, bf16[4096,128]{1,0:T(8,128)(2,1)S(1)}) custom-call(s32[84]{0:T(128)S(1)} %pad_add_fusion.meta, bf16[1024,192]{1,0:T(8,128)(2,1)S(1)} %copy-done.18, bf16[4096,128]{1,0:T(8,128)(2,1)S(1)} %bitcast.69, bf16[1024,192]{1,0:T(8,128)(2,1)S(1)} %copy-done.16, ...), custom_call_target="tpu_custom_call" | custom-call | flops 4000000000 | bytes 10000000 | tf_op jit(solution)/shard_map/attention_backward/pallas_call | solution.py:288
  271.9 1.0 copy-done.11
  272.9 101.1 %finish.1 = (bf16[128,1536]{1,0:T(8,128)(2,1)S(1)}, bf16[4,8,96,576]{3,2,1,0:T(8,128)(2,1)}) custom-call(bf16[1024,192]{1,0:T(8,128)(2,1)S(1)} %get-tuple-element.57.dq_ref, bf16[4,1024,128]{2,1,0:T(8,128)(2,1)} %bitcast.67, bf16[1024,1536]{1,0:T(8,128)(2,1)} %copy-done.24, bf16[1536,64]{1,0:T(8,128)(2,1)S(1)} %copy-done.19, bf16[8,128,192]{2,1,0:T(8,128)(2,1)} %bitcast.71, ...), custom_call_target="tpu_custom_call" | custom-call | flops 3000000000 | bytes 100000000 | tf_op jit(solution)/shard_map/finish/pallas_call | solution.py:1093
  374.1 0.4 convert_add_fusion
  374.5 1.3 fusion.5
  375.8 1.1 copy.66
  377.0 2.1 copy-done.3
  379.1 2.1 copy-done.6
  381.2 3.5 assemble.1
  384.7 0.8 slice_reduce_fusion
  385.6 0.6 convert_divide_fusion
  386.2 0.7 copy.65
  386.9 0.7 copy.74
  387.6 0.7 copy.75
  (70 shorter events, 0.5 us)
Async XLA Ops:
  7.2 55.4 %copy-start = (s32[4,64]{1,0:T(4,128)S(1)}, s32[4,64]{1,0:T(4,128)}, u32[]{:S(2)}) copy-start(s32[4,64]{1,0:T(4,128)} %param.15) | copy-start | bytes 3076
  7.2 108.3 %all-gather.3.cloned.1.call-start = ((), (), s32[]{:S(2)}) async-start(), calls=%async_computation | async-start | bytes 10616832 | tf_op jit(solution)/shard_map/all_gather | solution.py:1179
  9.7 2.1 copy-start.2
  11.8 1.7 copy-start.7
  13.4 1.1 copy-start.12
  14.6 1.1 copy-start.13
  15.7 1.1 copy-start.14
  16.8 1.3 copy-start.8
  18.1 34.9 %copy-start.10 = (bf16[3,384,512]{2,1,0:T(8,128)(2,1)}, bf16[3,384,512]{2,1,0:T(8,128)(2,1)S(1)}, u32[]{:S(2)}) copy-start(bf16[3,384,512]{2,1,0:T(8,128)(2,1)S(1)} %get-tuple-element.51) | copy-start | bytes 3538948
  53.0 1.4 copy-start.4
  54.4 2.2 copy-start.20
  56.6 1.1 copy-start.21
  58.5 1.3 copy-start.22
  59.3 2.3 copy-start.24
  81.2 1.1 copy-start.17
  82.3 20.6 %copy-start.5 = (bf16[8,384,384]{2,1,0:T(8,128)(2,1)S(1)}, bf16[8,384,384]{2,1,0:T(8,128)(2,1)}, u32[]{:S(2)}) copy-start(bf16[8,384,384]{2,1,0:T(8,128)(2,1)} %copy-done.4) | copy-start | bytes 7077892
  82.3 20.6 %copy-start.28 = (s32[1,128,2]{1,2,0:T(2,128)S(1)}, s32[1,128,2]{1,2,0:T(2,128)}, u32[]{:S(2)}) copy-start(s32[1,128,2]{1,2,0:T(2,128)} %param.16) | copy-start | bytes 3076
  102.1 0.8 copy-start.15
  102.9 136.5 %collective-permute-start.1 = (bf16[8,384,384]{2,1,0:T(8,128)(2,1)S(1)}, bf16[8,384,384]{2,1,0:T(8,128)(2,1)}, u32[]{:S(2)}, u32[]{:S(2)}) collective-permute-start(bf16[8,384,384]{2,1,0:T(8,128)(2,1)S(1)} %copy-done.5), channel_id=1, source_target_pairs={{0,1},{1,0},{2,3},{3,2},{4,5},{5,4},{6,7},{7,6},{8,9},{9,8},{10,11... | collective-permute-start | bytes 7077896 | tf_op jit(solution)/shard_map/ppermute | solution.py:1189
  102.9 136.5 %collective-permute-start = (bf16[8,384,384]{2,1,0:T(8,128)(2,1)S(1)}, bf16[8,384,384]{2,1,0:T(8,128)(2,1)}, u32[]{:S(2)}, u32[]{:S(2)}) collective-permute-start(bf16[8,384,384]{2,1,0:T(8,128)(2,1)S(1)} %copy-done.5), channel_id=1, source_target_pairs={{0,18},{1,19},{2,16},{3,17},{4,22},{5,23},{6,20},{7,21},{8,26},{9,... | collective-permute-start | bytes 7077896 | tf_op jit(solution)/shard_map/ppermute | solution.py:1188
  105.7 9.8 %copy-start.30 = (s32[128,2]{0,1:T(2,128)}, s32[128,2]{0,1:T(2,128)S(1)}, u32[]{:S(2)}) copy-start(s32[128,2]{0,1:T(2,128)S(1)} %multiply_add_fusion) | copy-start | bytes 3076
  239.4 6.1 %copy-start.23 = (bf16[8,128,192]{2,1,0:T(8,128)(2,1)S(1)}, bf16[8,128,192]{2,1,0:T(8,128)(2,1)}, u32[]{:S(2)}) copy-start(bf16[8,128,192]{2,1,0:T(8,128)(2,1)} %get-tuple-element.54) | copy-start | bytes 1179652
  239.4 33.5 %collective-permute-start.2 = (bf16[8,384,384]{2,1,0:T(8,128)(2,1)}, bf16[8,384,384]{2,1,0:T(8,128)(2,1)}, u32[]{:S(2)}, u32[]{:S(2)}) collective-permute-start(bf16[8,384,384]{2,1,0:T(8,128)(2,1)} %collective-permute-done.p2), channel_id=1, source_target_pairs={{0,1},{1,0},{2,3},{3,2},{4,5},{5,4},{6,7},{7,6},{8,9},{9,8},{10,11... | collective-permute-start | bytes 7077896 | tf_op jit(solution)/shard_map/ppermute | solution.py:1201
  240.7 133.3 %collective-permute-start.4 = (bf16[3,192,512]{2,1,0:T(8,128)(2,1)S(1)}, bf16[3,192,512]{2,1,0:T(8,128)(2,1)S(1)}, u32[]{:S(2)}, u32[]{:S(2)}) collective-permute-start(bf16[3,192,512]{2,1,0:T(8,128)(2,1)S(1)} %dynamic-slice_bitcast_fusion), channel_id=1, source_target_pairs={{0,4},{4,0},{8,12},{12,8},{16,20},{20,16},{24,28},{28,24},{32,36},... | collective-permute-start | bytes 1769480 | tf_op jit(solution)/shard_map/ppermute | solution.py:1209
  243.4 130.7 %collective-permute-start.3 = (bf16[3,192,512]{2,1,0:T(8,128)(2,1)S(1)}, bf16[3,192,512]{2,1,0:T(8,128)(2,1)S(1)}, u32[]{:S(2)}, u32[]{:S(2)}) collective-permute-start(bf16[3,192,512]{2,1,0:T(8,128)(2,1)S(1)} %dynamic-slice_bitcast_fusion.1), channel_id=1, source_target_pairs={{0,2},{1,3},{2,0},{3,1},{4,6},{5,7},{6,4},{7,5},{8,10},{9,11},{10,... | collective-permute-start | bytes 1769480 | tf_op jit(solution)/shard_map/ppermute | solution.py:1208
  245.5 1.0 copy-start.16
  246.6 1.0 copy-start.18
  247.6 25.3 %copy-start.9 = (bf16[1,128,1536]{2,1,0:T(8,128)(2,1)S(1)}, bf16[1,128,1536]{2,1,0:T(8,128)(2,1)}, u32[]{:S(2)}) copy-start(bf16[1,128,1536]{2,1,0:T(8,128)(2,1)} %param.13) | copy-start | bytes 1179652
  247.6 25.3 %copy-start.19 = (bf16[1536,64]{1,0:T(8,128)(2,1)S(1)}, bf16[1536,64]{1,0:T(8,128)(2,1)}, u32[]{:S(2)}) copy-start(bf16[1536,64]{1,0:T(8,128)(2,1)} %get-tuple-element.59.small_ref) | copy-start | bytes 589828
  271.9 1.0 copy-start.11
  272.9 101.2 %copy-start.25 = (bf16[3,2,192,512]{3,2,1,0:T(8,128)(2,1)S(1)}, bf16[3,2,192,512]{3,2,1,0:T(8,128)(2,1)}, u32[]{:S(2)}) copy-start(bf16[3,2,192,512]{3,2,1,0:T(8,128)(2,1)} %get-tuple-element.66) | copy-start | bytes 3538948
  272.9 101.2 %copy-start.26 = (bf16[3,2,192,512]{3,2,1,0:T(8,128)(2,1)S(1)}, bf16[3,2,192,512]{3,2,1,0:T(8,128)(2,1)}, u32[]{:S(2)}) copy-start(bf16[3,2,192,512]{3,2,1,0:T(8,128)(2,1)} %get-tuple-element.67) | copy-start | bytes 3538948
  377.0 2.1 copy-start.3
  379.1 2.1 copy-start.6
  381.2 4.4 %copy-start.29 = (f32[384]{0:T(512)S(1)}, f32[384]{0:T(512)}, u32[]{:S(2)}) copy-start(f32[384]{0:T(512)} %param.17) | copy-start | bytes 4612
  381.2 5.7 %copy-start.27 = (bf16[128,1536]{1,0:T(8,128)(2,1)S(1)}, bf16[128,1536]{1,0:T(8,128)(2,1)}, u32[]{:S(2)}) copy-start(bf16[128,1536]{1,0:T(8,128)(2,1)} %get-tuple-element.52) | copy-start | bytes 1179652
  381.2 7.2 %copy-start.1 = (s32[4,64]{1,0:T(4,128)S(1)}, s32[4,64]{1,0:T(4,128)}, u32[]{:S(2)}) copy-start(s32[4,64]{1,0:T(4,128)} %param.15) | copy-start | bytes 3076
Sparse Core Ops, SparseCore 0:
  57.8 57.6 all-gather.2
